TPU v7x, 32 devices: a whole 2x2x4 slice. The times are simulated.
32 devices in a mesh: mem: 2 (over core), gy: 4 (over y, x), gx: 4 (over z).
Axes of the slice: x: 2, y: 2, z: 4, core: 2. Of those that a mesh axis runs over, the one named last changes fastest.
Arguments:
- increment: float32 [4, 256, 4096], P(None, 'gy', 'gx'), may hold values from -6 to 6
- members: float32 [2, 4, 256, 4096], P('mem', None, 'gy', 'gx'), may hold values from -6 to 6
- zonal_diff: float32 [256, 4096], P('gy', 'gx'), may hold values from 0.05 to 0.35
- merid_diff: float32 [256, 4096], P('gy', 'gx'), may hold values from 0.02 to 0.15
- sea_mask: int32 [256, 4096], P('gy', 'gx'), may hold values 0 or 1
Outputs:
- product: float32 [4, 256, 4096], P(None, 'gy', 'gx')
All inputs are finite; a program needn't handle non-finite values. No bound on the sum of `sea_mask` on one device may be relied on, other than what follows from the above.
Results may differ from a plain program's by a relative error of at most 0.00002.
Values sent between devices are 32-bit elements; how exact they have to be, the bound alone decides.
No kernel may reach another device: no remote copies, remote signals or barrier semaphores. Data moves between devices by JAX's collectives and lax.ppermute only.
A program may use at most 64 MiB of HBM per device.

v0:
```python
import jax
import jax.numpy as jnp
from jax import lax
from jax.sharding import PartitionSpec as P

STEPS = 4


def extended(shard, sides, width, wrap):
    for axis, dim in sides:
        size, length = (lax.axis_size(axis), shard.shape[dim])
        up = [(i, (i + 1) % size) for i in range(size if wrap else size - 1)]
        down = [(j, i) for i, j in up]
        last = lax.slice_in_dim(shard, length - width, length, axis=dim)
        initial = lax.slice_in_dim(shard, 0, width, axis=dim)
        before = lax.ppermute(last, axis, up)
        after = lax.ppermute(initial, axis, down)
        shard = jnp.concatenate([before, shard, after], axis=dim)
    return shard


def face_weights(zonal, merid, wet):
    east = zonal[:, :-1] * wet[:, :-1] * wet[:, 1:]
    north = merid[:-1, :] * wet[:-1, :] * wet[1:, :]
    return (east, north)


def sweep(field, east, north):
    centre = field[:, 1:-1, 1:-1]
    go_east = east[1:-1, 1:] * (field[:, 1:-1, 2:] - centre)
    go_west = east[1:-1, :-1] * (centre - field[:, 1:-1, :-2])
    go_north = north[1:, 1:-1] * (field[:, 2:, 1:-1] - centre)
    go_south = north[:-1, 1:-1] * (centre - field[:, :-2, 1:-1])
    return centre + go_east - go_west + go_north - go_south


def trimmed(table, margin):
    return table[margin : table.shape[0] - margin, margin : table.shape[1] - margin]


def shards(increment, members, zonal_diff, merid_diff, sea_mask):
    member = members[0]
    wet = sea_mask.astype(jnp.float32)
    field = member * increment * wet
    stacked = jnp.stack([zonal_diff, merid_diff, wet])
    stacked = extended(stacked, (("gy", 1),), STEPS, False)
    stacked = extended(stacked, (("gx", 2),), STEPS, True)
    east, north = face_weights(stacked[0], stacked[1], stacked[2])
    near_east = trimmed(east, STEPS - 1)
    near_north = trimmed(north, STEPS - 1)
    first = 0
    for step in range(first, STEPS):
        padded = extended(field, (("gy", 1),), 1, False)
        padded = extended(padded, (("gx", 2),), 1, True)
        field = sweep(padded, near_east, near_north)
    term = member * field
    return lax.psum(term, "mem")


def solution(mesh):
    return jax.shard_map(
        shards,
        mesh=mesh,
        in_specs=(
            P(None, "gy", "gx"),
            P("mem", None, "gy", "gx"),
            P("gy", "gx"),
            P("gy", "gx"),
            P("gy", "gx"),
        ),
        out_specs=P(None, "gy", "gx"),
        check_vma=False,
    )
```

profile of v0, /device:TPU:0, one launch (start us, length us, event | category | flops | bytes accessed | tf_op | source)
XLA Modules:
  0.0 122.6 jit_solution(8452640712759282816)
XLA Ops:
  6.5 1.1 convert_bitcast_fusion
  7.7 4.8 %collective-permute-start = (f32[3,4,1024]{2,1,0:T(4,128)S(1)}, f32[3,4,1024]{2,1,0:T(4,128)S(1)}, u32[]{:S(2)}, u32[]{:S(2)}) collective-permute-start(f32[3,4,1024]{2,1,0:T(4,128)S(1)} %get-tuple-element.25), channel_id=1, source_target_pairs={{0,4},{4,8},{8,12},{1,5},{5,9},{9,13},{2,6},{6,10},{10,14},{3,7},{... | collective-permute-start | bytes 147464 | tf_op jit(solution)/shard_map/ppermute | solution.py:16
  12.6 1.3 %collective-permute-start.1 = (f32[3,4,1024]{2,1,0:T(4,128)S(1)}, f32[3,4,1024]{2,1,0:T(4,128)S(1)}, u32[]{:S(2)}, u32[]{:S(2)}) collective-permute-start(f32[3,4,1024]{2,1,0:T(4,128)S(1)} %get-tuple-element.26), channel_id=1, source_target_pairs={{4,0},{8,4},{12,8},{5,1},{9,5},{13,9},{6,2},{10,6},{14,10},{7,3},{... | collective-permute-start | bytes 147464 | tf_op jit(solution)/shard_map/ppermute | solution.py:17
  13.9 1.4 %fusion.49 = f32[4,64,1024]{2,1,0:T(8,128)S(1)} fusion(f32[4,64,1024]{2,1,0:T(8,128)} %param.5, f32[1,4,64,1024]{3,2,1,0:T(8,128)S(1)} %copy-done, f32[64,1024]{1,0:T(8,128)S(1)} %get-tuple-element.32), kind=kLoop, calls=%fused_computation.82 | loop fusion | flops 524288 | bytes 3407872 | tf_op jit(solution)/shard_map/mul | solution.py:44
  15.3 1.3 %collective-permute-start.5 = (f32[4,1,1024]{2,1,0:T(1,128)S(1)}, f32[4,1,1024]{2,1,0:T(1,128)S(1)}, u32[]{:S(2)}, u32[]{:S(2)}) collective-permute-start(f32[4,1,1024]{2,1,0:T(1,128)S(1)} %get-tuple-element.19), channel_id=1, source_target_pairs={{4,0},{8,4},{12,8},{5,1},{9,5},{13,9},{6,2},{10,6},{14,10},{7,3},{... | collective-permute-start | bytes 49160 | tf_op jit(solution)/shard_map/ppermute | solution.py:17
  16.6 5.2 %collective-permute-start.4 = (f32[4,1,1024]{2,1,0:T(1,128)S(1)}, f32[4,1,1024]{2,1,0:T(1,128)S(1)}, u32[]{:S(2)}, u32[]{:S(2)}) collective-permute-start(f32[4,1,1024]{2,1,0:T(1,128)S(1)} %get-tuple-element.20), channel_id=1, source_target_pairs={{0,4},{4,8},{8,12},{1,5},{5,9},{9,13},{2,6},{6,10},{10,14},{3,7},{... | collective-permute-start | bytes 49160 | tf_op jit(solution)/shard_map/ppermute | solution.py:16
  21.8 0.1 pad_maximum_fusion.32
  22.0 0.1 fusion.55
  22.1 3.7 %collective-permute-start.3 = (f32[3,72,4]{2,1,0:T(8,128)S(1)}, f32[3,72,4]{2,1,0:T(8,128)S(1)}, u32[]{:S(2)}, u32[]{:S(2)}) collective-permute-start(f32[3,72,4]{2,1,0:T(8,128)S(1)} %get-tuple-element.23), channel_id=1, source_target_pairs={{1,0},{2,1},{3,2},{0,3},{5,4},{6,5},{7,6},{4,7},{9,8},{10,9},{11,1... | collective-permute-start | bytes 10376 | tf_op jit(solution)/shard_map/ppermute | solution.py:17
  25.7 0.1 pad_maximum_fusion.44
  25.9 3.9 %collective-permute-start.6 = (f32[4,66,1]{2,1,0:T(8,128)S(1)}, f32[4,66,1]{2,1,0:T(8,128)S(1)}, u32[]{:S(2)}, u32[]{:S(2)}) collective-permute-start(f32[4,66,1]{2,1,0:T(8,128)S(1)} %get-tuple-element.11), channel_id=1, source_target_pairs={{1,0},{2,1},{3,2},{0,3},{5,4},{6,5},{7,6},{4,7},{9,8},{10,9},{11,1... | collective-permute-start | bytes 3176 | tf_op jit(solution)/shard_map/ppermute | solution.py:17
  29.7 0.6 copy-done.4
  30.4 3.3 %collective-permute-done.2 = f32[3,72,4]{2,1,0:T(8,128)} collective-permute-done((f32[3,72,4]{2,1,0:T(8,128)S(1)}, f32[3,72,4]{2,1,0:T(8,128)}, u32[]{:S(2)}, u32[]{:S(2)}) %collective-permute-start.2) | collective-permute-done | bytes 3488 | tf_op jit(solution)/shard_map/ppermute | solution.py:16
  33.7 1.4 %concatenate.71 = f32[3,72,1032]{2,1,0:T(8,128)S(1)} concatenate(f32[3,72,4]{2,1,0:T(8,128)} %collective-permute-done.2, f32[3,72,1024]{2,1,0:T(8,128)S(1)} %pad_maximum_fusion.32, f32[3,72,4]{2,1,0:T(8,128)} %copy-done.4), dimensions={2} | concatenate | bytes 1783296 | tf_op jit(solution)/shard_map/concatenate | solution.py:18
  35.2 0.2 slice_multiply_fusion.2
  35.4 0.4 fusion.56
  35.8 2.0 %collective-permute-done.7 = f32[4,66,1]{2,1,0:T(8,128)} collective-permute-done((f32[4,66,1]{2,1,0:T(8,128)S(1)}, f32[4,66,1]{2,1,0:T(8,128)}, u32[]{:S(2)}, u32[]{:S(2)}) %collective-permute-start.7) | collective-permute-done | bytes 1088 | tf_op jit(solution)/shard_map/ppermute | solution.py:16
  37.8 1.7 %fusion.39 = f32[4,64,1024]{2,1,0:T(8,128)S(1)} fusion(f32[4,64,1024]{2,1,0:T(8,128)S(1)} %fusion.49, f32[4,1,1024]{2,1,0:T(1,128)S(1)} %collective-permute-done.4, f32[4,1,1024]{2,1,0:T(1,128)S(1)} %collective-permute-done.5, f32[4,66,1]{2,1,0:T(8,128)} %collective-permute-done.7, f32[4,66,1]{2,1,0:T(8,128)S(1)} %collective-permute-done.6, ...), kind=kLoop, calls=%fused_computation.64 | loop fusion | flops 5242880 | bytes 3180608 | tf_op jit(solution)/shard_map/sub | solution.py:34
  39.6 1.3 %collective-permute-start.9 = (f32[4,1,1024]{2,1,0:T(1,128)S(1)}, f32[4,1,1024]{2,1,0:T(1,128)S(1)}, u32[]{:S(2)}, u32[]{:S(2)}) collective-permute-start(f32[4,1,1024]{2,1,0:T(1,128)S(1)} %get-tuple-element.17), channel_id=1, source_target_pairs={{4,0},{8,4},{12,8},{5,1},{9,5},{13,9},{6,2},{10,6},{14,10},{7,3},{... | collective-permute-start | bytes 49160 | tf_op jit(solution)/shard_map/ppermute | solution.py:17
  40.9 5.4 %collective-permute-start.8 = (f32[4,1,1024]{2,1,0:T(1,128)S(1)}, f32[4,1,1024]{2,1,0:T(1,128)S(1)}, u32[]{:S(2)}, u32[]{:S(2)}) collective-permute-start(f32[4,1,1024]{2,1,0:T(1,128)S(1)} %get-tuple-element.18), channel_id=1, source_target_pairs={{0,4},{4,8},{8,12},{1,5},{5,9},{9,13},{2,6},{6,10},{10,14},{3,7},{... | collective-permute-start | bytes 49160 | tf_op jit(solution)/shard_map/ppermute | solution.py:16
  46.3 1.4 %collective-permute-done.8 = f32[4,1,1024]{2,1,0:T(1,128)S(1)} collective-permute-done((f32[4,1,1024]{2,1,0:T(1,128)S(1)}, f32[4,1,1024]{2,1,0:T(1,128)S(1)}, u32[]{:S(2)}, u32[]{:S(2)}) %collective-permute-start.8) | collective-permute-done | bytes 16416 | tf_op jit(solution)/shard_map/ppermute | solution.py:16
  47.7 0.1 pad_maximum_fusion.41
  47.8 1.2 collective-permute-start.10
  49.0 0.9 collective-permute-start.11
  49.9 6.2 %collective-permute-done.10 = f32[4,66,1]{2,1,0:T(8,128)S(1)} collective-permute-done((f32[4,66,1]{2,1,0:T(8,128)S(1)}, f32[4,66,1]{2,1,0:T(8,128)S(1)}, u32[]{:S(2)}, u32[]{:S(2)}) %collective-permute-start.10) | collective-permute-done | bytes 1088 | tf_op jit(solution)/shard_map/ppermute | solution.py:17
  56.1 0.8 fusion.27
  57.0 1.3 %collective-permute-start.13 = (f32[4,1,1024]{2,1,0:T(1,128)S(1)}, f32[4,1,1024]{2,1,0:T(1,128)S(1)}, u32[]{:S(2)}, u32[]{:S(2)}) collective-permute-start(f32[4,1,1024]{2,1,0:T(1,128)S(1)} %get-tuple-element.15), channel_id=1, source_target_pairs={{4,0},{8,4},{12,8},{5,1},{9,5},{13,9},{6,2},{10,6},{14,10},{7,3},{... | collective-permute-start | bytes 49160 | tf_op jit(solution)/shard_map/ppermute | solution.py:17
  58.3 5.3 %collective-permute-start.12 = (f32[4,1,1024]{2,1,0:T(1,128)S(1)}, f32[4,1,1024]{2,1,0:T(1,128)S(1)}, u32[]{:S(2)}, u32[]{:S(2)}) collective-permute-start(f32[4,1,1024]{2,1,0:T(1,128)S(1)} %get-tuple-element.16), channel_id=1, source_target_pairs={{0,4},{4,8},{8,12},{1,5},{5,9},{9,13},{2,6},{6,10},{10,14},{3,7},{... | collective-permute-start | bytes 49160 | tf_op jit(solution)/shard_map/ppermute | solution.py:16
  63.6 1.4 %collective-permute-done.12 = f32[4,1,1024]{2,1,0:T(1,128)S(1)} collective-permute-done((f32[4,1,1024]{2,1,0:T(1,128)S(1)}, f32[4,1,1024]{2,1,0:T(1,128)S(1)}, u32[]{:S(2)}, u32[]{:S(2)}) %collective-permute-start.12) | collective-permute-done | bytes 16416 | tf_op jit(solution)/shard_map/ppermute | solution.py:16
  65.0 0.1 pad_maximum_fusion.38
  65.1 0.3 collective-permute-start.14
  65.5 1.8 %collective-permute-start.15 = (f32[4,66,1]{2,1,0:T(8,128)S(1)}, f32[4,66,1]{2,1,0:T(8,128)S(1)}, u32[]{:S(2)}, u32[]{:S(2)}) collective-permute-start(f32[4,66,1]{2,1,0:T(8,128)S(1)} %get-tuple-element.8), channel_id=1, source_target_pairs={{0,1},{1,2},{2,3},{3,0},{4,5},{5,6},{6,7},{7,4},{8,9},{9,10},{10,1... | collective-permute-start | bytes 3176 | tf_op jit(solution)/shard_map/ppermute | solution.py:16
  67.2 3.1 %collective-permute-done.14 = f32[4,66,1]{2,1,0:T(8,128)S(1)} collective-permute-done((f32[4,66,1]{2,1,0:T(8,128)S(1)}, f32[4,66,1]{2,1,0:T(8,128)S(1)}, u32[]{:S(2)}, u32[]{:S(2)}) %collective-permute-start.14) | collective-permute-done | bytes 1088 | tf_op jit(solution)/shard_map/ppermute | solution.py:17
  70.3 2.1 %collective-permute-done.15 = f32[4,66,1]{2,1,0:T(8,128)S(1)} collective-permute-done((f32[4,66,1]{2,1,0:T(8,128)S(1)}, f32[4,66,1]{2,1,0:T(8,128)S(1)}, u32[]{:S(2)}, u32[]{:S(2)}) %collective-permute-start.15) | collective-permute-done | bytes 1088 | tf_op jit(solution)/shard_map/ppermute | solution.py:16
  72.4 0.8 fusion.15
  73.3 0.0 copy-start.1
  73.3 1.4 %collective-permute-start.17 = (f32[4,1,1024]{2,1,0:T(1,128)S(1)}, f32[4,1,1024]{2,1,0:T(1,128)S(1)}, u32[]{:S(2)}, u32[]{:S(2)}) collective-permute-start(f32[4,1,1024]{2,1,0:T(1,128)S(1)} %get-tuple-element.13), channel_id=1, source_target_pairs={{4,0},{8,4},{12,8},{5,1},{9,5},{13,9},{6,2},{10,6},{14,10},{7,3},{... | collective-permute-start | bytes 49160 | tf_op jit(solution)/shard_map/ppermute | solution.py:17
  74.7 5.7 %collective-permute-start.16 = (f32[4,1,1024]{2,1,0:T(1,128)S(1)}, f32[4,1,1024]{2,1,0:T(1,128)S(1)}, u32[]{:S(2)}, u32[]{:S(2)}) collective-permute-start(f32[4,1,1024]{2,1,0:T(1,128)S(1)} %get-tuple-element.14), channel_id=1, source_target_pairs={{0,4},{4,8},{8,12},{1,5},{5,9},{9,13},{2,6},{6,10},{10,14},{3,7},{... | collective-permute-start | bytes 49160 | tf_op jit(solution)/shard_map/ppermute | solution.py:16
  80.5 1.4 %collective-permute-done.16 = f32[4,1,1024]{2,1,0:T(1,128)S(1)} collective-permute-done((f32[4,1,1024]{2,1,0:T(1,128)S(1)}, f32[4,1,1024]{2,1,0:T(1,128)S(1)}, u32[]{:S(2)}, u32[]{:S(2)}) %collective-permute-start.16) | collective-permute-done | bytes 16416 | tf_op jit(solution)/shard_map/ppermute | solution.py:16
  81.9 0.1 pad_maximum_fusion.35
  82.0 1.6 %collective-permute-start.18 = (f32[4,66,1]{2,1,0:T(8,128)S(1)}, f32[4,66,1]{2,1,0:T(8,128)S(1)}, u32[]{:S(2)}, u32[]{:S(2)}) collective-permute-start(f32[4,66,1]{2,1,0:T(8,128)S(1)} %get-tuple-element.5), channel_id=1, source_target_pairs={{1,0},{2,1},{3,2},{0,3},{5,4},{6,5},{7,6},{4,7},{9,8},{10,9},{11,1... | collective-permute-start | bytes 3176 | tf_op jit(solution)/shard_map/ppermute | solution.py:17
  83.6 0.5 collective-permute-start.19
  84.1 3.1 %collective-permute-done.18 = f32[4,66,1]{2,1,0:T(8,128)S(1)} collective-permute-done((f32[4,66,1]{2,1,0:T(8,128)S(1)}, f32[4,66,1]{2,1,0:T(8,128)S(1)}, u32[]{:S(2)}, u32[]{:S(2)}) %collective-permute-start.18) | collective-permute-done | bytes 1088 | tf_op jit(solution)/shard_map/ppermute | solution.py:17
  87.2 3.4 %collective-permute-done.19 = f32[4,66,1]{2,1,0:T(8,128)S(1)} collective-permute-done((f32[4,66,1]{2,1,0:T(8,128)S(1)}, f32[4,66,1]{2,1,0:T(8,128)S(1)}, u32[]{:S(2)}, u32[]{:S(2)}) %collective-permute-start.19) | collective-permute-done | bytes 1088 | tf_op jit(solution)/shard_map/ppermute | solution.py:16
  90.6 1.8 %fusion.3 = f32[4,64,1024]{2,1,0:T(8,128)} fusion(f32[4,64,1024]{2,1,0:T(8,128)S(1)} %fusion.15, f32[4,1,1024]{2,1,0:T(1,128)S(1)} %collective-permute-done.16, f32[4,1,1024]{2,1,0:T(1,128)S(1)} %collective-permute-done.17, f32[4,66,1]{2,1,0:T(8,128)S(1)} %collective-permute-done.19, f32[4,66,1]{2,1,0:T(8,128)S(1)} %collective-permute-done.18, ...), kind=kLoop, calls=%fused_computation.4 | loop fusion | flops 5505024 | bytes 4229184 | tf_op jit(solution)/shard_map/mul | solution.py:56
  92.4 0.0 all-reduce.2.cloned.1.call-update
  92.4 21.0 %all-reduce.2.cloned.1.call-done = f32[4,64,1024]{2,1,0:T(8,128)} async-done(((f32[4,64,1024]{2,1,0:T(8,128)}), f32[4,64,1024]{2,1,0:T(8,128)}) %all-reduce.2.cloned.1.call-update) | async-done | bytes 1048592 | tf_op jit(solution)/shard_map/psum | solution.py:57
  113.4 2.3 %copy.7 = f32[4,64,1024]{2,1,0:T(8,128)} copy(f32[4,64,1024]{2,1,0:T(8,128)} %all-reduce.2.cloned.1.call-done) | data formatting | bytes 2097152
  (28 shorter events, 0.3 us)
Async XLA Ops:
  6.5 1.1 copy-start.2
  6.5 1.1 copy-start.3
  6.5 7.3 %copy-start = (f32[1,4,64,1024]{3,2,1,0:T(8,128)S(1)}, f32[1,4,64,1024]{3,2,1,0:T(8,128)}, u32[]{:S(2)}) copy-start(f32[1,4,64,1024]{3,2,1,0:T(8,128)} %param.6) | copy-start | bytes 3145732
  6.5 106.9 %all-reduce.2.cloned.1.call-start = ((), (), s32[]{:S(2)}) async-start(), calls=%async_computation | async-start | bytes 2097152 | tf_op jit(solution)/shard_map/psum | solution.py:57
  7.7 14.1 %collective-permute-start = (f32[3,4,1024]{2,1,0:T(4,128)S(1)}, f32[3,4,1024]{2,1,0:T(4,128)S(1)}, u32[]{:S(2)}, u32[]{:S(2)}) collective-permute-start(f32[3,4,1024]{2,1,0:T(4,128)S(1)} %get-tuple-element.25), channel_id=1, source_target_pairs={{0,4},{4,8},{8,12},{1,5},{5,9},{9,13},{2,6},{6,10},{10,14},{3,7},{... | collective-permute-start | bytes 147464 | tf_op jit(solution)/shard_map/ppermute | solution.py:16
  12.6 9.3 %collective-permute-start.1 = (f32[3,4,1024]{2,1,0:T(4,128)S(1)}, f32[3,4,1024]{2,1,0:T(4,128)S(1)}, u32[]{:S(2)}, u32[]{:S(2)}) collective-permute-start(f32[3,4,1024]{2,1,0:T(4,128)S(1)} %get-tuple-element.26), channel_id=1, source_target_pairs={{4,0},{8,4},{12,8},{5,1},{9,5},{13,9},{6,2},{10,6},{14,10},{7,3},{... | collective-permute-start | bytes 147464 | tf_op jit(solution)/shard_map/ppermute | solution.py:17
  15.3 10.4 %collective-permute-start.5 = (f32[4,1,1024]{2,1,0:T(1,128)S(1)}, f32[4,1,1024]{2,1,0:T(1,128)S(1)}, u32[]{:S(2)}, u32[]{:S(2)}) collective-permute-start(f32[4,1,1024]{2,1,0:T(1,128)S(1)} %get-tuple-element.19), channel_id=1, source_target_pairs={{4,0},{8,4},{12,8},{5,1},{9,5},{13,9},{6,2},{10,6},{14,10},{7,3},{... | collective-permute-start | bytes 49160 | tf_op jit(solution)/shard_map/ppermute | solution.py:17
  16.6 9.1 %collective-permute-start.4 = (f32[4,1,1024]{2,1,0:T(1,128)S(1)}, f32[4,1,1024]{2,1,0:T(1,128)S(1)}, u32[]{:S(2)}, u32[]{:S(2)}) collective-permute-start(f32[4,1,1024]{2,1,0:T(1,128)S(1)} %get-tuple-element.20), channel_id=1, source_target_pairs={{0,4},{4,8},{8,12},{1,5},{5,9},{9,13},{2,6},{6,10},{10,14},{3,7},{... | collective-permute-start | bytes 49160 | tf_op jit(solution)/shard_map/ppermute | solution.py:16
  22.1 7.7 %collective-permute-start.3 = (f32[3,72,4]{2,1,0:T(8,128)S(1)}, f32[3,72,4]{2,1,0:T(8,128)S(1)}, u32[]{:S(2)}, u32[]{:S(2)}) collective-permute-start(f32[3,72,4]{2,1,0:T(8,128)S(1)} %get-tuple-element.23), channel_id=1, source_target_pairs={{1,0},{2,1},{3,2},{0,3},{5,4},{6,5},{7,6},{4,7},{9,8},{10,9},{11,1... | collective-permute-start | bytes 10376 | tf_op jit(solution)/shard_map/ppermute | solution.py:17
  25.7 8.0 %collective-permute-start.2 = (f32[3,72,4]{2,1,0:T(8,128)S(1)}, f32[3,72,4]{2,1,0:T(8,128)}, u32[]{:S(2)}, u32[]{:S(2)}) collective-permute-start(f32[3,72,4]{2,1,0:T(8,128)S(1)} %get-tuple-element.24), channel_id=1, source_target_pairs={{0,1},{1,2},{2,3},{3,0},{4,5},{5,6},{6,7},{7,4},{8,9},{9,10},{10,1... | collective-permute-start | bytes 10376 | tf_op jit(solution)/shard_map/ppermute | solution.py:16
  25.9 9.9 %collective-permute-start.6 = (f32[4,66,1]{2,1,0:T(8,128)S(1)}, f32[4,66,1]{2,1,0:T(8,128)S(1)}, u32[]{:S(2)}, u32[]{:S(2)}) collective-permute-start(f32[4,66,1]{2,1,0:T(8,128)S(1)} %get-tuple-element.11), channel_id=1, source_target_pairs={{1,0},{2,1},{3,2},{0,3},{5,4},{6,5},{7,6},{4,7},{9,8},{10,9},{11,1... | collective-permute-start | bytes 3176 | tf_op jit(solution)/shard_map/ppermute | solution.py:17
  29.7 8.0 %collective-permute-start.7 = (f32[4,66,1]{2,1,0:T(8,128)S(1)}, f32[4,66,1]{2,1,0:T(8,128)}, u32[]{:S(2)}, u32[]{:S(2)}) collective-permute-start(f32[4,66,1]{2,1,0:T(8,128)S(1)} %get-tuple-element.12), channel_id=1, source_target_pairs={{0,1},{1,2},{2,3},{3,0},{4,5},{5,6},{6,7},{7,4},{8,9},{9,10},{10,1... | collective-permute-start | bytes 3176 | tf_op jit(solution)/shard_map/ppermute | solution.py:16
  29.7 0.6 copy-start.4
  39.6 6.7 %collective-permute-start.9 = (f32[4,1,1024]{2,1,0:T(1,128)S(1)}, f32[4,1,1024]{2,1,0:T(1,128)S(1)}, u32[]{:S(2)}, u32[]{:S(2)}) collective-permute-start(f32[4,1,1024]{2,1,0:T(1,128)S(1)} %get-tuple-element.17), channel_id=1, source_target_pairs={{4,0},{8,4},{12,8},{5,1},{9,5},{13,9},{6,2},{10,6},{14,10},{7,3},{... | collective-permute-start | bytes 49160 | tf_op jit(solution)/shard_map/ppermute | solution.py:17
  40.9 6.8 %collective-permute-start.8 = (f32[4,1,1024]{2,1,0:T(1,128)S(1)}, f32[4,1,1024]{2,1,0:T(1,128)S(1)}, u32[]{:S(2)}, u32[]{:S(2)}) collective-permute-start(f32[4,1,1024]{2,1,0:T(1,128)S(1)} %get-tuple-element.18), channel_id=1, source_target_pairs={{0,4},{4,8},{8,12},{1,5},{5,9},{9,13},{2,6},{6,10},{10,14},{3,7},{... | collective-permute-start | bytes 49160 | tf_op jit(solution)/shard_map/ppermute | solution.py:16
  47.8 8.3 %collective-permute-start.10 = (f32[4,66,1]{2,1,0:T(8,128)S(1)}, f32[4,66,1]{2,1,0:T(8,128)S(1)}, u32[]{:S(2)}, u32[]{:S(2)}) collective-permute-start(f32[4,66,1]{2,1,0:T(8,128)S(1)} %get-tuple-element.9), channel_id=1, source_target_pairs={{1,0},{2,1},{3,2},{0,3},{5,4},{6,5},{7,6},{4,7},{9,8},{10,9},{11,1... | collective-permute-start | bytes 3176 | tf_op jit(solution)/shard_map/ppermute | solution.py:17
  49.0 7.1 %collective-permute-start.11 = (f32[4,66,1]{2,1,0:T(8,128)S(1)}, f32[4,66,1]{2,1,0:T(8,128)S(1)}, u32[]{:S(2)}, u32[]{:S(2)}) collective-permute-start(f32[4,66,1]{2,1,0:T(8,128)S(1)} %get-tuple-element.10), channel_id=1, source_target_pairs={{0,1},{1,2},{2,3},{3,0},{4,5},{5,6},{6,7},{7,4},{8,9},{9,10},{10,1... | collective-permute-start | bytes 3176 | tf_op jit(solution)/shard_map/ppermute | solution.py:16
  57.0 6.6 %collective-permute-start.13 = (f32[4,1,1024]{2,1,0:T(1,128)S(1)}, f32[4,1,1024]{2,1,0:T(1,128)S(1)}, u32[]{:S(2)}, u32[]{:S(2)}) collective-permute-start(f32[4,1,1024]{2,1,0:T(1,128)S(1)} %get-tuple-element.15), channel_id=1, source_target_pairs={{4,0},{8,4},{12,8},{5,1},{9,5},{13,9},{6,2},{10,6},{14,10},{7,3},{... | collective-permute-start | bytes 49160 | tf_op jit(solution)/shard_map/ppermute | solution.py:17
  58.3 6.7 %collective-permute-start.12 = (f32[4,1,1024]{2,1,0:T(1,128)S(1)}, f32[4,1,1024]{2,1,0:T(1,128)S(1)}, u32[]{:S(2)}, u32[]{:S(2)}) collective-permute-start(f32[4,1,1024]{2,1,0:T(1,128)S(1)} %get-tuple-element.16), channel_id=1, source_target_pairs={{0,4},{4,8},{8,12},{1,5},{5,9},{9,13},{2,6},{6,10},{10,14},{3,7},{... | collective-permute-start | bytes 49160 | tf_op jit(solution)/shard_map/ppermute | solution.py:16
  65.1 5.2 %collective-permute-start.14 = (f32[4,66,1]{2,1,0:T(8,128)S(1)}, f32[4,66,1]{2,1,0:T(8,128)S(1)}, u32[]{:S(2)}, u32[]{:S(2)}) collective-permute-start(f32[4,66,1]{2,1,0:T(8,128)S(1)} %get-tuple-element.7), channel_id=1, source_target_pairs={{1,0},{2,1},{3,2},{0,3},{5,4},{6,5},{7,6},{4,7},{9,8},{10,9},{11,1... | collective-permute-start | bytes 3176 | tf_op jit(solution)/shard_map/ppermute | solution.py:17
  65.5 6.9 %collective-permute-start.15 = (f32[4,66,1]{2,1,0:T(8,128)S(1)}, f32[4,66,1]{2,1,0:T(8,128)S(1)}, u32[]{:S(2)}, u32[]{:S(2)}) collective-permute-start(f32[4,66,1]{2,1,0:T(8,128)S(1)} %get-tuple-element.8), channel_id=1, source_target_pairs={{0,1},{1,2},{2,3},{3,0},{4,5},{5,6},{6,7},{7,4},{8,9},{9,10},{10,1... | collective-permute-start | bytes 3176 | tf_op jit(solution)/shard_map/ppermute | solution.py:16
  73.3 17.3 %copy-start.1 = (f32[1,4,64,1024]{3,2,1,0:T(8,128)S(1)}, f32[1,4,64,1024]{3,2,1,0:T(8,128)}, u32[]{:S(2)}) copy-start(f32[1,4,64,1024]{3,2,1,0:T(8,128)} %param.6) | copy-start | bytes 3145732
  73.3 7.2 %collective-permute-start.17 = (f32[4,1,1024]{2,1,0:T(1,128)S(1)}, f32[4,1,1024]{2,1,0:T(1,128)S(1)}, u32[]{:S(2)}, u32[]{:S(2)}) collective-permute-start(f32[4,1,1024]{2,1,0:T(1,128)S(1)} %get-tuple-element.13), channel_id=1, source_target_pairs={{4,0},{8,4},{12,8},{5,1},{9,5},{13,9},{6,2},{10,6},{14,10},{7,3},{... | collective-permute-start | bytes 49160 | tf_op jit(solution)/shard_map/ppermute | solution.py:17
  74.7 7.2 %collective-permute-start.16 = (f32[4,1,1024]{2,1,0:T(1,128)S(1)}, f32[4,1,1024]{2,1,0:T(1,128)S(1)}, u32[]{:S(2)}, u32[]{:S(2)}) collective-permute-start(f32[4,1,1024]{2,1,0:T(1,128)S(1)} %get-tuple-element.14), channel_id=1, source_target_pairs={{0,4},{4,8},{8,12},{1,5},{5,9},{9,13},{2,6},{6,10},{10,14},{3,7},{... | collective-permute-start | bytes 49160 | tf_op jit(solution)/shard_map/ppermute | solution.py:16
  82.0 5.2 %collective-permute-start.18 = (f32[4,66,1]{2,1,0:T(8,128)S(1)}, f32[4,66,1]{2,1,0:T(8,128)S(1)}, u32[]{:S(2)}, u32[]{:S(2)}) collective-permute-start(f32[4,66,1]{2,1,0:T(8,128)S(1)} %get-tuple-element.5), channel_id=1, source_target_pairs={{1,0},{2,1},{3,2},{0,3},{5,4},{6,5},{7,6},{4,7},{9,8},{10,9},{11,1... | collective-permute-start | bytes 3176 | tf_op jit(solution)/shard_map/ppermute | solution.py:17
  83.6 6.9 %collective-permute-start.19 = (f32[4,66,1]{2,1,0:T(8,128)S(1)}, f32[4,66,1]{2,1,0:T(8,128)S(1)}, u32[]{:S(2)}, u32[]{:S(2)}) collective-permute-start(f32[4,66,1]{2,1,0:T(8,128)S(1)} %get-tuple-element.6), channel_id=1, source_target_pairs={{0,1},{1,2},{2,3},{3,0},{4,5},{5,6},{6,7},{7,4},{8,9},{9,10},{10,1... | collective-permute-start | bytes 3176 | tf_op jit(solution)/shard_map/ppermute | solution.py:16
Sparse Core Ops, SparseCore 0:
  92.6 20.8 all-reduce.1
where the time goes:
time: 123 us
  waiting for transfers between devices  48.5 us (39%)
  starting transfers between devices  46.8 us (38%)
  between operations  13.7 us (11%)
  other arithmetic  8.6 us (7%)
  local copies, waits for them, and re-layouts  5.02 us (4%)
    ppermute x10, starting transfers between devices, extended(): before = lax.ppermute(last, axis, up)  29.5 us
    psum x1, waiting for transfers between devices, shards(): return lax.psum(term, 'mem')  21 us
    ppermute x10, starting transfers between devices, extended(): after = lax.ppermute(initial, axis, down)  17.3 us
    ppermute x10, waiting for transfers between devices, extended(): before = lax.ppermute(last, axis, up)  15 us
    ppermute x10, waiting for transfers between devices, extended(): after = lax.ppermute(initial, axis, down)  12.5 us
    sub x3, other arithmetic, sweep(): return centre + go_east - go_west + go_north - go_south  3.43 us
    unnamed x11, local copies, waits for them, and re-layouts  2.97 us
  transfers between devices with their start and end apart: 21, of which 11 were waited for; matrix products, arithmetic and copies ran while one was open for 3% of the time, Pallas kernels for 0%

commit v1 on v0

v1 whole, which is shorter than its diff:
```python
import functools
import jax
import jax.numpy as jnp
from jax import lax
from jax.experimental import pallas as pl
from jax.experimental.pallas import tpu as pltpu
from jax.sharding import PartitionSpec as P

STEPS = 4
TILE = 8
LANES = 128
AXES = ("mem", "gy", "gx")
LEFT = 2 * TILE
DEPTH = LANES + 2 * LEFT
LOW = slice(LEFT - TILE, LEFT)
HIGH = slice(LEFT + LANES, LEFT + LANES + TILE)
BODY = slice(LEFT, LEFT + LANES)
WIDE = slice(LEFT - TILE, LEFT + LANES + TILE)
AFTER = slice(LEFT - TILE + 1, LEFT + LANES + TILE + 1)

F32 = jnp.float32
VMEM = pl.BlockSpec(memory_space=pltpu.VMEM)
HBM = pl.BlockSpec(memory_space=pltpu.HBM)


def half_of(gy_size):
    core = lax.rem(lax.axis_index("mem"), 2)
    later = (lax.axis_index("gy") >= gy_size // 2).astype(jnp.int32)
    return lax.rem(core + later, 2)


def kept(*shape):
    return pltpu.VMEM(shape, F32)


def pinned(x):
    return pltpu.with_memory_space_constraint(x, pltpu.VMEM)


def in_hbm(x):
    return pltpu.with_memory_space_constraint(x, pltpu.HBM)


def tile(c):
    return slice(c * LANES, (c + 1) * LANES)


def lane_ids(rows):
    return lax.broadcasted_iota(jnp.int32, (rows, LANES), 1)


def row_start(half, rows):
    return pl.multiple_of(half * (rows // 2 - TILE), TILE)


def run(copies):
    for copy in copies:
        copy.start()
    for copy in copies:
        copy.wait()


def partner_rows_kernel(gy_size, members, out, sem):
    rows = members.shape[2]
    part = pl.ds(row_start(1 - half_of(gy_size), rows), out.shape[2])
    run([
        pltpu.make_async_copy(members.at[0, :, part, tile(c)], out.at[:, c], sem.at[c])
        for c in range(out.shape[1])
    ])


def load_kernel(gy_size, members, increment, zonal, merid, mask, own, forcing, zm, mm, wet, mask_buf, sems):
    rows = increment.shape[1]
    tiles, tall = zm.shape[:2]
    part = pl.ds(row_start(half_of(gy_size), rows), tall)
    flat = [
        [pltpu.make_async_copy(ref.at[part, tile(c)], buf.at[c], sems.at[k, c]) for c in range(tiles)]
        for k, (ref, buf) in enumerate(((mask, mask_buf), (zonal, zm), (merid, mm)))
    ]
    deep = [
        pltpu.make_async_copy(increment.at[:, part, tile(c)], forcing.at[:, c], sems.at[3, c]) for c in range(tiles)
    ]
    last = [
        pltpu.make_async_copy(members.at[0, :, part, tile(c)], own.at[:, c], sems.at[4, c]) for c in range(tiles)
    ]
    for copy in sum(flat, []) + deep + last:
        copy.start()
    for copy in sum(flat, []):
        copy.wait()
    wet[...] = mask_buf[...].astype(F32)
    zm[...] = zm[...] * wet[...]
    mm[...] = mm[...] * wet[...]
    for copy in deep:
        copy.wait()
    forcing[...] = forcing[...] * wet[...][None]
    for copy in last:
        copy.wait()


def pack_rows_kernel(gy_size, own, other, forcing, zm, mm, wet, strip):
    levels, tiles, tall, _ = own.shape
    half = half_of(gy_size)
    j = lax.axis_index("gy")
    same_core = jnp.where(half == 0, j == gy_size // 2, j == gy_size // 2 - 1)
    edge = pl.ds(pl.multiple_of(half * (tall - TILE), TILE), TILE)
    low = lax.broadcasted_iota(jnp.int32, (tiles, TILE, LANES), 1) < TILE // 2

    def put(place, first, second):
        first = jnp.where(half == 0, first, pltpu.roll(first, TILE // 2, 1))
        second = jnp.where(half == 0, pltpu.roll(second, TILE // 2, 1), second)
        strip[place] = jnp.where(low, first, second)

    for level in range(levels):
        force = forcing[level, :, edge, :]
        mine = own[level, :, edge, :] * force
        theirs = other[level, :, edge, :] * force
        put(level, jnp.where(same_core, mine, theirs), jnp.where(same_core, theirs, mine))
    put(levels, zm[:, edge, :], mm[:, edge, :])
    put(levels + 1, wet[:, edge, :], wet[:, edge, :])


def mirror(ref, p):
    ref[p, LOW, :] = pltpu.roll(ref[p, slice(LEFT + LANES - TILE, LEFT + LANES), :], 1, 1)
    ref[p, HIGH, :] = pltpu.roll(ref[p, slice(LEFT, LEFT + TILE), :], LANES - 1, 1)


def faces_east(east, zon, wets, p):
    east[p, WIDE, :] = zon[p, WIDE, :] * wets[p, AFTER, :]


def faces_north(north, mer, wets, p):
    north[p, WIDE, :] = mer[p, WIDE, :] * wets[p + 1, WIDE, :]


def edge_strips(west_out, east_out, u, zon, mer, wets, p, at):
    slot = lane_ids(4) % TILE
    for out, rows, base in ((west_out, slice(LEFT, LEFT + 4), 0), (east_out, slice(LEFT + LANES - 4, LEFT + LANES), 7)):
        sign = 1 if base == 0 else -1
        value = pltpu.roll(u[p, rows, :], (7 - base - base) % LANES, 1)
        for k, ref in enumerate((zon, mer, wets)):
            here = 7 - base - sign * (k + 1)
            value = jnp.where(slot == here, pltpu.roll(ref[p, rows, :], (here - base) % LANES, 1), value)
        out[at, :] = value


def turn(ref, start, height):
    parts = [ref[pl.ds(s, TILE, stride=height), :] for s in start]
    return jnp.concatenate(parts, axis=0).T


def prepare_kernel(gy_size, own, other, forcing, zm, mm, wet, u, zon, mer, wets, east, north, west_out, east_out, plain, flat):
    levels, tiles, tall, _ = own.shape
    full = tall + TILE
    planes = full // 2
    half = half_of(gy_size)
    lead = (1 - half) * TILE
    for f in range(2 * levels):
        member = (own, other)[f % 2]
        for c in range(tiles):
            base = (f * tiles + c) * full
            plain[pl.ds(pl.multiple_of(base + lead, TILE), tall), :] = member[f // 2, c] * forcing[f // 2, c]
            plain[pl.ds(pl.multiple_of(base + half * tall, TILE), TILE), :] = jnp.zeros((TILE, LANES), F32)
    for k, ref in enumerate((zm, mm, wet)):
        for c in range(tiles):
            base = (k * tiles + c) * full
            flat[pl.ds(pl.multiple_of(base + lead, TILE), tall), :] = ref[c]
            flat[pl.ds(pl.multiple_of(base + half * tall, TILE), TILE), :] = jnp.zeros((TILE, LANES), F32)
    blank = jnp.zeros((TILE, LANES), F32)
    for ref in (u, zon, mer, wets, east, north):
        for p in range(planes + 2):
            ref[p, slice(0, TILE), :] = blank
            ref[p, slice(DEPTH - TILE, DEPTH), :] = blank
    for q in range(planes):
        u[q + 1, BODY, :] = turn(
            plain, [f * tiles * full + ch * planes + q for f in range(2 * levels) for ch in range(2)], full
        )
        for k, ref in enumerate((zon, mer, wets)):
            ref[q + 1, BODY, :] = turn(
                flat, [k * tiles * full + ch * planes + q for f in range(2 * levels) for ch in range(2)], full
            )
        for ref in (u, zon, mer, wets):
            mirror(ref, q + 1)
    wets[planes + 1, WIDE, :] = pltpu.roll(wets[1, WIDE, :], LANES - TILE, 1)
    for q in range(planes):
        faces_east(east, zon, wets, q + 1)
        faces_north(north, mer, wets, q + 1)
        edge_strips(west_out, east_out, u, zon, mer, wets, q + 1, slice(4 * q, 4 * q + 4))


def halo_rows_kernel(gy_size, strip, *refs):
    u, zon, mer, wets, east, north, west_out, east_out = refs[8:]
    tiles = TILE
    levels = strip.shape[0] // (tiles * TILE) - 2
    planes = u.shape[0] - 2
    half = half_of(gy_size)
    mine = (lane_ids(LANES) // TILE) % 2 == half
    first = 1 + 4 + half * (planes // 2)
    for r in range(4):
        p = first + r
        for ref, places in (
            (u, range(2 * levels)),
            (zon, [2 * levels] * 2 * levels),
            (mer, [2 * levels + 1] * 2 * levels),
            (wets, [2 * levels + 2] * 2 * levels),
        ):
            new = turn(strip, [k // 2 * tiles * TILE + 4 * (k % 2) + r for k in places for ch in range(2)], TILE)
            ref[p, BODY, :] = jnp.where(mine, new, ref[p, BODY, :])
            mirror(ref, p)
    for r in range(-1, 4):
        p = first + r
        if r >= 0:
            faces_east(east, zon, wets, p)
            edge_strips(west_out, east_out, u, zon, mer, wets, p, pl.ds(4 * (p - 1), 4))
        faces_north(north, mer, wets, p)


def diffuse_kernel(gy_size, from_east, from_west, own, other, *refs):
    u, zon, mer, wets, east, north = refs[6:12]
    out, u_next, plain = refs[12:]
    levels, tiles, tall, _ = own.shape
    planes = u.shape[0] - 2
    full = 2 * planes
    half = half_of(gy_size)
    slot = lane_ids(4) % TILE
    for strip, rows, base in (
        (from_west, slice(LEFT - 4, LEFT), 0),
        (from_east, slice(LEFT + LANES, LEFT + LANES + 4), 7),
    ):
        sign = 1 if base == 0 else -1
        for k, ref in enumerate((u, zon, mer, wets)):
            value = strip[...]
            if k:
                value = pltpu.roll(value, (-sign * k) % LANES, 1)
            for q in range(planes):
                ref[q + 1, rows, :] = jnp.where(slot == base, value[4 * q : 4 * q + 4], ref[q + 1, rows, :])
    wets[planes + 1, WIDE, :] = pltpu.roll(wets[1, WIDE, :], LANES - TILE, 1)
    for q in range(planes):
        for rows in (LEFT - TILE, LEFT + LANES - TILE, LEFT + LANES):
            at = slice(rows, rows + TILE)
            east[q + 1, at, :] = zon[q + 1, at, :] * wets[q + 1, slice(rows + 1, rows + TILE + 1), :]
            north[q + 1, at, :] = mer[q + 1, at, :] * wets[q + 2, at, :]
    north[0, WIDE, :] = pltpu.roll(north[planes, WIDE, :], TILE, 1)

    source, target = u, u_next
    for step in range(STEPS):
        source[0, WIDE, :] = pltpu.roll(source[planes, WIDE, :], TILE, 1)
        source[planes + 1, WIDE, :] = pltpu.roll(source[1, WIDE, :], LANES - TILE, 1)
        if step == 0:
            blank = jnp.zeros((TILE, LANES), F32)
            for p in range(planes + 2):
                target[p, slice(0, TILE), :] = blank
                target[p, slice(DEPTH - TILE, DEPTH), :] = blank
        span = BODY if step == STEPS - 1 else WIDE
        for start in range(span.start, span.stop, TILE):
            at, ahead, behind = slice(start, start + TILE), slice(start + 1, start + 1 + TILE), slice(start - 1, start - 1 + TILE)
            here = source[1, at, :]
            south = north[0, at, :] * (here - source[0, at, :])
            for p in range(1, planes + 1):
                above = source[p + 1, at, :]
                flux = north[p, at, :] * (above - here)
                go_east = east[p, at, :] * (source[p, ahead, :] - here)
                go_west = east[p, behind, :] * (here - source[p, behind, :])
                target[p, at, :] = here + go_east - go_west + flux - south
                here, south = above, flux
        source, target = target, source
    for q in range(planes):
        flat = source[q + 1, BODY, :].T
        for f in range(2 * levels):
            for ch in range(2):
                group = (2 * f + ch) * tiles
                plain[pl.ds(f * tiles * full + ch * planes + q, tiles, stride=full), :] = flat[group : group + tiles]
    rows = tall - TILE
    part = pl.ds(pl.multiple_of(half * TILE, TILE), rows)
    for level in range(levels):
        for c in range(tiles):
            a, b = (((2 * level + k) * tiles + c) * full + TILE for k in range(2))
            out[level, c] = (
                own[level, c, part, :] * plain[pl.ds(a, rows), :] + other[level, c, part, :] * plain[pl.ds(b, rows), :]
            )


def join_kernel(gy_size, mine, theirs, out, sems):
    half = half_of(gy_size)
    tiles, rows = mine.shape[1:3]
    run([
        pltpu.make_async_copy(
            ref.at[:, c], out.at[:, pl.ds(pl.multiple_of(where * rows, TILE), rows), tile(c)], sems.at[k, c]
        )
        for k, (ref, where) in enumerate(((mine, half), (theirs, 1 - half)))
        for c in range(tiles)
    ])


def shards(sizes, increment, members, zonal_diff, merid_diff, sea_mask):
    n_mem, n_gy, n_gx = sizes
    levels, rows, width = increment.shape
    tiles = width // LANES
    mid = rows // 2
    tall = mid + TILE
    full = tall + TILE
    planes = full // 2
    assert tiles == TILE and 4 * levels * tiles == LANES and n_mem % 2 == 0

    def call(kernel, ins, specs, outs, scratch=(), out_specs=None, aliases={}):
        return pl.pallas_call(
            functools.partial(kernel, n_gy),
            out_shape=outs,
            in_specs=specs,
            out_specs=out_specs if out_specs is not None else jax.tree.map(lambda _: VMEM, outs),
            scratch_shapes=scratch,
            input_output_aliases=aliases,
            compiler_params=pltpu.CompilerParams(vmem_limit_bytes=40 * 1024 * 1024),
        )(*ins)

    def swap(x):
        return lax.ppermute(x, "mem", [(i, i ^ 1) for i in range(n_mem)])

    def along(x, shift):
        return lax.ppermute(x, "gx", [(i, (i + shift) % n_gx) for i in range(n_gx)])

    def across(x):
        def place(chip, core, j, i):
            return ((2 * chip + core) * n_gy + j) * n_gx + i

        first = [0 if j < n_gy // 2 else 1 for j in range(n_gy)]
        pairs = []
        for chip in range(n_mem // 2):
            for j in range(n_gy - 1):
                for i in range(n_gx):
                    a = place(chip, 1 - first[j], j, i)
                    b = place(chip, first[j + 1], j + 1, i)
                    pairs += [(a, b), (b, a)]
        return lax.ppermute(x, AXES, pairs)

    increment, members, zonal_diff, merid_diff, sea_mask = (
        in_hbm(x) for x in (increment, members, zonal_diff, merid_diff, sea_mask)
    )
    sent = call(
        partner_rows_kernel, [members], [HBM], kept(levels, tiles, tall, LANES), [pltpu.SemaphoreType.DMA((tiles,))]
    )
    other = pinned(swap(sent))
    local = call(
        load_kernel,
        [members, increment, zonal_diff, merid_diff, sea_mask],
        [HBM] * 5,
        [kept(levels, tiles, tall, LANES)] * 2 + [kept(tiles, tall, LANES)] * 3,
        [pltpu.VMEM((tiles, tall, LANES), jnp.int32), pltpu.SemaphoreType.DMA((5, tiles))],
    )
    local = [pinned(x) for x in local]
    local = [local[0], other] + local[1:]
    strip = call(pack_rows_kernel, local, [VMEM] * 6, kept(levels + 2, tiles, TILE, LANES))
    strip = pinned(across(strip).reshape((levels + 2) * tiles * TILE, LANES))
    turned = [kept(planes + 2, DEPTH, LANES)] * 6 + [kept(4 * planes, LANES)] * 2
    state = call(
        prepare_kernel,
        local,
        [VMEM] * 6,
        turned,
        [pltpu.VMEM((2 * levels * tiles * full, LANES), F32), pltpu.VMEM((3 * tiles * full, LANES), F32)],
    )
    state = call(
        halo_rows_kernel,
        [strip] + [pinned(x) for x in state],
        [VMEM] * 9,
        turned,
        aliases={k + 1: k for k in range(8)},
    )
    from_west = pinned(along(state[7], 1))
    from_east = pinned(along(state[6], -1))
    mine = call(
        diffuse_kernel,
        [from_east, from_west] + local[:2] + [pinned(x) for x in state[:6]],
        [VMEM] * 10,
        turned[:6] + [kept(levels, tiles, mid, LANES)],
        [
            pltpu.VMEM((planes + 2, DEPTH, LANES), F32),
            pltpu.VMEM((2 * levels * tiles * full, LANES), F32),
        ],
        aliases={k + 4: k for k in range(6)},
    )[6]
    if n_mem > 2:
        mine = lax.psum(mine, "mem", axis_index_groups=[list(range(k, n_mem, 2)) for k in range(2)])
    theirs = swap(mine)
    return call(
        join_kernel,
        [pinned(mine), pinned(theirs)],
        [VMEM] * 2,
        jax.ShapeDtypeStruct(increment.shape, F32),
        [pltpu.SemaphoreType.DMA((2, tiles))],
        HBM,
    )


def solution(mesh):
    return jax.shard_map(
        functools.partial(shards, tuple(mesh.shape[axis] for axis in AXES)),
        mesh=mesh,
        in_specs=(
            P(None, "gy", "gx"),
            P("mem", None, "gy", "gx"),
            P("gy", "gx"),
            P("gy", "gx"),
            P("gy", "gx"),
        ),
        out_specs=P(None, "gy", "gx"),
        check_vma=False,
    )
```

time: 123 us -> 30.3 us (0.25)
  waiting for transfers between devices: 48.5 us -> 7.44 us
  starting transfers between devices: 46.8 us -> 10.7 us
  between operations: 13.7 us -> 0.07 us
  Pallas kernels: 0 us -> 11.9 us
  other arithmetic: 8.6 us -> 0 us
  local copies, waits for them, and re-layouts: 5.02 us -> 0 us
    ppermute x20 -> x5, starting transfers between devices: 46.8 us -> 10.7 us  [the longest x2 5.17 us: swap(): return lax.ppermute(x, 'mem', [(i, i ^ 1) for i in range(n_mem)])]
    psum x1 -> x0, waiting for transfers between devices: 21 us -> none  [shards(): return lax.psum(term, 'mem')]
    ppermute x20 -> x5, waiting for transfers between devices: 27.5 us -> 7.44 us  [the longest x2 5.9 us: along(): return lax.ppermute(x, 'gx', [(i, (i + shift) % n_gx) for i in range(n_gx)])]
    pallas_call x0 -> x7, Pallas kernels: none -> 11.9 us  [call(): pl.pallas_call(functools.partial(kernel, n_gy), out_shape=outs, in_specs=...]
    mul x4 -> x0, other arithmetic: 3.46 us -> none  [the longest x1 1.82 us: shards(): term = member * field]
    sub x3 -> x0, other arithmetic: 3.43 us -> none  [sweep(): return centre + go_east - go_west + go_north - go_south]
    unnamed x11 -> x0, local copies, waits for them, and re-layouts: 2.97 us -> none
    concatenate x1 -> x0, local copies, waits for them, and re-layouts: 1.43 us -> none  [extended(): shard = jnp.concatenate([before, shard, after], axis=dim)]
  transfers between devices with their start and end apart: 21 -> 5, of which waited for: 11 -> 3; matrix products, arithmetic and copies ran while one was open for 3% -> 0% of each run, Pallas kernels for 0% -> 15%
where the time goes in v1:
time: 30.3 us; the launch traced here: 30.1 us
  Pallas kernels  11.9 us (39%)
  starting transfers between devices  10.7 us (35%)
  waiting for transfers between devices  7.44 us (25%)
    pallas_call x7, Pallas kernels, call(): pl.pallas_call(functools.partial(kernel, n_gy), out_shape=outs, in_specs=...  11.9 us
    ppermute x2, waiting for transfers between devices, along(): return lax.ppermute(x, 'gx', [(i, (i + shift) % n_gx) for i in range(n_gx)])  5.9 us
    ppermute x2, starting transfers between devices, swap(): return lax.ppermute(x, 'mem', [(i, i ^ 1) for i in range(n_mem)])  5.17 us
    ppermute x2, starting transfers between devices, along(): return lax.ppermute(x, 'gx', [(i, (i + shift) % n_gx) for i in range(n_gx)])  4.81 us
    ppermute x2, waiting for transfers between devices, swap(): return lax.ppermute(x, 'mem', [(i, i ^ 1) for i in range(n_mem)])  1.54 us
    ppermute x1, starting transfers between devices, across(): return lax.ppermute(x, AXES, pairs)  0.67 us
  transfers between devices with their start and end apart: 5, of which 3 were waited for; matrix products, arithmetic and copies ran while one was open for 0% of the time, Pallas kernels for 15%

profile of v1, /device:TPU:0, one launch (start us, length us, event | category | flops | bytes accessed | tf_op | source)
XLA Modules:
  0.0 30.1 jit_solution(13229542438134713186)
XLA Ops:
  0.0 1.2 %shard_map.56 = f32[4,8,40,128]{3,2,1,0:T(8,128)S(1)} custom-call(f32[1,4,64,1024]{3,2,1,0:T(8,128)} %members.3), custom_call_target="tpu_custom_call" | custom-call | tf_op jit(solution)/shard_map/pallas_call | solution.py:305
  1.3 0.5 %collective-permute-start = (f32[4,8,40,128]{3,2,1,0:T(8,128)S(1)}, f32[4,8,40,128]{3,2,1,0:T(8,128)S(1)}, u32[]{:S(2)}, u32[]{:S(2)}) collective-permute-start(f32[4,8,40,128]{3,2,1,0:T(8,128)S(1)} %shard_map.56), channel_id=1, source_target_pairs={{0,16},{16,0},{1,17},{17,1},{2,18},{18,2},{3,19},{19,3},{4,20},{20... | collective-permute-start | bytes 1966088 | tf_op jit(solution)/shard_map/ppermute | solution.py:316
  1.8 1.9 %shard_map.55 = (f32[4,8,40,128]{3,2,1,0:T(8,128)S(1)}, f32[4,8,40,128]{3,2,1,0:T(8,128)S(1)}, f32[8,40,128]{2,1,0:T(8,128)S(1)}, f32[8,40,128]{2,1,0:T(8,128)S(1)}, f32[8,40,128]{2,1,0:T(8,128)S(1)}) custom-call(f32[1,4,64,1024]{3,2,1,0:T(8,128)} %members.3, f32[4,64,1024]{2,1,0:T(8,128)} %increment.1, f32[64,1024]{1,0:T(8,128)} %zonal.1, ...), custom_call_target="tpu_custom_call" | custom-call | tf_op jit(solution)/shard_map/pallas_call | solution.py:305
  3.7 0.0 collective-permute-done.other
  3.7 0.1 shard_map.57
  3.8 0.7 %collective-permute-start.1 = (f32[6,8,8,128]{3,2,1,0:T(8,128)S(1)}, f32[6,8,8,128]{3,2,1,0:T(8,128)S(1)}, u32[]{:S(2)}, u32[]{:S(2)}) collective-permute-start(f32[6,8,8,128]{3,2,1,0:T(8,128)S(1)} %shard_map.57), channel_id=1, source_target_pairs={{16,4},{4,16},{17,5},{5,17},{18,6},{6,18},{19,7},{7,19},{20,24},{2... | collective-permute-start | bytes 589832 | tf_op jit(solution)/shard_map/ppermute | solution.py:333
  4.5 2.7 %shard_map.58 = (f32[26,160,128]{2,1,0:T(8,128)S(1)}, f32[26,160,128]{2,1,0:T(8,128)S(1)}, f32[26,160,128]{2,1,0:T(8,128)S(1)}, f32[26,160,128]{2,1,0:T(8,128)S(...) custom-call(f32[4,8,40,128]{3,2,1,0:T(8,128)S(1)} %get-tuple-element, ...), custom_call_target="tpu_custom_call" | custom-call | tf_op jit(solution)/shard_map/pallas_call | solution.py:305
  7.2 0.0 collective-permute-done.1
  7.2 0.5 %shard_map.59 = (f32[26,160,128]{2,1,0:T(8,128)S(1)}, f32[26,160,128]{2,1,0:T(8,128)S(1)}, f32[26,160,128]{2,1,0:T(8,128)S(1)}, f32[26,160,128]{2,1,0:T(8,128)S(...) custom-call(f32[384,128]{1,0:T(8,128)S(1)} %bitcast.1, ...), custom_call_target="tpu_custom_call", output_to_operand_aliasing={{0}: (1, {}), {1}: (2, {}), {2}: (3, {}), {3}: (4, {}), {4}... | custom-call | tf_op jit(solution)/shard_map/pallas_call | solution.py:305
  7.7 4.8 %collective-permute-start.2 = (f32[96,128]{1,0:T(8,128)S(1)}, f32[96,128]{1,0:T(8,128)S(1)}, u32[]{:S(2)}, u32[]{:S(2)}) collective-permute-start(f32[96,128]{1,0:T(8,128)S(1)} %get-tuple-element.40), channel_id=1, source_target_pairs={{0,3},{1,0},{2,1},{3,2},{4,7},{5,4},{6,5},{7,6},{8,11},{9,8},{10,9... | collective-permute-start | bytes 147464 | tf_op jit(solution)/shard_map/ppermute | solution.py:319
  12.5 0.0 collective-permute-start.3
  12.5 1.7 %collective-permute-done.2.from_east = f32[96,128]{1,0:T(8,128)S(1)} collective-permute-done((f32[96,128]{1,0:T(8,128)S(1)}, f32[96,128]{1,0:T(8,128)S(1)}, u32[]{:S(2)}, u32[]{:S(2)}) %collective-permute-start.2) | collective-permute-done | bytes 49184 | tf_op jit(solution)/shard_map/ppermute | solution.py:319
  14.3 4.2 %collective-permute-done.3.from_west = f32[96,128]{1,0:T(8,128)S(1)} collective-permute-done((f32[96,128]{1,0:T(8,128)S(1)}, f32[96,128]{1,0:T(8,128)S(1)}, u32[]{:S(2)}, u32[]{:S(2)}) %collective-permute-start.3) | collective-permute-done | bytes 49184 | tf_op jit(solution)/shard_map/ppermute | solution.py:319
  18.4 4.4 %shard_map.60 = (f32[26,160,128]{2,1,0:T(8,128)S(1)}, f32[26,160,128]{2,1,0:T(8,128)S(1)}, f32[26,160,128]{2,1,0:T(8,128)S(1)}, f32[26,160,128]{2,1,0:T(8,128)S(...) custom-call(f32[96,128]{1,0:T(8,128)S(1)} %collective-permute-done.2, ...), custom_call_target="tpu_custom_call", output_to_operand_aliasing={{0}: (4, {}), {1}: (5, {}), {2}: (6, {}), {3}: (7, {}), {4}... | custom-call | tf_op jit(solution)/shard_map/pallas_call | solution.py:305
  22.8 4.7 %collective-permute-start.4 = (f32[4,8,32,128]{3,2,1,0:T(8,128)S(1)}, f32[4,8,32,128]{3,2,1,0:T(8,128)S(1)}, u32[]{:S(2)}, u32[]{:S(2)}) collective-permute-start(f32[4,8,32,128]{3,2,1,0:T(8,128)S(1)} %get-tuple-element.48.mine), channel_id=1, source_target_pairs={{0,16},{16,0},{1,17},{17,1},{2,18},{18,2},{3,19},{19,3},{4,20},{20... | collective-permute-start | bytes 1572872 | tf_op jit(solution)/shard_map/ppermute | solution.py:316
  27.5 1.5 %collective-permute-done.4.theirs = f32[4,8,32,128]{3,2,1,0:T(8,128)S(1)} collective-permute-done((f32[4,8,32,128]{3,2,1,0:T(8,128)S(1)}, f32[4,8,32,128]{3,2,1,0:T(8,128)S(1)}, u32[]{:S(2)}, u32[]{:S(2)}) %collective-permute-start.4) | collective-permute-done | bytes 524320 | tf_op jit(solution)/shard_map/ppermute | solution.py:316
  29.0 1.1 %shard_map.61 = f32[4,64,1024]{2,1,0:T(8,128)} custom-call(f32[4,8,32,128]{3,2,1,0:T(8,128)S(1)} %get-tuple-element.48.mine, f32[4,8,32,128]{3,2,1,0:T(8,128)S(1)} %collective-permute-done.4.theirs), custom_call_target="tpu_custom_call" | custom-call | tf_op jit(solution)/shard_map/pallas_call | solution.py:305
Async XLA Ops:
  1.3 2.4 %collective-permute-start = (f32[4,8,40,128]{3,2,1,0:T(8,128)S(1)}, f32[4,8,40,128]{3,2,1,0:T(8,128)S(1)}, u32[]{:S(2)}, u32[]{:S(2)}) collective-permute-start(f32[4,8,40,128]{3,2,1,0:T(8,128)S(1)} %shard_map.56), channel_id=1, source_target_pairs={{0,16},{16,0},{1,17},{17,1},{2,18},{18,2},{3,19},{19,3},{4,20},{20... | collective-permute-start | bytes 1966088 | tf_op jit(solution)/shard_map/ppermute | solution.py:316
  3.8 3.4 %collective-permute-start.1 = (f32[6,8,8,128]{3,2,1,0:T(8,128)S(1)}, f32[6,8,8,128]{3,2,1,0:T(8,128)S(1)}, u32[]{:S(2)}, u32[]{:S(2)}) collective-permute-start(f32[6,8,8,128]{3,2,1,0:T(8,128)S(1)} %shard_map.57), channel_id=1, source_target_pairs={{16,4},{4,16},{17,5},{5,17},{18,6},{6,18},{19,7},{7,19},{20,24},{2... | collective-permute-start | bytes 589832 | tf_op jit(solution)/shard_map/ppermute | solution.py:333
  7.7 6.6 %collective-permute-start.2 = (f32[96,128]{1,0:T(8,128)S(1)}, f32[96,128]{1,0:T(8,128)S(1)}, u32[]{:S(2)}, u32[]{:S(2)}) collective-permute-start(f32[96,128]{1,0:T(8,128)S(1)} %get-tuple-element.40), channel_id=1, source_target_pairs={{0,3},{1,0},{2,1},{3,2},{4,7},{5,4},{6,5},{7,6},{8,11},{9,8},{10,9... | collective-permute-start | bytes 147464 | tf_op jit(solution)/shard_map/ppermute | solution.py:319
  12.5 5.9 %collective-permute-start.3 = (f32[96,128]{1,0:T(8,128)S(1)}, f32[96,128]{1,0:T(8,128)S(1)}, u32[]{:S(2)}, u32[]{:S(2)}) collective-permute-start(f32[96,128]{1,0:T(8,128)S(1)} %get-tuple-element.41), channel_id=1, source_target_pairs={{0,1},{1,2},{2,3},{3,0},{4,5},{5,6},{6,7},{7,4},{8,9},{9,10},{10,1... | collective-permute-start | bytes 147464 | tf_op jit(solution)/shard_map/ppermute | solution.py:319
  22.8 6.2 %collective-permute-start.4 = (f32[4,8,32,128]{3,2,1,0:T(8,128)S(1)}, f32[4,8,32,128]{3,2,1,0:T(8,128)S(1)}, u32[]{:S(2)}, u32[]{:S(2)}) collective-permute-start(f32[4,8,32,128]{3,2,1,0:T(8,128)S(1)} %get-tuple-element.48.mine), channel_id=1, source_target_pairs={{0,16},{16,0},{1,17},{17,1},{2,18},{18,2},{3,19},{19,3},{4,20},{20... | collective-permute-start | bytes 1572872 | tf_op jit(solution)/shard_map/ppermute | solution.py:316

commit v2 on v0

v2 whole, which is shorter than its diff:
```python
import functools
import jax
import jax.numpy as jnp
from jax import lax
from jax.experimental import pallas as pl
from jax.experimental.pallas import tpu as pltpu
from jax.sharding import PartitionSpec as P

STEPS = 4
TILE = 8
LANES = 128
AXES = ("mem", "gy", "gx")
F32 = jnp.float32
VMEM = pl.BlockSpec(memory_space=pltpu.VMEM)
HBM = pl.BlockSpec(memory_space=pltpu.HBM)

BODY = slice(TILE, TILE + LANES)
DEPTH = LANES + 2 * TILE
GROUP = 32


def half_of(gy_size):
    core = lax.rem(lax.axis_index("mem"), 2)
    later = (lax.axis_index("gy") >= gy_size // 2).astype(jnp.int32)
    return lax.rem(core + later, 2)


def kept(*shape):
    return pltpu.VMEM(shape, F32)


def pinned(x):
    return pltpu.with_memory_space_constraint(x, pltpu.VMEM)


def in_hbm(x):
    return pltpu.with_memory_space_constraint(x, pltpu.HBM)


def tile(c):
    return slice(c * LANES, (c + 1) * LANES)


def lane_ids(rows):
    return lax.broadcasted_iota(jnp.int32, (rows, LANES), 1)


def row_ids(rows, width):
    return lax.broadcasted_iota(jnp.int32, (rows, width), 0)


def aligned(start):
    return pl.multiple_of(start, TILE)


def run(copies):
    for copy in copies:
        copy.start()
    for copy in copies:
        copy.wait()


def edge_kernel(gy_size, members, increment, zonal, merid, mask, sent, own, forcing, coef, mask_buf, sems):
    rows = increment.shape[1]
    half = half_of(gy_size)
    outer = pl.ds(aligned(half * (rows - TILE)), TILE)
    other = pl.ds(aligned((1 - half) * (rows - TILE)), TILE)
    run([
        pltpu.make_async_copy(members.at[0, :, other, :], sent, sems.at[0]),
        pltpu.make_async_copy(members.at[0, :, outer, :], own, sems.at[1]),
        pltpu.make_async_copy(increment.at[:, outer, :], forcing, sems.at[2]),
        pltpu.make_async_copy(zonal.at[outer, :], coef.at[0], sems.at[3]),
        pltpu.make_async_copy(merid.at[outer, :], coef.at[1], sems.at[4]),
        pltpu.make_async_copy(mask.at[outer, :], mask_buf, sems.at[5]),
    ])
    wet = mask_buf[...].astype(F32)
    coef[0] = coef[0] * wet
    coef[1] = coef[1] * wet
    coef[2] = wet
    forcing[...] = forcing[...] * wet[None]


def pack_rows_kernel(gy_size, own, other, forcing, coef, strip):
    levels, _, width = own.shape
    half = half_of(gy_size)
    j = lax.axis_index("gy")
    same_core = jnp.where(half == 0, j == gy_size // 2, j == gy_size // 2 - 1)
    low = row_ids(TILE, width) < TILE // 2

    def put(place, first, second):
        first = jnp.where(half == 0, first, pltpu.roll(first, TILE // 2, 0))
        second = jnp.where(half == 0, pltpu.roll(second, TILE // 2, 0), second)
        strip[place] = jnp.where(low, first, second)

    for level in range(levels):
        mine = own[level] * forcing[level]
        theirs = other[level] * forcing[level]
        put(level, jnp.where(same_core, mine, theirs), jnp.where(same_core, theirs, mine))
    put(levels, coef[0], coef[1])
    put(levels + 1, coef[2], coef[2])


def received(half, strip, place, cols):
    value = strip[place // 2, :, cols]
    natural = jnp.equal(half, 1 - place % 2)
    return jnp.where(natural, value, pltpu.roll(value, TILE // 2, 0))


def edge_columns(first, last):
    rows = first[0].shape[0]
    lane = lane_ids(rows)
    total = jnp.zeros((rows, LANES), F32)
    for level, (a, b) in enumerate(zip(first, last)):
        base = GROUP * level
        total = jnp.where((lane >= base + 8) & (lane < base + 16), pltpu.roll(a, base + 8, 1), total)
        total = jnp.where((lane >= base + 16) & (lane < base + 24), pltpu.roll(b, (base + 16 - 120) % LANES, 1), total)
    return total


def spread(value):
    value = value + pltpu.roll(value, GROUP, 1)
    return value + pltpu.roll(value, 2 * GROUP, 1)


def edge_coefficient(first, last):
    rows = first.shape[0]
    lane = lane_ids(rows)
    total = jnp.where((lane >= 8) & (lane < 16), pltpu.roll(first, 8, 1), 0.0)
    return spread(jnp.where((lane >= 16) & (lane < 24), pltpu.roll(last, 24, 1), total))


def outgoing(fields, coefs, west):
    rows = coefs[0].shape[0]
    lane = lane_ids(rows)
    start, step, source = (24, -4, 0) if west else (4, 4, 124)
    total = jnp.zeros((rows, LANES), F32)
    for k, value in enumerate(coefs):
        at = start + step * (k + 2)
        total = jnp.where((lane >= at) & (lane < at + 4), pltpu.roll(value, (at - source) % LANES, 1), total)
    total = spread(total)
    for k, member in enumerate(fields):
        for level, value in enumerate(member):
            at = GROUP * level + start + step * k
            total = jnp.where((lane >= at) & (lane < at + 4), pltpu.roll(value, (at - source) % LANES, 1), total)
    return total


def turn(ref, start, stride):
    return jnp.concatenate([ref[pl.ds(s, TILE, stride=stride), :] for s in start], axis=0).T


def refresh(ref, first, count):
    flat = ref.reshape(ref.shape[0] * DEPTH, LANES)

    def rows(j):
        return pl.ds(first * DEPTH + TILE + j, count, stride=DEPTH)

    flat[rows(-1), :] = pltpu.roll(flat[rows(LANES - 1), :], 1, 1)
    flat[rows(LANES), :] = pltpu.roll(flat[rows(0), :], LANES - 1, 1)


def sweep(source, target, east, north, first, last):
    refresh(source, first, last - first + 1)
    for start in range(TILE, TILE + LANES, TILE):
        at, ahead, behind = (slice(start + d, start + d + TILE) for d in (0, 1, -1))
        here = source[first, at, :]
        south = north[first - 1, at, :] * (here - source[first - 1, at, :])
        for p in range(first, last + 1):
            above = source[p + 1, at, :]
            flux = north[p, at, :] * (above - here)
            go_east = east[p, at, :] * (source[p, ahead, :] - here)
            go_west = east[p, behind, :] * (here - source[p, behind, :])
            target[p, at, :] = here + go_east - go_west + flux - south
            here, south = above, flux


def faces(zm, mm, wet, cols, width, rows):
    after = slice(cols.start + LANES, cols.stop + LANES) if cols.stop < width else cols
    lane = lane_ids(rows)
    here = pltpu.roll(wet[:rows, cols], LANES - 1, 1)
    beyond = pltpu.roll(wet[:rows, after], LANES - 1, 1)
    east = zm[:, cols] * jnp.where(lane == LANES - 1, beyond, here)
    north = mm[:, cols] * wet[1 : rows + 1, cols]
    return east, north


def interior_kernel(
    gy_size, members, others, increment, zonal, merid, mask,
    out, pack_own, pack_other, pack_coef, weight_own, weight_other, west_out, east_out,
    zm, mm, wet, field, face, u, u_next, east, north, result,
):
    _, levels, rows, width = members.shape
    tiles = width // LANES
    mid = rows // 2
    tall = mid + TILE
    offset = tall - 3 * TILE
    planes = tall - offset
    half = half_of(gy_size)
    part = pl.ds(aligned(half * (mid - TILE)), tall)
    wet[:tall, :] = mask[part, :].astype(F32)
    wet[tall:, :] = jnp.zeros((TILE, width), F32)
    zm[...] = zonal[part, :] * wet[:tall, :]
    mm[...] = merid[part, :] * wet[:tall, :]
    sources = (members, others)
    for c in range(tiles):
        cols = tile(c)
        face[pl.ds(c * tall, tall), :], face[pl.ds((tiles + c) * tall, tall), :] = faces(zm, mm, wet, cols, width, tall)
        for level in range(levels):
            force = increment[level, part, cols] * wet[:tall, cols]
            for k, member in enumerate(sources):
                field[pl.ds(((2 * level + k) * tiles + c) * tall, tall), :] = member[0, level, part, cols] * force

    def at(f, c):
        return field[pl.ds((f * tiles + c) * tall, tall), :]

    ends = (tile(0), tile(tiles - 1))
    lead = pl.ds(aligned((1 - half) * TILE), tall)
    for k, pack in enumerate((pack_own, pack_other)):
        pack[lead, :] = edge_columns(*([at(2 * level + k, c) for level in range(levels)] for c in (0, tiles - 1)))
    for k, ref in enumerate((zm, mm, wet)):
        pack_coef[k, lead, :] = edge_coefficient(*(ref[:tall, cols] for cols in ends))
    keep = pl.ds(aligned(half * mid), mid)
    for member, weight in zip(sources, (weight_own, weight_other)):
        weight[...] = edge_columns(*([member[0, level, keep, cols] for level in range(levels)] for cols in ends))
    for out_strip, c, west in ((west_out, 0, True), (east_out, tiles - 1, False)):
        out_strip[lead, :] = outgoing(
            [[at(2 * level + k, c) for level in range(levels)] for k in range(2)],
            [ref[:tall, tile(c)] for ref in (zm, mm, wet)],
            west,
        )

    fields = range(2 * levels)
    for q in range(planes):
        u[q, BODY, :] = turn(field, [f * tiles * tall + ch * offset + q for f in fields for ch in range(2)], tall)
        for k, ref in enumerate((east, north)):
            ref[q, BODY, :] = turn(face, [k * tiles * tall + ch * offset + q for f in fields for ch in range(2)], tall)
    refresh(east, 0, planes)
    source, target = u, u_next
    for step in range(STEPS):
        sweep(source, target, east, north, step + 1, planes - 2 - step)
        source, target = target, source
    for q in range(STEPS, planes - STEPS):
        flat = source[q, BODY, :].T
        for f in fields:
            for ch in range(2):
                group = (2 * f + ch) * tiles
                result[pl.ds(f * tiles * tall + ch * offset + q, tiles, stride=tall), :] = flat[group : group + tiles]
    for level in range(levels):
        for c in range(tiles):
            a, b = (
                result[pl.ds(aligned(((2 * level + k) * tiles + c) * tall + half * TILE), mid), :] for k in range(2)
            )
            out[level, :, tile(c)] = members[0, level, keep, tile(c)] * a + others[0, level, keep, tile(c)] * b


def halo_columns_kernel(gy_size, strip, west_in, east_in, west_out, east_out):
    levels = strip.shape[0] - 2
    width = strip.shape[2]
    half = half_of(gy_size)
    full = west_out.shape[0]
    halo = pl.ds(aligned(half * (full - TILE)), TILE)
    main = pl.ds(aligned((1 - half) * TILE), full - TILE)
    for source, out, cols, west in (
        (west_in, west_out, slice(0, LANES), True),
        (east_in, east_out, slice(width - LANES, width), False),
    ):
        out[main, :] = source[main, :]
        out[halo, :] = outgoing(
            [[received(half, strip, 2 * level + k, cols) for level in range(levels)] for k in range(2)],
            [received(half, strip, 2 * levels + k, cols) for k in range(3)],
            west,
        )


def outer_rows_kernel(
    gy_size, strip, own, other, forcing, coef, pack_own, pack_other, pack_coef,
    sums, full_own, full_other, full_coef,
    zm, mm, wet, field, face, u, u_next, east, north, result,
):
    levels, _, width = own.shape
    tiles = width // LANES
    half = half_of(gy_size)
    edge = pl.ds(aligned((1 - half) * TILE), TILE)
    halo = pl.ds(aligned(half * TILE), TILE)
    block = 2 * TILE
    every = slice(0, width)
    for k, ref in enumerate((zm, mm, wet)):
        ref[edge, :] = coef[k]
        ref[halo, :] = received(half, strip, 2 * levels + k, every)
    wet[block:, :] = jnp.zeros((TILE, width), F32)
    for c in range(tiles):
        cols = tile(c)
        face[pl.ds(c * block, block), :], face[pl.ds((tiles + c) * block, block), :] = faces(zm, mm, wet, cols, width, block)
        for level in range(levels):
            for k, member in enumerate((own, other)):
                base = ((2 * level + k) * tiles + c) * block
                field[pl.ds(aligned(base + (1 - half) * TILE), TILE), :] = member[level, :, cols] * forcing[level, :, cols]
                field[pl.ds(aligned(base + half * TILE), TILE), :] = received(half, strip, 2 * level + k, cols)

    fields = range(2 * levels)
    planes = 10
    lead = (1 - half) * 4
    for q in range(planes):
        u[q, BODY, :] = turn(field, [f * tiles * block + 2 * ch + q + lead for f in fields for ch in range(2)], block)
        for k, ref in enumerate((east, north)):
            ref[q, BODY, :] = turn(face, [k * tiles * block + 2 * ch + q + lead for f in fields for ch in range(2)], block)
    refresh(east, 0, planes)
    source, target = u, u_next
    for step in range(STEPS):
        sweep(source, target, east, north, step + 1, planes - 2 - step)
        source, target = target, source
    for p in range(2):
        flat = source[STEPS + p, BODY, :].T
        for f in fields:
            for ch in range(2):
                group = (2 * f + ch) * tiles
                result[pl.ds(f * tiles * TILE + 4 * half + 2 * ch + p, tiles, stride=TILE), :] = flat[group : group + tiles]
    natural = row_ids(TILE, LANES) // 4 == half
    for c in range(tiles):
        cols = tile(c)
        terms = []
        for level in range(levels):
            a, b = (result[pl.ds(((2 * level + k) * tiles + c) * TILE, TILE), :] for k in range(2))
            terms.append(own[level, :, cols] * a + other[level, :, cols] * b)
        for pair in range(levels // 2):
            sums[pl.ds((c * levels // 2 + pair) * TILE, TILE), :] = jnp.where(
                natural, terms[2 * pair], pltpu.roll(terms[2 * pair + 1], 4, 0)
            )

    full = full_own.shape[0]
    main = pl.ds(aligned((1 - half) * TILE), full - TILE)
    beyond = pl.ds(aligned(half * (full - TILE)), TILE)
    ends = (slice(0, LANES), slice(width - LANES, width))
    for k, (source, out) in enumerate(((pack_own, full_own), (pack_other, full_other))):
        out[main, :] = source[main, :]
        out[beyond, :] = edge_columns(
            *([received(half, strip, 2 * level + k, cols) for level in range(levels)] for cols in ends)
        )
    for k in range(3):
        full_coef[k, main, :] = pack_coef[k, main, :]
        full_coef[k, beyond, :] = edge_coefficient(*(received(half, strip, 2 * levels + k, cols) for cols in ends))


def end_columns_kernel(
    gy_size, from_west, from_east, own, other, coef, weight_own, weight_other, sums, out,
    a, b, a_next, b_next, east, north, wet,
):
    full = own.shape[0]
    body = pl.ds(TILE, full)
    place = lane_ids(full) % GROUP
    on_west = (place >= 4) & (place < 8)
    on_east = (place >= 24) & (place < 28)
    west, east_strip = from_west[...], from_east[...]

    def with_ends(value, k):
        value = jnp.where(on_west, pltpu.roll(west, (-4 * k) % LANES, 1), value)
        return jnp.where(on_east, pltpu.roll(east_strip, 4 * k, 1), value)

    blank = jnp.zeros((TILE, LANES), F32)
    for ref in (a, b, a_next, b_next, east, north, wet):
        ref[:TILE, :] = blank
        ref[full + TILE :, :] = blank
    a[body, :] = with_ends(own[...], 0)
    b[body, :] = with_ends(other[...], 1)
    wet[body, :] = with_ends(coef[2], 4)
    east[body, :] = with_ends(coef[0], 2) * pltpu.roll(wet[body, :], LANES - 1, 1)
    north[body, :] = with_ends(coef[1], 3) * wet[pl.ds(TILE + 1, full), :]
    now, later = (a, b), (a_next, b_next)
    for step in range(STEPS):
        for t in range(TILE, full + TILE, TILE):
            at, above, below = (pl.ds(t + d, TILE) for d in (0, 1, -1))
            e, n, s = east[at, :], north[at, :], north[below, :]
            for source, target in zip(now, later):
                here = source[at, :]
                flux = e * (pltpu.roll(here, LANES - 1, 1) - here)
                go_north = n * (source[above, :] - here)
                go_south = s * (here - source[below, :])
                target[at, :] = here + flux - pltpu.roll(flux, 1, 1) + go_north - go_south
        now, later = later, now
    mid = weight_own.shape[0]
    rows = pl.ds(2 * TILE, mid)
    out[:mid, :] = weight_own[...] * now[0][rows, :] + weight_other[...] * now[1][rows, :]
    out[mid:, :] = sums[...]


def join_kernel(gy_size, mine_in, theirs_in, mine_edge, theirs_edge, mine, theirs, out, sems):
    half = half_of(gy_size)
    levels, mid, width = mine.shape
    tiles = width // LANES
    lane = lane_ids(mid)
    copies = []
    for k, (ref, edges, where) in enumerate(((mine, mine_edge, half), (theirs, theirs_edge, 1 - half))):
        outer = pl.ds(aligned(where * (mid - TILE)), TILE)
        natural = row_ids(TILE, LANES) // 4 == where
        for level in range(levels):
            for c in range(tiles):
                value = edges[pl.ds(mid + (c * levels // 2 + level // 2) * TILE, TILE), :]
                if level % 2:
                    value = pltpu.roll(value, 4, 0)
                ref[level, outer, tile(c)] = jnp.where(natural, value, ref[level, outer, tile(c)])
            first, last = tile(0), tile(tiles - 1)
            base = GROUP * level
            packed = edges[:mid, :]
            ref[level, :, first] = jnp.where(lane < 4, pltpu.roll(packed, (-base - 8) % LANES, 1), ref[level, :, first])
            ref[level, :, last] = jnp.where(
                lane >= LANES - 4, pltpu.roll(packed, (LANES - 4 - base - 20) % LANES, 1), ref[level, :, last]
            )
            copies.append(
                pltpu.make_async_copy(
                    ref.at[level], out.at[level, pl.ds(aligned(where * mid), mid), :], sems.at[k, level]
                )
            )
            copies[-1].start()
    for copy in copies:
        copy.wait()


def shards(sizes, increment, members, zonal_diff, merid_diff, sea_mask):
    n_mem, n_gy, n_gx = sizes
    levels, rows, width = increment.shape
    tiles = width // LANES
    mid = rows // 2
    tall = mid + TILE
    full = tall + TILE
    planes = 3 * TILE
    assert tiles == TILE and 4 * levels * tiles == LANES and tall == 5 * TILE and n_mem % 2 == 0

    def call(kernel, ins, specs, outs, scratch=(), out_specs=None, aliases={}):
        return pl.pallas_call(
            functools.partial(kernel, n_gy),
            out_shape=outs,
            in_specs=specs,
            out_specs=out_specs if out_specs is not None else jax.tree.map(lambda _: VMEM, outs),
            scratch_shapes=scratch,
            input_output_aliases=aliases,
            compiler_params=pltpu.CompilerParams(vmem_limit_bytes=40 * 1024 * 1024),
        )(*ins)

    def held(kernel, ins, outs, scratch=(), **kw):
        got = call(kernel, [pinned(x) for x in ins], [VMEM] * len(ins), outs, scratch, **kw)
        return got

    def swap(x):
        return lax.ppermute(x, "mem", [(i, i ^ 1) for i in range(n_mem)])

    def along(x, shift):
        return lax.ppermute(x, "gx", [(i, (i + shift) % n_gx) for i in range(n_gx)])

    def across(x):
        def place(chip, core, j, i):
            return ((2 * chip + core) * n_gy + j) * n_gx + i

        first = [0 if j < n_gy // 2 else 1 for j in range(n_gy)]
        pairs = []
        for chip in range(n_mem // 2):
            for j in range(n_gy - 1):
                for i in range(n_gx):
                    a = place(chip, 1 - first[j], j, i)
                    b = place(chip, first[j + 1], j + 1, i)
                    pairs += [(a, b), (b, a)]
        return lax.ppermute(x, AXES, pairs)

    def scratch(*shape):
        return pltpu.VMEM(shape, F32)

    arrays = [members, increment, zonal_diff, merid_diff, sea_mask]
    sent, own, forcing, coef = call(
        edge_kernel,
        [in_hbm(x) for x in arrays],
        [HBM] * 5,
        [kept(levels, TILE, width)] * 3 + [kept(3, TILE, width)],
        [pltpu.VMEM((TILE, width), jnp.int32), pltpu.SemaphoreType.DMA((6,))],
    )
    other = swap(sent)
    members_later, other = lax.optimization_barrier((members, other))
    others = swap(members_later)
    strip = held(pack_rows_kernel, [own, other, forcing, coef], kept(levels + 2, TILE, width))
    zonal_later, strip = lax.optimization_barrier((zonal_diff, strip))
    strip = across(strip)

    end = kept(full, LANES)
    inside, pack_own, pack_other, pack_coef, weight_own, weight_other, west, east = held(
        interior_kernel,
        [members, others, increment, zonal_later, merid_diff, sea_mask],
        [kept(levels, mid, width), end, end, kept(3, full, LANES), kept(mid, LANES), kept(mid, LANES), end, end],
        [
            scratch(tall, width),
            scratch(tall, width),
            scratch(full, width),
            scratch(2 * levels * tiles * tall, LANES),
            scratch(2 * tiles * tall, LANES),
            scratch(planes, DEPTH, LANES),
            scratch(planes, DEPTH, LANES),
            scratch(planes, DEPTH, LANES),
            scratch(planes, DEPTH, LANES),
            scratch(2 * levels * tiles * tall, LANES),
        ],
    )
    west, east = held(halo_columns_kernel, [strip, west, east], [end, end])
    inside, west, east = lax.optimization_barrier((inside, west, east))
    from_west = along(east, 1)
    from_east = along(west, -1)
    sums, full_own, full_other, full_coef = held(
        outer_rows_kernel,
        [strip, own, other, forcing, coef, pack_own, pack_other, pack_coef],
        [kept(levels // 2 * tiles * TILE, LANES), end, end, kept(3, full, LANES)],
        [
            scratch(2 * TILE, width),
            scratch(2 * TILE, width),
            scratch(3 * TILE, width),
            scratch(2 * levels * tiles * 2 * TILE, LANES),
            scratch(2 * tiles * 2 * TILE, LANES),
            scratch(10, DEPTH, LANES),
            scratch(10, DEPTH, LANES),
            scratch(10, DEPTH, LANES),
            scratch(10, DEPTH, LANES),
            scratch(2 * levels * tiles * TILE, LANES),
        ],
    )
    edges = held(
        end_columns_kernel,
        [from_west, from_east, full_own, full_other, full_coef, weight_own, weight_other, sums],
        kept(mid + levels // 2 * tiles * TILE, LANES),
        [scratch(full + 2 * TILE, LANES)] * 7,
    )
    if n_mem > 2:
        groups = [list(range(k, n_mem, 2)) for k in range(2)]
        inside, edges = (lax.psum(x, "mem", axis_index_groups=groups) for x in (inside, edges))
    inside_theirs, edges_theirs = swap(inside), swap(edges)
    return held(
        join_kernel,
        [inside, inside_theirs, edges, edges_theirs],
        [kept(levels, mid, width)] * 2 + [jax.ShapeDtypeStruct(increment.shape, F32)],
        [pltpu.SemaphoreType.DMA((2, levels))],
        out_specs=[VMEM, VMEM, HBM],
        aliases={0: 0, 1: 1},
    )[2]


def solution(mesh):
    return jax.shard_map(
        functools.partial(shards, tuple(mesh.shape[axis] for axis in AXES)),
        mesh=mesh,
        in_specs=(
            P(None, "gy", "gx"),
            P("mem", None, "gy", "gx"),
            P("gy", "gx"),
            P("gy", "gx"),
            P("gy", "gx"),
        ),
        out_specs=P(None, "gy", "gx"),
        check_vma=False,
    )
```

time: 123 us -> 22.9 us (0.19)
  waiting for transfers between devices: 48.5 us -> 4.28 us
  starting transfers between devices: 46.8 us -> 9.51 us
  between operations: 13.7 us -> 0.08 us
  Pallas kernels: 0 us -> 8.87 us
  other arithmetic: 8.6 us -> 0 us
  local copies, waits for them, and re-layouts: 5.02 us -> 0.02 us
    ppermute x20 -> x7, starting transfers between devices: 46.8 us -> 9.51 us  [the longest x2 4.65 us: along(): return lax.ppermute(x, 'gx', [(i, (i + shift) % n_gx) for i in range(n_gx)])]
    ppermute x20 -> x7, waiting for transfers between devices: 27.5 us -> 4.28 us  [the longest x4 3.67 us: swap(): return lax.ppermute(x, 'mem', [(i, i ^ 1) for i in range(n_mem)])]
    psum x1 -> x0, waiting for transfers between devices: 21 us -> none  [shards(): return lax.psum(term, 'mem')]
    pallas_call x0 -> x7, Pallas kernels: none -> 8.87 us  [call(): pl.pallas_call(functools.partial(kernel, n_gy), out_shape=outs, in_specs=...]
    mul x4 -> x0, other arithmetic: 3.46 us -> none  [the longest x1 1.82 us: shards(): term = member * field]
    sub x3 -> x0, other arithmetic: 3.43 us -> none  [sweep(): return centre + go_east - go_west + go_north - go_south]
    unnamed x11 -> x10, local copies, waits for them, and re-layouts: 2.97 us -> 0.02 us
    concatenate x1 -> x0, local copies, waits for them, and re-layouts: 1.43 us -> none  [extended(): shard = jnp.concatenate([before, shard, after], axis=dim)]
  transfers between devices with their start and end apart: 21 -> 7, of which waited for: 11 -> 5; matrix products, arithmetic and copies ran while one was open for 3% -> 0% of each run, Pallas kernels for 0% -> 28%
where the time goes in v2:
time: 22.9 us; the launch traced here: 22.8 us
  starting transfers between devices  9.51 us (42%)
  Pallas kernels  8.87 us (39%)
  waiting for transfers between devices  4.28 us (19%)
    pallas_call x7, Pallas kernels, call(): pl.pallas_call(functools.partial(kernel, n_gy), out_shape=outs, in_specs=...  8.87 us
    ppermute x2, starting transfers between devices, along(): return lax.ppermute(x, 'gx', [(i, (i + shift) % n_gx) for i in range(n_gx)])  4.65 us
    ppermute x4, starting transfers between devices, swap(): return lax.ppermute(x, 'mem', [(i, i ^ 1) for i in range(n_mem)])  4.05 us
    ppermute x4, waiting for transfers between devices, swap(): return lax.ppermute(x, 'mem', [(i, i ^ 1) for i in range(n_mem)])  3.67 us
    ppermute x1, starting transfers between devices, across(): return lax.ppermute(x, AXES, pairs)  0.8 us
    ppermute x2, waiting for transfers between devices, along(): return lax.ppermute(x, 'gx', [(i, (i + shift) % n_gx) for i in range(n_gx)])  0.61 us
  transfers between devices with their start and end apart: 7, of which 5 were waited for; matrix products, arithmetic and copies ran while one was open for 0% of the time, Pallas kernels for 28%

profile of v2, /device:TPU:0, one launch (start us, length us, event | category | flops | bytes accessed | tf_op | source)
XLA Modules:
  0.0 22.8 jit_solution(4775684009952756671)
XLA Ops:
  0.0 0.0 copy-start
  0.0 0.0 copy-start.1
  0.0 0.0 copy-start.4
  0.0 1.3 %shard_map.55 = (f32[4,8,1024]{2,1,0:T(8,128)S(1)}, f32[4,8,1024]{2,1,0:T(8,128)S(1)}, f32[4,8,1024]{2,1,0:T(8,128)S(1)}, f32[3,8,1024]{2,1,0:T(8,128)S(1)}) custom-call(f32[1,4,64,1024]{3,2,1,0:T(8,128)} %members.3, f32[4,64,1024]{2,1,0:T(8,128)} %increment.3, f32[64,1024]{1,0:T(8,128)} %zonal.2, f32[64,1024]{1,0:T(8,128)} %merid.3, s32[64,1024]{1,0:T(8,128)} %mask.3), custom_call_target="tpu_custom_call" | custom-call | tf_op jit(solution)/shard_map/pallas_call | solution.py:429
  1.3 0.5 %collective-permute-start = (f32[4,8,1024]{2,1,0:T(8,128)S(1)}, f32[4,8,1024]{2,1,0:T(8,128)S(1)}, u32[]{:S(2)}, u32[]{:S(2)}) collective-permute-start(f32[4,8,1024]{2,1,0:T(8,128)S(1)} %get-tuple-element.31), channel_id=1, source_target_pairs={{0,16},{16,0},{1,17},{17,1},{2,18},{18,2},{3,19},{19,3},{4,20},{20... | collective-permute-start | bytes 393224 | tf_op jit(solution)/shard_map/ppermute | solution.py:444
  1.8 1.0 %collective-permute-done.other = f32[4,8,1024]{2,1,0:T(8,128)S(1)} collective-permute-done((f32[4,8,1024]{2,1,0:T(8,128)S(1)}, f32[4,8,1024]{2,1,0:T(8,128)S(1)}, u32[]{:S(2)}, u32[]{:S(2)}) %collective-permute-start) | collective-permute-done | bytes 131104 | tf_op jit(solution)/shard_map/ppermute | solution.py:444
  2.8 0.0 copy-done
  2.8 0.4 %collective-permute-start.1 = (f32[1,4,64,1024]{3,2,1,0:T(8,128)S(1)}, f32[1,4,64,1024]{3,2,1,0:T(8,128)S(1)}, u32[]{:S(2)}, u32[]{:S(2)}) collective-permute-start(f32[1,4,64,1024]{3,2,1,0:T(8,128)S(1)} %copy-done), channel_id=1, source_target_pairs={{0,16},{16,0},{1,17},{17,1},{2,18},{18,2},{3,19},{19,3},{4,20},{20... | collective-permute-start | bytes 3145736 | tf_op jit(solution)/shard_map/ppermute | solution.py:444
  3.2 0.0 copy-start.2
  3.2 0.0 copy-start.3
  3.2 0.1 shard_map.56
  3.2 0.8 %collective-permute-start.2 = (f32[6,8,1024]{2,1,0:T(8,128)S(1)}, f32[6,8,1024]{2,1,0:T(8,128)S(1)}, u32[]{:S(2)}, u32[]{:S(2)}) collective-permute-start(f32[6,8,1024]{2,1,0:T(8,128)S(1)} %shard_map.56), channel_id=1, source_target_pairs={{16,4},{4,16},{17,5},{5,17},{18,6},{6,18},{19,7},{7,19},{20,24},{2... | collective-permute-start | bytes 589832 | tf_op jit(solution)/shard_map/ppermute | solution.py:461
  4.0 1.4 %collective-permute-done.1.others = f32[1,4,64,1024]{3,2,1,0:T(8,128)S(1)} collective-permute-done((f32[1,4,64,1024]{3,2,1,0:T(8,128)S(1)}, f32[1,4,64,1024]{3,2,1,0:T(8,128)S(1)}, u32[]{:S(2)}, u32[]{:S(2)}) %collective-permute-start.1) | collective-permute-done | bytes 1048608 | tf_op jit(solution)/shard_map/ppermute | solution.py:444
  5.5 0.0 copy-done.1
  5.5 0.0 copy-done.4
  5.5 0.0 copy-done.2
  5.5 0.0 copy-done.3
  5.5 4.1 %shard_map.57 = (f32[4,32,1024]{2,1,0:T(8,128)S(1)}, f32[48,128]{1,0:T(8,128)S(1)}, f32[48,128]{1,0:T(8,128)S(1)}, f32[3,48,128]{2,1,0:T(8,128)S(1)}, f32[32,128...) custom-call(f32[1,4,64,1024]{3,2,1,0:T(8,128)S(1)} %copy-done, ...), custom_call_target="tpu_custom_call" | custom-call | tf_op jit(solution)/shard_map/pallas_call | solution.py:429
  9.6 0.0 collective-permute-done.2.strip
  9.6 0.2 %shard_map.58 = (f32[48,128]{1,0:T(8,128)S(1)}, f32[48,128]{1,0:T(8,128)S(1)}) custom-call(f32[6,8,1024]{2,1,0:T(8,128)S(1)} %collective-permute-done.2.strip, f32[48,128]{1,0:T(8,128)S(1)} %get-tuple-element.40.west_in, f32[48,128]{1,0:T(8,128)S(1)} %get-tuple-element.41.east_in), custom_call_target="tpu_custom_call" | custom-call | tf_op jit(solution)/shard_map/pallas_call | solution.py:429
  9.8 3.1 %collective-permute-start.3 = (f32[4,32,1024]{2,1,0:T(8,128)S(1)}, f32[4,32,1024]{2,1,0:T(8,128)S(1)}, u32[]{:S(2)}, u32[]{:S(2)}) collective-permute-start(f32[4,32,1024]{2,1,0:T(8,128)S(1)} %get-tuple-element.44.mine_in), channel_id=1, source_target_pairs={{0,16},{16,0},{1,17},{17,1},{2,18},{18,2},{3,19},{19,3},{4,20},{20... | collective-permute-start | bytes 1572872 | tf_op jit(solution)/shard_map/ppermute | solution.py:444
  12.9 2.6 %collective-permute-start.4 = (f32[48,128]{1,0:T(8,128)S(1)}, f32[48,128]{1,0:T(8,128)S(1)}, u32[]{:S(2)}, u32[]{:S(2)}) collective-permute-start(f32[48,128]{1,0:T(8,128)S(1)} %get-tuple-element.45), channel_id=1, source_target_pairs={{0,1},{1,2},{2,3},{3,0},{4,5},{5,6},{6,7},{7,4},{8,9},{9,10},{10,1... | collective-permute-start | bytes 73736 | tf_op jit(solution)/shard_map/ppermute | solution.py:447
  15.5 2.0 %collective-permute-start.5 = (f32[48,128]{1,0:T(8,128)S(1)}, f32[48,128]{1,0:T(8,128)S(1)}, u32[]{:S(2)}, u32[]{:S(2)}) collective-permute-start(f32[48,128]{1,0:T(8,128)S(1)} %get-tuple-element.46), channel_id=1, source_target_pairs={{0,3},{1,0},{2,1},{3,2},{4,7},{5,4},{6,5},{7,6},{8,11},{9,8},{10,9... | collective-permute-start | bytes 73736 | tf_op jit(solution)/shard_map/ppermute | solution.py:447
  17.6 1.4 %shard_map.59 = (f32[128,128]{1,0:T(8,128)S(1)}, f32[48,128]{1,0:T(8,128)S(1)}, f32[48,128]{1,0:T(8,128)S(1)}, f32[3,48,128]{2,1,0:T(8,128)S(1)}) custom-call(f32[6,8,1024]{2,1,0:T(8,128)S(1)} %collective-permute-done.2.strip, f32[4,8,1024]{2,1,0:T(8,128)S(1)} %get-tuple-element.33.own, f32[4,8,1024]{2,1,0:T(8,128)S(1)} %collective-permute-done.other, ...), custom_call_target="tpu_custom_call" | custom-call | tf_op jit(solution)/shard_map/pallas_call | solution.py:429
  19.0 0.5 %collective-permute-done.4.from_west = f32[48,128]{1,0:T(8,128)S(1)} collective-permute-done((f32[48,128]{1,0:T(8,128)S(1)}, f32[48,128]{1,0:T(8,128)S(1)}, u32[]{:S(2)}, u32[]{:S(2)}) %collective-permute-start.4) | collective-permute-done | bytes 24608 | tf_op jit(solution)/shard_map/ppermute | solution.py:447
  19.5 0.1 collective-permute-done.5.from_east
  19.6 0.7 %shard_map.60.mine_edge = f32[160,128]{1,0:T(8,128)S(1)} custom-call(f32[48,128]{1,0:T(8,128)S(1)} %collective-permute-done.4.from_west, f32[48,128]{1,0:T(8,128)S(1)} %collective-permute-done.5.from_east, f32[48,128]{1,0:T(8,128)S(1)} %get-tuple-element.50.own, f32[48,128]{1,0:T(8,128)S(1)} %get-tuple-element.51.other, ...), custom_call_target="tpu_custom_call" | custom-call | tf_op jit(solution)/shard_map/pallas_call | solution.py:429
  20.3 0.1 collective-permute-start.6
  20.4 1.3 %collective-permute-done.6.theirs_edge = f32[160,128]{1,0:T(8,128)S(1)} collective-permute-done((f32[160,128]{1,0:T(8,128)S(1)}, f32[160,128]{1,0:T(8,128)S(1)}, u32[]{:S(2)}, u32[]{:S(2)}) %collective-permute-start.6) | collective-permute-done | bytes 81952 | tf_op jit(solution)/shard_map/ppermute | solution.py:444
  21.6 0.0 collective-permute-done.3.theirs_in
  21.6 1.1 %shard_map.61 = (f32[4,32,1024]{2,1,0:T(8,128)S(1)}, f32[4,32,1024]{2,1,0:T(8,128)S(1)}, f32[4,64,1024]{2,1,0:T(8,128)}) custom-call(f32[4,32,1024]{2,1,0:T(8,128)S(1)} %get-tuple-element.44.mine_in, f32[4,32,1024]{2,1,0:T(8,128)S(1)} %collective-permute-done.3.theirs_in, ...), custom_call_target="tpu_custom_call", output_to_operand_aliasing={{0}: (0, {}), {1}: (1, {})} | custom-call | tf_op jit(solution)/shard_map/pallas_call | solution.py:429
Async XLA Ops:
  0.0 2.8 %copy-start = (f32[1,4,64,1024]{3,2,1,0:T(8,128)S(1)}, f32[1,4,64,1024]{3,2,1,0:T(8,128)}, u32[]{:S(2)}) copy-start(f32[1,4,64,1024]{3,2,1,0:T(8,128)} %members.3) | copy-start | bytes 3145732
  0.0 5.5 %copy-start.1 = (f32[4,64,1024]{2,1,0:T(8,128)S(1)}, f32[4,64,1024]{2,1,0:T(8,128)}, u32[]{:S(2)}) copy-start(f32[4,64,1024]{2,1,0:T(8,128)} %increment.3) | copy-start | bytes 3145732
  0.0 5.5 %copy-start.4 = (s32[64,1024]{1,0:T(8,128)S(1)}, s32[64,1024]{1,0:T(8,128)}, u32[]{:S(2)}) copy-start(s32[64,1024]{1,0:T(8,128)} %mask.3) | copy-start | bytes 786436
  1.3 1.5 %collective-permute-start = (f32[4,8,1024]{2,1,0:T(8,128)S(1)}, f32[4,8,1024]{2,1,0:T(8,128)S(1)}, u32[]{:S(2)}, u32[]{:S(2)}) collective-permute-start(f32[4,8,1024]{2,1,0:T(8,128)S(1)} %get-tuple-element.31), channel_id=1, source_target_pairs={{0,16},{16,0},{1,17},{17,1},{2,18},{18,2},{3,19},{19,3},{4,20},{20... | collective-permute-start | bytes 393224 | tf_op jit(solution)/shard_map/ppermute | solution.py:444
  2.8 2.7 %collective-permute-start.1 = (f32[1,4,64,1024]{3,2,1,0:T(8,128)S(1)}, f32[1,4,64,1024]{3,2,1,0:T(8,128)S(1)}, u32[]{:S(2)}, u32[]{:S(2)}) collective-permute-start(f32[1,4,64,1024]{3,2,1,0:T(8,128)S(1)} %copy-done), channel_id=1, source_target_pairs={{0,16},{16,0},{1,17},{17,1},{2,18},{18,2},{3,19},{19,3},{4,20},{20... | collective-permute-start | bytes 3145736 | tf_op jit(solution)/shard_map/ppermute | solution.py:444
  3.2 2.3 %copy-start.2 = (f32[64,1024]{1,0:T(8,128)S(1)}, f32[64,1024]{1,0:T(8,128)}, u32[]{:S(2)}) copy-start(f32[64,1024]{1,0:T(8,128)} %zonal.2) | copy-start | bytes 786436
  3.2 2.3 %copy-start.3 = (f32[64,1024]{1,0:T(8,128)S(1)}, f32[64,1024]{1,0:T(8,128)}, u32[]{:S(2)}) copy-start(f32[64,1024]{1,0:T(8,128)} %merid.3) | copy-start | bytes 786436
  3.2 6.4 %collective-permute-start.2 = (f32[6,8,1024]{2,1,0:T(8,128)S(1)}, f32[6,8,1024]{2,1,0:T(8,128)S(1)}, u32[]{:S(2)}, u32[]{:S(2)}) collective-permute-start(f32[6,8,1024]{2,1,0:T(8,128)S(1)} %shard_map.56), channel_id=1, source_target_pairs={{16,4},{4,16},{17,5},{5,17},{18,6},{6,18},{19,7},{7,19},{20,24},{2... | collective-permute-start | bytes 589832 | tf_op jit(solution)/shard_map/ppermute | solution.py:461
  9.8 11.8 %collective-permute-start.3 = (f32[4,32,1024]{2,1,0:T(8,128)S(1)}, f32[4,32,1024]{2,1,0:T(8,128)S(1)}, u32[]{:S(2)}, u32[]{:S(2)}) collective-permute-start(f32[4,32,1024]{2,1,0:T(8,128)S(1)} %get-tuple-element.44.mine_in), channel_id=1, source_target_pairs={{0,16},{16,0},{1,17},{17,1},{2,18},{18,2},{3,19},{19,3},{4,20},{20... | collective-permute-start | bytes 1572872 | tf_op jit(solution)/shard_map/ppermute | solution.py:444
  12.9 6.6 %collective-permute-start.4 = (f32[48,128]{1,0:T(8,128)S(1)}, f32[48,128]{1,0:T(8,128)S(1)}, u32[]{:S(2)}, u32[]{:S(2)}) collective-permute-start(f32[48,128]{1,0:T(8,128)S(1)} %get-tuple-element.45), channel_id=1, source_target_pairs={{0,1},{1,2},{2,3},{3,0},{4,5},{5,6},{6,7},{7,4},{8,9},{9,10},{10,1... | collective-permute-start | bytes 73736 | tf_op jit(solution)/shard_map/ppermute | solution.py:447
  15.5 4.1 %collective-permute-start.5 = (f32[48,128]{1,0:T(8,128)S(1)}, f32[48,128]{1,0:T(8,128)S(1)}, u32[]{:S(2)}, u32[]{:S(2)}) collective-permute-start(f32[48,128]{1,0:T(8,128)S(1)} %get-tuple-element.46), channel_id=1, source_target_pairs={{0,3},{1,0},{2,1},{3,2},{4,7},{5,4},{6,5},{7,6},{8,11},{9,8},{10,9... | collective-permute-start | bytes 73736 | tf_op jit(solution)/shard_map/ppermute | solution.py:447
  20.3 1.3 %collective-permute-start.6 = (f32[160,128]{1,0:T(8,128)S(1)}, f32[160,128]{1,0:T(8,128)S(1)}, u32[]{:S(2)}, u32[]{:S(2)}) collective-permute-start(f32[160,128]{1,0:T(8,128)S(1)} %shard_map.60.mine_edge), channel_id=1, source_target_pairs={{0,16},{16,0},{1,17},{17,1},{2,18},{18,2},{3,19},{19,3},{4,20},{20... | collective-permute-start | bytes 245768 | tf_op jit(solution)/shard_map/ppermute | solution.py:444

commit v3 on v2

--- a/solution.py
+++ b/solution.py
@@ -60,50 +60,78 @@
         copy.wait()
 
 
-def edge_kernel(gy_size, members, increment, zonal, merid, mask, sent, own, forcing, coef, mask_buf, sems):
-    rows = increment.shape[1]
+def pack_coefficients(half, coef, out):
+    width = out.shape[1]
+    zm, mm, wet = coef[0], coef[1], coef[2]
+    row = row_ids(TILE, width)
+    col = lax.broadcasted_iota(jnp.int32, (TILE, width), 1)
+    east = zm * jnp.where(col == width - 1, 1.0, pltpu.roll(wet, width - 1, 1))
+    north = mm * jnp.where(row == TILE - 1, 1.0, pltpu.roll(wet, TILE - 1, 0))
+    upper = jnp.where(row < 4, north, pltpu.roll(east, 4, 0))
+    upper = jnp.where(row == 3, pltpu.roll(wet, 3, 0), upper)
+    lower = jnp.where(row < 4, pltpu.roll(north, 4, 0), east)
+    out[...] = jnp.where(half == 0, upper, lower)
+    first = wet[:, :LANES]
+    lane, line = lane_ids(TILE), row_ids(TILE, LANES)
+    value = out[:, :LANES]
+    for r in range(4):
+        moved = jnp.where(half == 0, pltpu.roll(first, 7 - r, 0), pltpu.roll(first, (-r) % TILE, 0))
+        value = jnp.where((line == jnp.where(half == 0, 7, 4)) & (lane == r), pltpu.roll(moved, r, 1), value)
+    out[:, :LANES] = value
+
+
+def pack_rows_kernel(gy_size, own, others, forcing, weights, strip, other):
+    levels, tall, width = own.shape
     half = half_of(gy_size)
-    outer = pl.ds(aligned(half * (rows - TILE)), TILE)
-    other = pl.ds(aligned((1 - half) * (rows - TILE)), TILE)
-    run([
-        pltpu.make_async_copy(members.at[0, :, other, :], sent, sems.at[0]),
-        pltpu.make_async_copy(members.at[0, :, outer, :], own, sems.at[1]),
-        pltpu.make_async_copy(increment.at[:, outer, :], forcing, sems.at[2]),
-        pltpu.make_async_copy(zonal.at[outer, :], coef.at[0], sems.at[3]),
-        pltpu.make_async_copy(merid.at[outer, :], coef.at[1], sems.at[4]),
-        pltpu.make_async_copy(mask.at[outer, :], mask_buf, sems.at[5]),
-    ])
-    wet = mask_buf[...].astype(F32)
-    coef[0] = coef[0] * wet
-    coef[1] = coef[1] * wet
-    coef[2] = wet
-    forcing[...] = forcing[...] * wet[None]
-
-
-def pack_rows_kernel(gy_size, own, other, forcing, coef, strip):
-    levels, _, width = own.shape
-    half = half_of(gy_size)
+    outer = pl.ds(aligned(half * (tall - TILE)), TILE)
+    other[...] = others[0, :, pl.ds(aligned(half * (others.shape[2] - TILE)), TILE), :]
     j = lax.axis_index("gy")
     same_core = jnp.where(half == 0, j == gy_size // 2, j == gy_size // 2 - 1)
     low = row_ids(TILE, width) < TILE // 2
-
-    def put(place, first, second):
+    for level in range(levels):
+        force = forcing[level, outer, :]
+        mine = own[level, outer, :] * force
+        theirs = other[level] * force
+        first, second = jnp.where(same_core, mine, theirs), jnp.where(same_core, theirs, mine)
         first = jnp.where(half == 0, first, pltpu.roll(first, TILE // 2, 0))
         second = jnp.where(half == 0, pltpu.roll(second, TILE // 2, 0), second)
-        strip[place] = jnp.where(low, first, second)
-
-    for level in range(levels):
-        mine = own[level] * forcing[level]
-        theirs = other[level] * forcing[level]
-        put(level, jnp.where(same_core, mine, theirs), jnp.where(same_core, theirs, mine))
-    put(levels, coef[0], coef[1])
-    put(levels + 1, coef[2], coef[2])
-
-
-def received(half, strip, place, cols):
+        strip[level] = jnp.where(low, first, second)
+    strip[levels] = weights[...]
+
+
+def inside_domain(gy_size):
+    half, j = half_of(gy_size), lax.axis_index("gy")
+    return jnp.where(half == 0, j > 0, j < gy_size - 1)
+
+
+def beyond(value, real):
+    return jnp.where(real, value, 0.0)
+
+
+def received(gy_size, strip, place, cols):
     value = strip[place // 2, :, cols]
-    natural = jnp.equal(half, 1 - place % 2)
-    return jnp.where(natural, value, pltpu.roll(value, TILE // 2, 0))
+    natural = jnp.equal(half_of(gy_size), 1 - place % 2)
+    return beyond(jnp.where(natural, value, pltpu.roll(value, TILE // 2, 0)), inside_domain(gy_size))
+
+
+def received_coefficients(gy_size, strip, cols):
+    half, real = half_of(gy_size), inside_domain(gy_size)
+    value = strip[strip.shape[0] - 1, :, cols]
+    moved = pltpu.roll(value, TILE // 2, 0)
+    zm = jnp.where(half == 0, value, moved)
+    mm = jnp.where(half == 0, moved, value)
+    row = row_ids(*value.shape)
+    wet = jnp.where((half == 1) & (row == 0), pltpu.roll(value, 5, 0), 1.0)
+    if cols.start == 0:
+        lane, line = lane_ids(TILE), row_ids(TILE, LANES)
+        first = value[:, :LANES]
+        column = wet[:, :LANES]
+        for r in range(4):
+            shifted = jnp.where(half == 0, pltpu.roll(first, r, 0), pltpu.roll(first, (r + 1) % TILE, 0))
+            at = (line == jnp.where(half == 0, 4 + r, r)) & (lane == 0)
+            column = jnp.where(at, pltpu.roll(shifted, (-r) % LANES, 1), column)
+        wet = jnp.concatenate([column, wet[:, LANES:]], axis=1) if value.shape[1] > LANES else column
+    return [beyond(x, real) for x in (zm, mm, wet)]
 
 
 def edge_columns(first, last):
@@ -129,15 +157,23 @@
     return spread(jnp.where((lane >= 16) & (lane < 24), pltpu.roll(last, 24, 1), total))
 
 
-def outgoing(fields, coefs, west):
-    rows = coefs[0].shape[0]
-    lane = lane_ids(rows)
-    start, step, source = (24, -4, 0) if west else (4, 4, 124)
-    total = jnp.zeros((rows, LANES), F32)
+def outgoing_lanes(west):
+    return (24, -4, 0) if west else (4, 4, 124)
+
+
+def outgoing_coefficients(coefs, west):
+    start, step, source = outgoing_lanes(west)
+    lane = lane_ids(coefs[0].shape[0])
+    total = jnp.zeros(lane.shape, F32)
     for k, value in enumerate(coefs):
         at = start + step * (k + 2)
         total = jnp.where((lane >= at) & (lane < at + 4), pltpu.roll(value, (at - source) % LANES, 1), total)
-    total = spread(total)
+    return spread(total)
+
+
+def outgoing(fields, total, west):
+    start, step, source = outgoing_lanes(west)
+    lane = lane_ids(total.shape[0])
     for k, member in enumerate(fields):
         for level, value in enumerate(member):
             at = GROUP * level + start + step * k
@@ -184,31 +220,74 @@
     return east, north
 
 
+def load_kernel(
+    gy_size, members, increment, zonal, merid, mask,
+    own, forcing, coef, weights, east, north, pack_coef, west_out, east_out,
+    mask_buf, zm, mm, wet, face, sems,
+):
+    _, tall, width = own.shape
+    tiles = width // LANES
+    planes = east.shape[0]
+    offset = tall - planes
+    half = half_of(gy_size)
+    part = pl.ds(aligned(half * (tall - 2 * TILE)), tall)
+    small = [
+        pltpu.make_async_copy(mask.at[part, :], mask_buf, sems.at[0]),
+        pltpu.make_async_copy(zonal.at[part, :], zm, sems.at[1]),
+        pltpu.make_async_copy(merid.at[part, :], mm, sems.at[2]),
+    ]
+    large = [
+        pltpu.make_async_copy(increment.at[:, part, :], forcing, sems.at[3]),
+        pltpu.make_async_copy(members.at[0, :, part, :], own, sems.at[4]),
+    ]
+    for copy in small + large:
+        copy.start()
+    for copy in small:
+        copy.wait()
+    wet[:tall, :] = mask_buf[...].astype(F32)
+    wet[tall:, :] = jnp.zeros((TILE, width), F32)
+    zm[...] = zm[...] * wet[:tall, :]
+    mm[...] = mm[...] * wet[:tall, :]
+    outer = pl.ds(aligned(half * (tall - TILE)), TILE)
+    for k, ref in enumerate((zm, mm, wet)):
+        coef[k] = ref[outer, :]
+    pack_coefficients(half, coef, weights)
+    for c in range(tiles):
+        face[pl.ds(c * tall, tall), :], face[pl.ds((tiles + c) * tall, tall), :] = faces(zm, mm, wet, tile(c), width, tall)
+    for q in range(planes):
+        for k, ref in enumerate((east, north)):
+            ref[q, BODY, :] = turn(face, [k * tiles * tall + ch * offset + q for _ in range(TILE) for ch in range(2)], tall)
+    refresh(east, 0, planes)
+    lead = pl.ds(aligned((1 - half) * TILE), tall)
+    ends = (tile(0), tile(tiles - 1))
+    for k, ref in enumerate((zm, mm, wet)):
+        pack_coef[k, lead, :] = edge_coefficient(*(ref[:tall, cols] for cols in ends))
+    for out_strip, c, west in ((west_out, 0, True), (east_out, tiles - 1, False)):
+        out_strip[lead, :] = outgoing_coefficients([ref[:tall, tile(c)] for ref in (zm, mm, wet)], west)
+    large[0].wait()
+    forcing[...] = forcing[...] * wet[:tall, :][None]
+    large[1].wait()
+
+
 def interior_kernel(
-    gy_size, members, others, increment, zonal, merid, mask,
-    out, pack_own, pack_other, pack_coef, weight_own, weight_other, west_out, east_out,
-    zm, mm, wet, field, face, u, u_next, east, north, result,
+    gy_size, own, others, forcing, east, north, west_in, east_in,
+    out, pack_own, pack_other, weight_own, weight_other, west_out, east_out,
+    field, u, u_next, result,
 ):
-    _, levels, rows, width = members.shape
+    levels, tall, width = own.shape
     tiles = width // LANES
-    mid = rows // 2
-    tall = mid + TILE
-    offset = tall - 3 * TILE
-    planes = tall - offset
+    mid = tall - TILE
+    planes = east.shape[0]
+    offset = tall - planes
     half = half_of(gy_size)
     part = pl.ds(aligned(half * (mid - TILE)), tall)
-    wet[:tall, :] = mask[part, :].astype(F32)
-    wet[tall:, :] = jnp.zeros((TILE, width), F32)
-    zm[...] = zonal[part, :] * wet[:tall, :]
-    mm[...] = merid[part, :] * wet[:tall, :]
-    sources = (members, others)
+    keep_own, keep_other = pl.ds(aligned(half * TILE), mid), pl.ds(aligned(half * mid), mid)
     for c in range(tiles):
         cols = tile(c)
-        face[pl.ds(c * tall, tall), :], face[pl.ds((tiles + c) * tall, tall), :] = faces(zm, mm, wet, cols, width, tall)
         for level in range(levels):
-            force = increment[level, part, cols] * wet[:tall, cols]
-            for k, member in enumerate(sources):
-                field[pl.ds(((2 * level + k) * tiles + c) * tall, tall), :] = member[0, level, part, cols] * force
+            force = forcing[level, :, cols]
+            for k, member in enumerate((own[level, :, cols], others[0, level, part, cols])):
+                field[pl.ds(((2 * level + k) * tiles + c) * tall, tall), :] = member * force
 
     def at(f, c):
         return field[pl.ds((f * tiles + c) * tall, tall), :]
@@ -217,24 +296,15 @@
     lead = pl.ds(aligned((1 - half) * TILE), tall)
     for k, pack in enumerate((pack_own, pack_other)):
         pack[lead, :] = edge_columns(*([at(2 * level + k, c) for level in range(levels)] for c in (0, tiles - 1)))
-    for k, ref in enumerate((zm, mm, wet)):
-        pack_coef[k, lead, :] = edge_coefficient(*(ref[:tall, cols] for cols in ends))
-    keep = pl.ds(aligned(half * mid), mid)
-    for member, weight in zip(sources, (weight_own, weight_other)):
-        weight[...] = edge_columns(*([member[0, level, keep, cols] for level in range(levels)] for cols in ends))
-    for out_strip, c, west in ((west_out, 0, True), (east_out, tiles - 1, False)):
-        out_strip[lead, :] = outgoing(
-            [[at(2 * level + k, c) for level in range(levels)] for k in range(2)],
-            [ref[:tall, tile(c)] for ref in (zm, mm, wet)],
-            west,
-        )
+    weight_own[...] = edge_columns(*([own[level, keep_own, cols] for level in range(levels)] for cols in ends))
+    weight_other[...] = edge_columns(*([others[0, level, keep_other, cols] for level in range(levels)] for cols in ends))
+    for source, out_strip, c, west in ((west_in, west_out, 0, True), (east_in, east_out, tiles - 1, False)):
+        columns = [[at(2 * level + k, c) for level in range(levels)] for k in range(2)]
+        out_strip[lead, :] = outgoing(columns, source[lead, :], west)
 
     fields = range(2 * levels)
     for q in range(planes):
         u[q, BODY, :] = turn(field, [f * tiles * tall + ch * offset + q for f in fields for ch in range(2)], tall)
-        for k, ref in enumerate((east, north)):
-            ref[q, BODY, :] = turn(face, [k * tiles * tall + ch * offset + q for f in fields for ch in range(2)], tall)
-    refresh(east, 0, planes)
     source, target = u, u_next
     for step in range(STEPS):
         sweep(source, target, east, north, step + 1, planes - 2 - step)
@@ -250,11 +320,11 @@
             a, b = (
                 result[pl.ds(aligned(((2 * level + k) * tiles + c) * tall + half * TILE), mid), :] for k in range(2)
             )
-            out[level, :, tile(c)] = members[0, level, keep, tile(c)] * a + others[0, level, keep, tile(c)] * b
+            out[level, :, tile(c)] = own[level, keep_own, tile(c)] * a + others[0, level, keep_other, tile(c)] * b
 
 
 def halo_columns_kernel(gy_size, strip, west_in, east_in, west_out, east_out):
-    levels = strip.shape[0] - 2
+    levels = strip.shape[0] - 1
     width = strip.shape[2]
     half = half_of(gy_size)
     full = west_out.shape[0]
@@ -266,8 +336,8 @@
     ):
         out[main, :] = source[main, :]
         out[halo, :] = outgoing(
-            [[received(half, strip, 2 * level + k, cols) for level in range(levels)] for k in range(2)],
-            [received(half, strip, 2 * levels + k, cols) for k in range(3)],
+            [[received(gy_size, strip, 2 * level + k, cols) for level in range(levels)] for k in range(2)],
+            outgoing_coefficients(received_coefficients(gy_size, strip, cols), west),
             west,
         )
 
@@ -277,25 +347,26 @@
     sums, full_own, full_other, full_coef,
     zm, mm, wet, field, face, u, u_next, east, north, result,
 ):
-    levels, _, width = own.shape
+    levels, tall, width = own.shape
     tiles = width // LANES
     half = half_of(gy_size)
+    outer = pl.ds(aligned(half * (tall - TILE)), TILE)
     edge = pl.ds(aligned((1 - half) * TILE), TILE)
     halo = pl.ds(aligned(half * TILE), TILE)
     block = 2 * TILE
     every = slice(0, width)
-    for k, ref in enumerate((zm, mm, wet)):
+    for k, (ref, value) in enumerate(zip((zm, mm, wet), received_coefficients(gy_size, strip, every))):
         ref[edge, :] = coef[k]
-        ref[halo, :] = received(half, strip, 2 * levels + k, every)
+        ref[halo, :] = value
     wet[block:, :] = jnp.zeros((TILE, width), F32)
     for c in range(tiles):
         cols = tile(c)
         face[pl.ds(c * block, block), :], face[pl.ds((tiles + c) * block, block), :] = faces(zm, mm, wet, cols, width, block)
         for level in range(levels):
-            for k, member in enumerate((own, other)):
+            for k, member in enumerate((own[level, outer, cols], other[level, :, cols])):
                 base = ((2 * level + k) * tiles + c) * block
-                field[pl.ds(aligned(base + (1 - half) * TILE), TILE), :] = member[level, :, cols] * forcing[level, :, cols]
-                field[pl.ds(aligned(base + half * TILE), TILE), :] = received(half, strip, 2 * level + k, cols)
+                field[pl.ds(aligned(base + (1 - half) * TILE), TILE), :] = member * forcing[level, outer, cols]
+                field[pl.ds(aligned(base + half * TILE), TILE), :] = received(gy_size, strip, 2 * level + k, cols)
 
     fields = range(2 * levels)
     planes = 10
@@ -321,7 +392,7 @@
         terms = []
         for level in range(levels):
             a, b = (result[pl.ds(((2 * level + k) * tiles + c) * TILE, TILE), :] for k in range(2))
-            terms.append(own[level, :, cols] * a + other[level, :, cols] * b)
+            terms.append(own[level, outer, cols] * a + other[level, :, cols] * b)
         for pair in range(levels // 2):
             sums[pl.ds((c * levels // 2 + pair) * TILE, TILE), :] = jnp.where(
                 natural, terms[2 * pair], pltpu.roll(terms[2 * pair + 1], 4, 0)
@@ -329,16 +400,16 @@
 
     full = full_own.shape[0]
     main = pl.ds(aligned((1 - half) * TILE), full - TILE)
-    beyond = pl.ds(aligned(half * (full - TILE)), TILE)
+    outside = pl.ds(aligned(half * (full - TILE)), TILE)
     ends = (slice(0, LANES), slice(width - LANES, width))
     for k, (source, out) in enumerate(((pack_own, full_own), (pack_other, full_other))):
         out[main, :] = source[main, :]
-        out[beyond, :] = edge_columns(
-            *([received(half, strip, 2 * level + k, cols) for level in range(levels)] for cols in ends)
+        out[outside, :] = edge_columns(
+            *([received(gy_size, strip, 2 * level + k, cols) for level in range(levels)] for cols in ends)
         )
-    for k in range(3):
+    for k, (first, last) in enumerate(zip(*(received_coefficients(gy_size, strip, cols) for cols in ends))):
         full_coef[k, main, :] = pack_coef[k, main, :]
-        full_coef[k, beyond, :] = edge_coefficient(*(received(half, strip, 2 * levels + k, cols) for cols in ends))
+        full_coef[k, outside, :] = edge_coefficient(first, last)
 
 
 def end_columns_kernel(
@@ -458,39 +529,46 @@
                     a = place(chip, 1 - first[j], j, i)
                     b = place(chip, first[j + 1], j + 1, i)
                     pairs += [(a, b), (b, a)]
+            for i in range(n_gx - n_gx % 2):
+                pairs.append((place(chip, first[0], 0, i), place(chip, first[0], 0, i ^ 1)))
+                pairs.append((place(chip, 1 - first[-1], n_gy - 1, i), place(chip, 1 - first[-1], n_gy - 1, i ^ 1)))
         return lax.ppermute(x, AXES, pairs)
 
     def scratch(*shape):
         return pltpu.VMEM(shape, F32)
 
-    arrays = [members, increment, zonal_diff, merid_diff, sea_mask]
-    sent, own, forcing, coef = call(
-        edge_kernel,
-        [in_hbm(x) for x in arrays],
+    others = swap(members)
+    end = kept(full, LANES)
+    turned = kept(planes, DEPTH, LANES)
+    own, forcing, coef, weights, face_east, face_north, pack_coef, west, east = call(
+        load_kernel,
+        [in_hbm(x) for x in (members, increment, zonal_diff, merid_diff, sea_mask)],
         [HBM] * 5,
-        [kept(levels, TILE, width)] * 3 + [kept(3, TILE, width)],
-        [pltpu.VMEM((TILE, width), jnp.int32), pltpu.SemaphoreType.DMA((6,))],
-    )
-    other = swap(sent)
-    members_later, other = lax.optimization_barrier((members, other))
-    others = swap(members_later)
-    strip = held(pack_rows_kernel, [own, other, forcing, coef], kept(levels + 2, TILE, width))
-    zonal_later, strip = lax.optimization_barrier((zonal_diff, strip))
-    strip = across(strip)
-
-    end = kept(full, LANES)
-    inside, pack_own, pack_other, pack_coef, weight_own, weight_other, west, east = held(
-        interior_kernel,
-        [members, others, increment, zonal_later, merid_diff, sea_mask],
-        [kept(levels, mid, width), end, end, kept(3, full, LANES), kept(mid, LANES), kept(mid, LANES), end, end],
+        [kept(levels, tall, width)] * 2
+        + [kept(3, TILE, width), kept(TILE, width), turned, turned, kept(3, full, LANES), end, end],
         [
+            pltpu.VMEM((tall, width), jnp.int32),
             scratch(tall, width),
             scratch(tall, width),
             scratch(full, width),
+            scratch(2 * tiles * tall, LANES),
+            pltpu.SemaphoreType.DMA((5,)),
+        ],
+    )
+    strip, other = held(
+        pack_rows_kernel,
+        [own, others, forcing, weights],
+        [kept(levels + 1, TILE, width), kept(levels, TILE, width)],
+    )
+    forcing, strip = lax.optimization_barrier((forcing, strip))
+    strip = across(strip)
+
+    inside, pack_own, pack_other, weight_own, weight_other, west, east = held(
+        interior_kernel,
+        [own, others, forcing, face_east, face_north, west, east],
+        [kept(levels, mid, width), end, end, kept(mid, LANES), kept(mid, LANES), end, end],
+        [
             scratch(2 * levels * tiles * tall, LANES),
-            scratch(2 * tiles * tall, LANES),
-            scratch(planes, DEPTH, LANES),
-            scratch(planes, DEPTH, LANES),
             scratch(planes, DEPTH, LANES),
             scratch(planes, DEPTH, LANES),
             scratch(2 * levels * tiles * tall, LANES),

time: 22.9 us -> 20.1 us (0.88)
  waiting for transfers between devices: 4.28 us -> 2.1 us
  starting transfers between devices: 9.51 us -> 8.67 us
  Pallas kernels: 8.87 us -> 9.14 us
    ppermute x4 -> x3, starting transfers between devices: 4.05 us -> 1.42 us  [swap(): return lax.ppermute(x, 'mem', [(i, i ^ 1) for i in range(n_mem)])]
    ppermute x4 -> x3, waiting for transfers between devices: 3.67 us -> 1.27 us  [swap(): return lax.ppermute(x, 'mem', [(i, i ^ 1) for i in range(n_mem)])]
    ppermute x1, starting transfers between devices: 0.8 us -> 2.96 us  [across(): return lax.ppermute(x, AXES, pairs)]
    ppermute x2, starting transfers between devices: 4.65 us -> 4.28 us  [along(): return lax.ppermute(x, 'gx', [(i, (i + shift) % n_gx) for i in range(n_gx)])]
    ppermute x1, waiting for transfers between devices: 0.01 us -> 0.34 us  [across(): return lax.ppermute(x, AXES, pairs)]
    pallas_call x7, Pallas kernels: 8.87 us -> 9.14 us  [call(): pl.pallas_call(functools.partial(kernel, n_gy), out_shape=outs, in_specs=...]
  transfers between devices with their start and end apart: 7 -> 6, of which waited for: 5 -> 4; matrix products, arithmetic and copies ran while one was open for 0% -> 0% of each run, Pallas kernels for 28% -> 38%
where the time goes in v3:
time: 20.1 us; the launch traced here: 20 us
  Pallas kernels  9.14 us (45%)
  starting transfers between devices  8.67 us (43%)
  waiting for transfers between devices  2.1 us (10%)
    pallas_call x7, Pallas kernels, call(): pl.pallas_call(functools.partial(kernel, n_gy), out_shape=outs, in_specs=...  9.14 us
    ppermute x2, starting transfers between devices, along(): return lax.ppermute(x, 'gx', [(i, (i + shift) % n_gx) for i in range(n_gx)])  4.28 us
    ppermute x1, starting transfers between devices, across(): return lax.ppermute(x, AXES, pairs)  2.96 us
    ppermute x3, starting transfers between devices, swap(): return lax.ppermute(x, 'mem', [(i, i ^ 1) for i in range(n_mem)])  1.42 us
    ppermute x3, waiting for transfers between devices, swap(): return lax.ppermute(x, 'mem', [(i, i ^ 1) for i in range(n_mem)])  1.27 us
    ppermute x2, waiting for transfers between devices, along(): return lax.ppermute(x, 'gx', [(i, (i + shift) % n_gx) for i in range(n_gx)])  0.49 us
  transfers between devices with their start and end apart: 6, of which 4 were waited for; matrix products, arithmetic and copies ran while one was open for 0% of the time, Pallas kernels for 38%

profile of v3, /device:TPU:0, one launch (start us, length us, event | category | flops | bytes accessed | tf_op | source)
XLA Modules:
  0.0 20.0 jit_solution(13476001005065489490)
XLA Ops:
  0.0 0.5 %collective-permute-start = (f32[1,4,64,1024]{3,2,1,0:T(8,128)}, f32[1,4,64,1024]{3,2,1,0:T(8,128)S(1)}, u32[]{:S(2)}, u32[]{:S(2)}) collective-permute-start(f32[1,4,64,1024]{3,2,1,0:T(8,128)} %members.1), channel_id=1, source_target_pairs={{0,16},{16,0},{1,17},{17,1},{2,18},{18,2},{3,19},{19,3},{4,20},{20... | collective-permute-start | bytes 3145736 | tf_op jit(solution)/shard_map/ppermute | solution.py:515
  0.5 2.5 %shard_map.55 = (f32[4,40,1024]{2,1,0:T(8,128)S(1)}, f32[4,40,1024]{2,1,0:T(8,128)S(1)}, f32[3,8,1024]{2,1,0:T(8,128)S(1)}, f32[8,1024]{1,0:T(8,128)S(1)}, f32[2...) custom-call(f32[1,4,64,1024]{3,2,1,0:T(8,128)} %members.1, ...), custom_call_target="tpu_custom_call" | custom-call | tf_op jit(solution)/shard_map/pallas_call | solution.py:500
  3.0 0.0 collective-permute-done.others
  3.0 0.1 shard_map.56
  3.1 3.0 %collective-permute-start.1 = (f32[5,8,1024]{2,1,0:T(8,128)S(1)}, f32[5,8,1024]{2,1,0:T(8,128)S(1)}, u32[]{:S(2)}, u32[]{:S(2)}) collective-permute-start(f32[5,8,1024]{2,1,0:T(8,128)S(1)} %get-tuple-element.45), channel_id=1, source_target_pairs={{16,4},{4,16},{17,5},{5,17},{18,6},{6,18},{19,7},{7,19},{20,24},{2... | collective-permute-start | bytes 491528 | tf_op jit(solution)/shard_map/ppermute | solution.py:535
  6.0 2.9 %shard_map.57 = (f32[4,32,1024]{2,1,0:T(8,128)S(1)}, f32[48,128]{1,0:T(8,128)S(1)}, f32[48,128]{1,0:T(8,128)S(1)}, f32[32,128]{1,0:T(8,128)S(1)}, f32[32,128]{1,...) custom-call(f32[4,40,1024]{2,1,0:T(8,128)S(1)} %get-tuple-element.35.own, ...), custom_call_target="tpu_custom_call" | custom-call | tf_op jit(solution)/shard_map/pallas_call | solution.py:500
  9.0 0.3 %collective-permute-done.1.strip = f32[5,8,1024]{2,1,0:T(8,128)S(1)} collective-permute-done((f32[5,8,1024]{2,1,0:T(8,128)S(1)}, f32[5,8,1024]{2,1,0:T(8,128)S(1)}, u32[]{:S(2)}, u32[]{:S(2)}) %collective-permute-start.1) | collective-permute-done | bytes 163872 | tf_op jit(solution)/shard_map/ppermute | solution.py:535
  9.3 0.3 %shard_map.58 = (f32[48,128]{1,0:T(8,128)S(1)}, f32[48,128]{1,0:T(8,128)S(1)}) custom-call(f32[5,8,1024]{2,1,0:T(8,128)S(1)} %collective-permute-done.1.strip, f32[48,128]{1,0:T(8,128)S(1)} %get-tuple-element.46.west_in, f32[48,128]{1,0:T(8,128)S(1)} %get-tuple-element.47.east_in), custom_call_target="tpu_custom_call" | custom-call | tf_op jit(solution)/shard_map/pallas_call | solution.py:500
  9.6 0.9 %collective-permute-start.2 = (f32[4,32,1024]{2,1,0:T(8,128)S(1)}, f32[4,32,1024]{2,1,0:T(8,128)S(1)}, u32[]{:S(2)}, u32[]{:S(2)}) collective-permute-start(f32[4,32,1024]{2,1,0:T(8,128)S(1)} %get-tuple-element.50.mine_in), channel_id=1, source_target_pairs={{0,16},{16,0},{1,17},{17,1},{2,18},{18,2},{3,19},{19,3},{4,20},{20... | collective-permute-start | bytes 1572872 | tf_op jit(solution)/shard_map/ppermute | solution.py:515
  10.5 2.3 %collective-permute-start.3 = (f32[48,128]{1,0:T(8,128)S(1)}, f32[48,128]{1,0:T(8,128)S(1)}, u32[]{:S(2)}, u32[]{:S(2)}) collective-permute-start(f32[48,128]{1,0:T(8,128)S(1)} %get-tuple-element.51), channel_id=1, source_target_pairs={{0,1},{1,2},{2,3},{3,0},{4,5},{5,6},{6,7},{7,4},{8,9},{9,10},{10,1... | collective-permute-start | bytes 73736 | tf_op jit(solution)/shard_map/ppermute | solution.py:518
  12.8 2.0 %collective-permute-start.4 = (f32[48,128]{1,0:T(8,128)S(1)}, f32[48,128]{1,0:T(8,128)S(1)}, u32[]{:S(2)}, u32[]{:S(2)}) collective-permute-start(f32[48,128]{1,0:T(8,128)S(1)} %get-tuple-element.52), channel_id=1, source_target_pairs={{0,3},{1,0},{2,1},{3,2},{4,7},{5,4},{6,5},{7,6},{8,11},{9,8},{10,9... | collective-permute-start | bytes 73736 | tf_op jit(solution)/shard_map/ppermute | solution.py:518
  14.8 1.6 %shard_map.59 = (f32[128,128]{1,0:T(8,128)S(1)}, f32[48,128]{1,0:T(8,128)S(1)}, f32[48,128]{1,0:T(8,128)S(1)}, f32[3,48,128]{2,1,0:T(8,128)S(1)}) custom-call(f32[5,8,1024]{2,1,0:T(8,128)S(1)} %collective-permute-done.1.strip, f32[4,40,1024]{2,1,0:T(8,128)S(1)} %get-tuple-element.35.own, f32[4,8,1024]{2,1,0:T(8,128)S(1)} %get-tuple-element.53.other, ...), custom_call_target="tpu_custom_call" | custom-call | tf_op jit(solution)/shard_map/pallas_call | solution.py:500
  16.4 0.4 %collective-permute-done.3.from_west = f32[48,128]{1,0:T(8,128)S(1)} collective-permute-done((f32[48,128]{1,0:T(8,128)S(1)}, f32[48,128]{1,0:T(8,128)S(1)}, u32[]{:S(2)}, u32[]{:S(2)}) %collective-permute-start.3) | collective-permute-done | bytes 24608 | tf_op jit(solution)/shard_map/ppermute | solution.py:518
  16.7 0.1 collective-permute-done.4.from_east
  16.9 0.7 %shard_map.60.mine_edge = f32[160,128]{1,0:T(8,128)S(1)} custom-call(f32[48,128]{1,0:T(8,128)S(1)} %collective-permute-done.3.from_west, f32[48,128]{1,0:T(8,128)S(1)} %collective-permute-done.4.from_east, f32[48,128]{1,0:T(8,128)S(1)} %get-tuple-element.58.own, f32[48,128]{1,0:T(8,128)S(1)} %get-tuple-element.59.other, ...), custom_call_target="tpu_custom_call" | custom-call | tf_op jit(solution)/shard_map/pallas_call | solution.py:500
  17.5 0.1 collective-permute-start.5
  17.6 1.3 %collective-permute-done.5.theirs_edge = f32[160,128]{1,0:T(8,128)S(1)} collective-permute-done((f32[160,128]{1,0:T(8,128)S(1)}, f32[160,128]{1,0:T(8,128)S(1)}, u32[]{:S(2)}, u32[]{:S(2)}) %collective-permute-start.5) | collective-permute-done | bytes 81952 | tf_op jit(solution)/shard_map/ppermute | solution.py:515
  18.9 0.0 collective-permute-done.2.theirs_in
  18.9 1.1 %shard_map.61 = (f32[4,32,1024]{2,1,0:T(8,128)S(1)}, f32[4,32,1024]{2,1,0:T(8,128)S(1)}, f32[4,64,1024]{2,1,0:T(8,128)}) custom-call(f32[4,32,1024]{2,1,0:T(8,128)S(1)} %get-tuple-element.50.mine_in, f32[4,32,1024]{2,1,0:T(8,128)S(1)} %collective-permute-done.2.theirs_in, ...), custom_call_target="tpu_custom_call", output_to_operand_aliasing={{0}: (0, {}), {1}: (1, {})} | custom-call | tf_op jit(solution)/shard_map/pallas_call | solution.py:500
Async XLA Ops:
  0.0 3.0 %collective-permute-start = (f32[1,4,64,1024]{3,2,1,0:T(8,128)}, f32[1,4,64,1024]{3,2,1,0:T(8,128)S(1)}, u32[]{:S(2)}, u32[]{:S(2)}) collective-permute-start(f32[1,4,64,1024]{3,2,1,0:T(8,128)} %members.1), channel_id=1, source_target_pairs={{0,16},{16,0},{1,17},{17,1},{2,18},{18,2},{3,19},{19,3},{4,20},{20... | collective-permute-start | bytes 3145736 | tf_op jit(solution)/shard_map/ppermute | solution.py:515
  3.1 6.3 %collective-permute-start.1 = (f32[5,8,1024]{2,1,0:T(8,128)S(1)}, f32[5,8,1024]{2,1,0:T(8,128)S(1)}, u32[]{:S(2)}, u32[]{:S(2)}) collective-permute-start(f32[5,8,1024]{2,1,0:T(8,128)S(1)} %get-tuple-element.45), channel_id=1, source_target_pairs={{16,4},{4,16},{17,5},{5,17},{18,6},{6,18},{19,7},{7,19},{20,24},{2... | collective-permute-start | bytes 491528 | tf_op jit(solution)/shard_map/ppermute | solution.py:535
  9.6 9.3 %collective-permute-start.2 = (f32[4,32,1024]{2,1,0:T(8,128)S(1)}, f32[4,32,1024]{2,1,0:T(8,128)S(1)}, u32[]{:S(2)}, u32[]{:S(2)}) collective-permute-start(f32[4,32,1024]{2,1,0:T(8,128)S(1)} %get-tuple-element.50.mine_in), channel_id=1, source_target_pairs={{0,16},{16,0},{1,17},{17,1},{2,18},{18,2},{3,19},{19,3},{4,20},{20... | collective-permute-start | bytes 1572872 | tf_op jit(solution)/shard_map/ppermute | solution.py:515
  10.5 6.2 %collective-permute-start.3 = (f32[48,128]{1,0:T(8,128)S(1)}, f32[48,128]{1,0:T(8,128)S(1)}, u32[]{:S(2)}, u32[]{:S(2)}) collective-permute-start(f32[48,128]{1,0:T(8,128)S(1)} %get-tuple-element.51), channel_id=1, source_target_pairs={{0,1},{1,2},{2,3},{3,0},{4,5},{5,6},{6,7},{7,4},{8,9},{9,10},{10,1... | collective-permute-start | bytes 73736 | tf_op jit(solution)/shard_map/ppermute | solution.py:518
  12.8 4.1 %collective-permute-start.4 = (f32[48,128]{1,0:T(8,128)S(1)}, f32[48,128]{1,0:T(8,128)S(1)}, u32[]{:S(2)}, u32[]{:S(2)}) collective-permute-start(f32[48,128]{1,0:T(8,128)S(1)} %get-tuple-element.52), channel_id=1, source_target_pairs={{0,3},{1,0},{2,1},{3,2},{4,7},{5,4},{6,5},{7,6},{8,11},{9,8},{10,9... | collective-permute-start | bytes 73736 | tf_op jit(solution)/shard_map/ppermute | solution.py:518
  17.5 1.3 %collective-permute-start.5 = (f32[160,128]{1,0:T(8,128)S(1)}, f32[160,128]{1,0:T(8,128)S(1)}, u32[]{:S(2)}, u32[]{:S(2)}) collective-permute-start(f32[160,128]{1,0:T(8,128)S(1)} %shard_map.60.mine_edge), channel_id=1, source_target_pairs={{0,16},{16,0},{1,17},{17,1},{2,18},{18,2},{3,19},{19,3},{4,20},{20... | collective-permute-start | bytes 245768 | tf_op jit(solution)/shard_map/ppermute | solution.py:515

commit v4 on v3

--- a/solution.py
+++ b/solution.py
@@ -7,6 +7,7 @@
 from jax.sharding import PartitionSpec as P
 
 STEPS = 4
+FIRST_STEPS = 2
 TILE = 8
 LANES = 128
 AXES = ("mem", "gy", "gx")
@@ -60,7 +61,8 @@
         copy.wait()
 
 
-def pack_coefficients(half, coef, out):
+def pack_coefficients_kernel(gy_size, coef, out):
+    half = half_of(gy_size)
     width = out.shape[1]
     zm, mm, wet = coef[0], coef[1], coef[2]
     row = row_ids(TILE, width)
@@ -80,22 +82,34 @@
     out[:, :LANES] = value
 
 
-def pack_rows_kernel(gy_size, own, others, forcing, weights, strip, other):
-    levels, tall, width = own.shape
-    half = half_of(gy_size)
-    outer = pl.ds(aligned(half * (tall - TILE)), TILE)
-    other[...] = others[0, :, pl.ds(aligned(half * (others.shape[2] - TILE)), TILE), :]
+def outer_rows_of(gy_size, level, own, other, forcing, cols):
+    half = half_of(gy_size)
     j = lax.axis_index("gy")
     same_core = jnp.where(half == 0, j == gy_size // 2, j == gy_size // 2 - 1)
-    low = row_ids(TILE, width) < TILE // 2
+    outer = pl.ds(aligned(half * (own.shape[1] - TILE)), TILE)
+    force = forcing[level, outer, cols]
+    mine = own[level, outer, cols] * force
+    theirs = other[level, :, cols] * force
+    first, second = jnp.where(same_core, mine, theirs), jnp.where(same_core, theirs, mine)
+    first = jnp.where(half == 0, first, pltpu.roll(first, TILE // 2, 0))
+    second = jnp.where(half == 0, pltpu.roll(second, TILE // 2, 0), second)
+    return jnp.where(row_ids(*first.shape) < TILE // 2, first, second)
+
+
+def pack_corner_kernel(gy_size, own, others, forcing, weights, other, corner):
+    levels, _, width = own.shape
+    other[...] = others[0, :, pl.ds(aligned(half_of(gy_size) * (others.shape[2] - TILE)), TILE), :]
+    ends = (tile(0), slice(width - LANES, width))
+    corner[:TILE, :] = edge_columns(
+        *([outer_rows_of(gy_size, level, own, other, forcing, cols) for level in range(levels)] for cols in ends)
+    )
+    corner[TILE:, :] = edge_coefficient(*(weights[:, cols] for cols in ends))
+
+
+def pack_rows_kernel(gy_size, own, other, forcing, weights, strip):
+    levels, _, width = own.shape
     for level in range(levels):
-        force = forcing[level, outer, :]
-        mine = own[level, outer, :] * force
-        theirs = other[level] * force
-        first, second = jnp.where(same_core, mine, theirs), jnp.where(same_core, theirs, mine)
-        first = jnp.where(half == 0, first, pltpu.roll(first, TILE // 2, 0))
-        second = jnp.where(half == 0, pltpu.roll(second, TILE // 2, 0), second)
-        strip[level] = jnp.where(low, first, second)
+        strip[level] = outer_rows_of(gy_size, level, own, other, forcing, slice(0, width))
     strip[levels] = weights[...]
 
 
@@ -108,29 +122,24 @@
     return jnp.where(real, value, 0.0)
 
 
-def received(gy_size, strip, place, cols):
-    value = strip[place // 2, :, cols]
+def unfold(gy_size, value, place):
     natural = jnp.equal(half_of(gy_size), 1 - place % 2)
     return beyond(jnp.where(natural, value, pltpu.roll(value, TILE // 2, 0)), inside_domain(gy_size))
 
 
-def received_coefficients(gy_size, strip, cols):
+def unfold_weights(gy_size, value, packed):
     half, real = half_of(gy_size), inside_domain(gy_size)
-    value = strip[strip.shape[0] - 1, :, cols]
     moved = pltpu.roll(value, TILE // 2, 0)
     zm = jnp.where(half == 0, value, moved)
     mm = jnp.where(half == 0, moved, value)
-    row = row_ids(*value.shape)
-    wet = jnp.where((half == 1) & (row == 0), pltpu.roll(value, 5, 0), 1.0)
-    if cols.start == 0:
-        lane, line = lane_ids(TILE), row_ids(TILE, LANES)
-        first = value[:, :LANES]
-        column = wet[:, :LANES]
+    line = row_ids(*value.shape)
+    wet = jnp.where((half == 1) & (line == 0), pltpu.roll(value, 5, 0), 1.0)
+    if packed:
+        place = lane_ids(TILE) % GROUP
         for r in range(4):
-            shifted = jnp.where(half == 0, pltpu.roll(first, r, 0), pltpu.roll(first, (r + 1) % TILE, 0))
-            at = (line == jnp.where(half == 0, 4 + r, r)) & (lane == 0)
-            column = jnp.where(at, pltpu.roll(shifted, (-r) % LANES, 1), column)
-        wet = jnp.concatenate([column, wet[:, LANES:]], axis=1) if value.shape[1] > LANES else column
+            shifted = jnp.where(half == 0, pltpu.roll(value, r, 0), pltpu.roll(value, (r + 1) % TILE, 0))
+            at = (line == jnp.where(half == 0, 4 + r, r)) & (place == 8)
+            wet = jnp.where(at, pltpu.roll(shifted, (-r) % LANES, 1), wet)
     return [beyond(x, real) for x in (zm, mm, wet)]
 
 
@@ -157,27 +166,13 @@
     return spread(jnp.where((lane >= 16) & (lane < 24), pltpu.roll(last, 24, 1), total))
 
 
-def outgoing_lanes(west):
-    return (24, -4, 0) if west else (4, 4, 124)
-
-
-def outgoing_coefficients(coefs, west):
-    start, step, source = outgoing_lanes(west)
-    lane = lane_ids(coefs[0].shape[0])
-    total = jnp.zeros(lane.shape, F32)
-    for k, value in enumerate(coefs):
-        at = start + step * (k + 2)
-        total = jnp.where((lane >= at) & (lane < at + 4), pltpu.roll(value, (at - source) % LANES, 1), total)
-    return spread(total)
-
-
-def outgoing(fields, total, west):
-    start, step, source = outgoing_lanes(west)
-    lane = lane_ids(total.shape[0])
-    for k, member in enumerate(fields):
-        for level, value in enumerate(member):
-            at = GROUP * level + start + step * k
-            total = jnp.where((lane >= at) & (lane < at + 4), pltpu.roll(value, (at - source) % LANES, 1), total)
+def outgoing(values, west):
+    place = lane_ids(values[0].shape[0]) % GROUP
+    start, step, source = (24, -4, 8) if west else (4, 4, 20)
+    total = jnp.zeros(values[0].shape, F32)
+    for k, value in enumerate(values):
+        at = start + step * k
+        total = jnp.where((place >= at) & (place < at + 4), pltpu.roll(value, (at - source) % LANES, 1), total)
     return total
 
 
@@ -196,7 +191,6 @@
 
 
 def sweep(source, target, east, north, first, last):
-    refresh(source, first, last - first + 1)
     for start in range(TILE, TILE + LANES, TILE):
         at, ahead, behind = (slice(start + d, start + d + TILE) for d in (0, 1, -1))
         here = source[first, at, :]
@@ -222,7 +216,7 @@
 
 def load_kernel(
     gy_size, members, increment, zonal, merid, mask,
-    own, forcing, coef, weights, east, north, pack_coef, west_out, east_out,
+    own, forcing, coef, east, north, pack_coef,
     mask_buf, zm, mm, wet, face, sems,
 ):
     _, tall, width = own.shape
@@ -251,28 +245,24 @@
     outer = pl.ds(aligned(half * (tall - TILE)), TILE)
     for k, ref in enumerate((zm, mm, wet)):
         coef[k] = ref[outer, :]
-    pack_coefficients(half, coef, weights)
     for c in range(tiles):
         face[pl.ds(c * tall, tall), :], face[pl.ds((tiles + c) * tall, tall), :] = faces(zm, mm, wet, tile(c), width, tall)
     for q in range(planes):
         for k, ref in enumerate((east, north)):
             ref[q, BODY, :] = turn(face, [k * tiles * tall + ch * offset + q for _ in range(TILE) for ch in range(2)], tall)
     refresh(east, 0, planes)
-    lead = pl.ds(aligned((1 - half) * TILE), tall)
     ends = (tile(0), tile(tiles - 1))
     for k, ref in enumerate((zm, mm, wet)):
-        pack_coef[k, lead, :] = edge_coefficient(*(ref[:tall, cols] for cols in ends))
-    for out_strip, c, west in ((west_out, 0, True), (east_out, tiles - 1, False)):
-        out_strip[lead, :] = outgoing_coefficients([ref[:tall, tile(c)] for ref in (zm, mm, wet)], west)
+        pack_coef[k] = edge_coefficient(*(ref[:tall, cols] for cols in ends))
     large[0].wait()
     forcing[...] = forcing[...] * wet[:tall, :][None]
     large[1].wait()
 
 
 def interior_kernel(
-    gy_size, own, others, forcing, east, north, west_in, east_in,
-    out, pack_own, pack_other, weight_own, weight_other, west_out, east_out,
-    field, u, u_next, result,
+    gy_size, own, others, forcing, east, north,
+    halfway, pack_own, pack_other, weight_own, weight_other,
+    field, u, u_next,
 ):
     levels, tall, width = own.shape
     tiles = width // LANES
@@ -293,22 +283,38 @@
         return field[pl.ds((f * tiles + c) * tall, tall), :]
 
     ends = (tile(0), tile(tiles - 1))
-    lead = pl.ds(aligned((1 - half) * TILE), tall)
     for k, pack in enumerate((pack_own, pack_other)):
-        pack[lead, :] = edge_columns(*([at(2 * level + k, c) for level in range(levels)] for c in (0, tiles - 1)))
+        pack[...] = edge_columns(*([at(2 * level + k, c) for level in range(levels)] for c in (0, tiles - 1)))
     weight_own[...] = edge_columns(*([own[level, keep_own, cols] for level in range(levels)] for cols in ends))
     weight_other[...] = edge_columns(*([others[0, level, keep_other, cols] for level in range(levels)] for cols in ends))
-    for source, out_strip, c, west in ((west_in, west_out, 0, True), (east_in, east_out, tiles - 1, False)):
-        columns = [[at(2 * level + k, c) for level in range(levels)] for k in range(2)]
-        out_strip[lead, :] = outgoing(columns, source[lead, :], west)
-
     fields = range(2 * levels)
     for q in range(planes):
         u[q, BODY, :] = turn(field, [f * tiles * tall + ch * offset + q for f in fields for ch in range(2)], tall)
-    source, target = u, u_next
-    for step in range(STEPS):
-        sweep(source, target, east, north, step + 1, planes - 2 - step)
-        source, target = target, source
+    buffers = [u, u_next, halfway]
+    for step in range(FIRST_STEPS):
+        count = planes - 2 - 2 * step
+        refresh(buffers[step], step + 1, count)
+        sweep(buffers[step], buffers[step + 1], east, north, step + 1, step + count)
+    refresh(halfway, FIRST_STEPS + 1, planes - 2 - 2 * FIRST_STEPS)
+
+
+def interior_rest_kernel(gy_size, halfway, own, others, east, north, out, u, u_next, result):
+    levels, tall, width = own.shape
+    tiles = width // LANES
+    mid = tall - TILE
+    planes = east.shape[0]
+    offset = tall - planes
+    half = half_of(gy_size)
+    keep_own, keep_other = pl.ds(aligned(half * TILE), mid), pl.ds(aligned(half * mid), mid)
+    fields = range(2 * levels)
+    source = halfway
+    for step in range(FIRST_STEPS, STEPS):
+        count = planes - 2 - 2 * step
+        if step > FIRST_STEPS:
+            refresh(source, step + 1, count)
+        target = u if step % 2 == 0 else u_next
+        sweep(source, target, east, north, step + 1, step + count)
+        source = target
     for q in range(STEPS, planes - STEPS):
         flat = source[q, BODY, :].T
         for f in fields:
@@ -323,28 +329,27 @@
             out[level, :, tile(c)] = own[level, keep_own, tile(c)] * a + others[0, level, keep_other, tile(c)] * b
 
 
-def halo_columns_kernel(gy_size, strip, west_in, east_in, west_out, east_out):
-    levels = strip.shape[0] - 1
-    width = strip.shape[2]
-    half = half_of(gy_size)
-    full = west_out.shape[0]
-    halo = pl.ds(aligned(half * (full - TILE)), TILE)
-    main = pl.ds(aligned((1 - half) * TILE), full - TILE)
-    for source, out, cols, west in (
-        (west_in, west_out, slice(0, LANES), True),
-        (east_in, east_out, slice(width - LANES, width), False),
-    ):
-        out[main, :] = source[main, :]
-        out[halo, :] = outgoing(
-            [[received(gy_size, strip, 2 * level + k, cols) for level in range(levels)] for k in range(2)],
-            outgoing_coefficients(received_coefficients(gy_size, strip, cols), west),
-            west,
-        )
+def halo_columns_kernel(
+    gy_size, corner, pack_own, pack_other, pack_coef, full_own, full_other, full_coef, west_out, east_out
+):
+    half = half_of(gy_size)
+    tall = pack_own.shape[0]
+    halo = pl.ds(aligned(half * tall), TILE)
+    main = pl.ds(aligned((1 - half) * TILE), tall)
+    local = [pack_own[...], pack_other[...]] + [pack_coef[k] for k in range(3)]
+    fields = [unfold(gy_size, corner[:TILE, :], k) for k in range(2)]
+    received = fields + unfold_weights(gy_size, corner[TILE:, :], True)
+    full = [full_own, full_other] + [full_coef.at[k] for k in range(3)]
+    for rows, values in ((main, local), (halo, received)):
+        west_out[rows, :] = outgoing(values, True)
+        east_out[rows, :] = outgoing(values, False)
+    for ref, inner, outer in zip(full, local, received):
+        ref[main, :] = inner
+        ref[halo, :] = outer
 
 
 def outer_rows_kernel(
-    gy_size, strip, own, other, forcing, coef, pack_own, pack_other, pack_coef,
-    sums, full_own, full_other, full_coef,
+    gy_size, strip, own, other, forcing, coef, sums,
     zm, mm, wet, field, face, u, u_next, east, north, result,
 ):
     levels, tall, width = own.shape
@@ -354,8 +359,7 @@
     edge = pl.ds(aligned((1 - half) * TILE), TILE)
     halo = pl.ds(aligned(half * TILE), TILE)
     block = 2 * TILE
-    every = slice(0, width)
-    for k, (ref, value) in enumerate(zip((zm, mm, wet), received_coefficients(gy_size, strip, every))):
+    for k, (ref, value) in enumerate(zip((zm, mm, wet), unfold_weights(gy_size, strip[levels], False))):
         ref[edge, :] = coef[k]
         ref[halo, :] = value
     wet[block:, :] = jnp.zeros((TILE, width), F32)
@@ -366,7 +370,7 @@
             for k, member in enumerate((own[level, outer, cols], other[level, :, cols])):
                 base = ((2 * level + k) * tiles + c) * block
                 field[pl.ds(aligned(base + (1 - half) * TILE), TILE), :] = member * forcing[level, outer, cols]
-                field[pl.ds(aligned(base + half * TILE), TILE), :] = received(gy_size, strip, 2 * level + k, cols)
+                field[pl.ds(aligned(base + half * TILE), TILE), :] = unfold(gy_size, strip[level, :, cols], k)
 
     fields = range(2 * levels)
     planes = 10
@@ -378,7 +382,9 @@
     refresh(east, 0, planes)
     source, target = u, u_next
     for step in range(STEPS):
-        sweep(source, target, east, north, step + 1, planes - 2 - step)
+        count = planes - 2 - 2 * step
+        refresh(source, step + 1, count)
+        sweep(source, target, east, north, step + 1, step + count)
         source, target = target, source
     for p in range(2):
         flat = source[STEPS + p, BODY, :].T
@@ -397,19 +403,6 @@
             sums[pl.ds((c * levels // 2 + pair) * TILE, TILE), :] = jnp.where(
                 natural, terms[2 * pair], pltpu.roll(terms[2 * pair + 1], 4, 0)
             )
-
-    full = full_own.shape[0]
-    main = pl.ds(aligned((1 - half) * TILE), full - TILE)
-    outside = pl.ds(aligned(half * (full - TILE)), TILE)
-    ends = (slice(0, LANES), slice(width - LANES, width))
-    for k, (source, out) in enumerate(((pack_own, full_own), (pack_other, full_other))):
-        out[main, :] = source[main, :]
-        out[outside, :] = edge_columns(
-            *([received(gy_size, strip, 2 * level + k, cols) for level in range(levels)] for cols in ends)
-        )
-    for k, (first, last) in enumerate(zip(*(received_coefficients(gy_size, strip, cols) for cols in ends))):
-        full_coef[k, main, :] = pack_coef[k, main, :]
-        full_coef[k, outside, :] = edge_coefficient(first, last)
 
 
 def end_columns_kernel(
@@ -540,12 +533,12 @@
     others = swap(members)
     end = kept(full, LANES)
     turned = kept(planes, DEPTH, LANES)
-    own, forcing, coef, weights, face_east, face_north, pack_coef, west, east = call(
+    own, forcing, coef, face_east, face_north, pack_coef = call(
         load_kernel,
         [in_hbm(x) for x in (members, increment, zonal_diff, merid_diff, sea_mask)],
         [HBM] * 5,
         [kept(levels, tall, width)] * 2
-        + [kept(3, TILE, width), kept(TILE, width), turned, turned, kept(3, full, LANES), end, end],
+        + [kept(3, TILE, width), turned, turned, kept(3, tall, LANES)],
         [
             pltpu.VMEM((tall, width), jnp.int32),
             scratch(tall, width),
@@ -555,33 +548,46 @@
             pltpu.SemaphoreType.DMA((5,)),
         ],
     )
-    strip, other = held(
-        pack_rows_kernel,
+    weights = held(pack_coefficients_kernel, [coef], kept(TILE, width))
+    other, corner = held(
+        pack_corner_kernel,
         [own, others, forcing, weights],
-        [kept(levels + 1, TILE, width), kept(levels, TILE, width)],
-    )
-    forcing, strip = lax.optimization_barrier((forcing, strip))
-    strip = across(strip)
-
-    inside, pack_own, pack_other, weight_own, weight_other, west, east = held(
+        [kept(levels, TILE, width), kept(2 * TILE, LANES)],
+    )
+    forcing, corner = lax.optimization_barrier((forcing, corner))
+    corner = across(corner)
+    packed = kept(tall, LANES)
+    halfway, pack_own, pack_other, weight_own, weight_other = held(
         interior_kernel,
-        [own, others, forcing, face_east, face_north, west, east],
-        [kept(levels, mid, width), end, end, kept(mid, LANES), kept(mid, LANES), end, end],
+        [own, others, forcing, face_east, face_north],
+        [turned, packed, packed, kept(mid, LANES), kept(mid, LANES)],
+        [scratch(2 * levels * tiles * tall, LANES), scratch(planes, DEPTH, LANES), scratch(planes, DEPTH, LANES)],
+    )
+    halfway, weights, corner = lax.optimization_barrier((halfway, weights, corner))
+    strip = across(held(pack_rows_kernel, [own, other, forcing, weights], kept(levels + 1, TILE, width)))
+    full_own, full_other, full_coef, west, east = held(
+        halo_columns_kernel,
+        [corner, pack_own, pack_other, pack_coef],
+        [end, end, kept(3, full, LANES), end, end],
+    )
+    halfway, west, east = lax.optimization_barrier((halfway, west, east))
+    from_west = along(east, 1)
+    from_east = along(west, -1)
+    inside = held(
+        interior_rest_kernel,
+        [halfway, own, others, face_east, face_north],
+        kept(levels, mid, width),
         [
-            scratch(2 * levels * tiles * tall, LANES),
             scratch(planes, DEPTH, LANES),
             scratch(planes, DEPTH, LANES),
             scratch(2 * levels * tiles * tall, LANES),
         ],
     )
-    west, east = held(halo_columns_kernel, [strip, west, east], [end, end])
-    inside, west, east = lax.optimization_barrier((inside, west, east))
-    from_west = along(east, 1)
-    from_east = along(west, -1)
-    sums, full_own, full_other, full_coef = held(
+    inside, forcing = lax.optimization_barrier((inside, forcing))
+    sums = held(
         outer_rows_kernel,
-        [strip, own, other, forcing, coef, pack_own, pack_other, pack_coef],
-        [kept(levels // 2 * tiles * TILE, LANES), end, end, kept(3, full, LANES)],
+        [strip, own, other, forcing, coef],
+        kept(levels // 2 * tiles * TILE, LANES),
         [
             scratch(2 * TILE, width),
             scratch(2 * TILE, width),
@@ -595,6 +601,7 @@
             scratch(2 * levels * tiles * TILE, LANES),
         ],
     )
+    inside, sums, from_west, from_east = lax.optimization_barrier((inside, sums, from_west, from_east))
     edges = held(
         end_columns_kernel,
         [from_west, from_east, full_own, full_other, full_coef, weight_own, weight_other, sums],

time: 20.1 us -> 20 us (level)
  waiting for transfers between devices: 2.1 us -> 0.94 us
  starting transfers between devices: 8.67 us -> 9.54 us
    ppermute x1 -> x2, starting transfers between devices: 2.96 us -> 4.58 us  [across(): return lax.ppermute(x, AXES, pairs)]
    ppermute x2, waiting for transfers between devices: 0.49 us -> 0.01 us  [along(): return lax.ppermute(x, 'gx', [(i, (i + shift) % n_gx) for i in range(n_gx)])]
    ppermute x2, starting transfers between devices: 4.28 us -> 3.88 us  [along(): return lax.ppermute(x, 'gx', [(i, (i + shift) % n_gx) for i in range(n_gx)])]
    ppermute x3, waiting for transfers between devices: 1.27 us -> 0.93 us  [swap(): return lax.ppermute(x, 'mem', [(i, i ^ 1) for i in range(n_mem)])]
    ppermute x3, starting transfers between devices: 1.42 us -> 1.08 us  [swap(): return lax.ppermute(x, 'mem', [(i, i ^ 1) for i in range(n_mem)])]
    ppermute x1 -> x2, waiting for transfers between devices: 0.34 us -> 0.01 us  [across(): return lax.ppermute(x, AXES, pairs)]
    pallas_call x7 -> x10, Pallas kernels: 9.14 us -> 9.33 us  [call(): pl.pallas_call(functools.partial(kernel, n_gy), out_shape=outs, in_specs=...]
  transfers between devices with their start and end apart: 6 -> 7, of which waited for: 4 -> 1; matrix products, arithmetic and copies ran while one was open for 0% -> 0% of each run, Pallas kernels for 38% -> 40%
where the time goes in v4:
time: 20 us; the launch traced here: 19.9 us
  starting transfers between devices  9.54 us (48%)
  Pallas kernels  9.33 us (47%)
  waiting for transfers between devices  0.94 us (5%)
    pallas_call x10, Pallas kernels, call(): pl.pallas_call(functools.partial(kernel, n_gy), out_shape=outs, in_specs=...  9.33 us
    ppermute x2, starting transfers between devices, across(): return lax.ppermute(x, AXES, pairs)  4.58 us
    ppermute x2, starting transfers between devices, along(): return lax.ppermute(x, 'gx', [(i, (i + shift) % n_gx) for i in range(n_gx)])  3.88 us
    ppermute x3, starting transfers between devices, swap(): return lax.ppermute(x, 'mem', [(i, i ^ 1) for i in range(n_mem)])  1.08 us
    ppermute x3, waiting for transfers between devices, swap(): return lax.ppermute(x, 'mem', [(i, i ^ 1) for i in range(n_mem)])  0.93 us
  transfers between devices with their start and end apart: 7, of which 1 were waited for; matrix products, arithmetic and copies ran while one was open for 0% of the time, Pallas kernels for 40%

profile of v4, /device:TPU:0, one launch (start us, length us, event | category | flops | bytes accessed | tf_op | source)
XLA Modules:
  0.0 19.9 jit_solution(14321278680307147786)
XLA Ops:
  0.0 0.5 %collective-permute-start = (f32[1,4,64,1024]{3,2,1,0:T(8,128)}, f32[1,4,64,1024]{3,2,1,0:T(8,128)S(1)}, u32[]{:S(2)}, u32[]{:S(2)}) collective-permute-start(f32[1,4,64,1024]{3,2,1,0:T(8,128)} %members.1), channel_id=1, source_target_pairs={{0,16},{16,0},{1,17},{17,1},{2,18},{18,2},{3,19},{19,3},{4,20},{20... | collective-permute-start | bytes 3145736 | tf_op jit(solution)/shard_map/ppermute | solution.py:508
  0.5 2.4 %shard_map.55 = (f32[4,40,1024]{2,1,0:T(8,128)S(1)}, f32[4,40,1024]{2,1,0:T(8,128)S(1)}, f32[3,8,1024]{2,1,0:T(8,128)S(1)}, f32[24,144,128]{2,1,0:T(8,128)S(1)},...) custom-call(f32[1,4,64,1024]{3,2,1,0:T(8,128)} %members.1, f32[4,64,1024]{2,1,0:T(8,128)} %increment.1, ...), custom_call_target="tpu_custom_call" | custom-call | tf_op jit(solution)/shard_map/pallas_call | solution.py:493
  2.9 0.1 shard_map.56.weights
  3.0 0.0 collective-permute-done.others
  3.0 0.2 %shard_map.57 = (f32[4,8,1024]{2,1,0:T(8,128)S(1)}, f32[16,128]{1,0:T(8,128)S(1)}) custom-call(f32[4,40,1024]{2,1,0:T(8,128)S(1)} %get-tuple-element.38.own, f32[1,4,64,1024]{3,2,1,0:T(8,128)S(1)} %collective-permute-done.others, f32[4,40,1024]{2,1,0:T(8,128)S(1)} %get-tuple-element.58.forcing, f32[8,1024]{1,0:T(8,128)S(1)} %shard_map.56.weights), custom_call_target="tpu_custom_call" | custom-call | tf_op jit(solution)/shard_map/pallas_call | solution.py:493
  3.2 2.9 %collective-permute-start.1 = (f32[16,128]{1,0:T(8,128)S(1)}, f32[16,128]{1,0:T(8,128)S(1)}, u32[]{:S(2)}, u32[]{:S(2)}) collective-permute-start(f32[16,128]{1,0:T(8,128)S(1)} %get-tuple-element.46), channel_id=1, source_target_pairs={{16,4},{4,16},{17,5},{5,17},{18,6},{6,18},{19,7},{7,19},{20,24},{2... | collective-permute-start | bytes 24584 | tf_op jit(solution)/shard_map/ppermute | solution.py:528
  6.1 2.0 %shard_map.58 = (f32[24,144,128]{2,1,0:T(8,128)S(1)}, f32[40,128]{1,0:T(8,128)S(1)}, f32[40,128]{1,0:T(8,128)S(1)}, f32[32,128]{1,0:T(8,128)S(1)}, f32[32,128]{1,0:T(8,128)S(1)}) custom-call(f32[4,40,1024]{2,1,0:T(8,128)S(1)} %get-tuple-element.38.own, f32[1,4,64,1024]{3,2,1,0:T(8,128)S(1)} %collective-permute-done.others, ...), custom_call_target="tpu_custom_call" | custom-call | tf_op jit(solution)/shard_map/pallas_call | solution.py:493
  8.2 0.0 collective-permute-done.1.corner
  8.2 0.1 shard_map.61
  8.2 1.6 %collective-permute-start.2 = (f32[5,8,1024]{2,1,0:T(8,128)S(1)}, f32[5,8,1024]{2,1,0:T(8,128)S(1)}, u32[]{:S(2)}, u32[]{:S(2)}) collective-permute-start(f32[5,8,1024]{2,1,0:T(8,128)S(1)} %shard_map.61), channel_id=1, source_target_pairs={{16,4},{4,16},{17,5},{5,17},{18,6},{6,18},{19,7},{7,19},{20,24},{2... | collective-permute-start | bytes 491528 | tf_op jit(solution)/shard_map/ppermute | solution.py:528
  9.9 0.1 shard_map.59
  10.0 0.5 %collective-permute-start.3 = (f32[48,128]{1,0:T(8,128)S(1)}, f32[48,128]{1,0:T(8,128)S(1)}, u32[]{:S(2)}, u32[]{:S(2)}) collective-permute-start(f32[48,128]{1,0:T(8,128)S(1)} %get-tuple-element.59), channel_id=1, source_target_pairs={{0,1},{1,2},{2,3},{3,0},{4,5},{5,6},{6,7},{7,4},{8,9},{9,10},{10,1... | collective-permute-start | bytes 73736 | tf_op jit(solution)/shard_map/ppermute | solution.py:511
  10.5 3.4 %collective-permute-start.4 = (f32[48,128]{1,0:T(8,128)S(1)}, f32[48,128]{1,0:T(8,128)S(1)}, u32[]{:S(2)}, u32[]{:S(2)}) collective-permute-start(f32[48,128]{1,0:T(8,128)S(1)} %get-tuple-element.60), channel_id=1, source_target_pairs={{0,3},{1,0},{2,1},{3,2},{4,7},{5,4},{6,5},{7,6},{8,11},{9,8},{10,9... | collective-permute-start | bytes 73736 | tf_op jit(solution)/shard_map/ppermute | solution.py:511
  13.9 1.3 %shard_map.60.mine_in = f32[4,32,1024]{2,1,0:T(8,128)S(1)} custom-call(f32[24,144,128]{2,1,0:T(8,128)S(1)} %get-tuple-element.54.halfway, f32[4,40,1024]{2,1,0:T(8,128)S(1)} %get-tuple-element.38.own, f32[1,4,64,1024]{3,2,1,0:T(8,128)S(1)} %collective-permute-done.others, f32[24,144,128]{2,1,0:T(8,128)S(1)} %get-tuple-element.43.east, ...), custom_call_target="tpu_custom_call" | custom-call | tf_op jit(solution)/shard_map/pallas_call | solution.py:493
  15.2 0.0 collective-permute-done.2.strip
  15.2 1.3 %shard_map.62.sums = f32[128,128]{1,0:T(8,128)S(1)} custom-call(f32[5,8,1024]{2,1,0:T(8,128)S(1)} %collective-permute-done.2.strip, f32[4,40,1024]{2,1,0:T(8,128)S(1)} %get-tuple-element.38.own, f32[4,8,1024]{2,1,0:T(8,128)S(1)} %get-tuple-element.56.other, f32[4,40,1024]{2,1,0:T(8,128)S(1)} %get-tuple-element.58.forcing, ...), custom_call_target="tpu_custom_call" | custom-call | tf_op jit(solution)/shard_map/pallas_call | solution.py:493
  16.5 0.0 collective-permute-done.3.from_west
  16.6 0.0 collective-permute-done.4.from_east
  16.6 0.1 collective-permute-start.5
  16.6 0.7 %shard_map.63.mine_edge = f32[160,128]{1,0:T(8,128)S(1)} custom-call(f32[48,128]{1,0:T(8,128)S(1)} %collective-permute-done.3.from_west, f32[48,128]{1,0:T(8,128)S(1)} %collective-permute-done.4.from_east, f32[48,128]{1,0:T(8,128)S(1)} %get-tuple-element.64.own, f32[48,128]{1,0:T(8,128)S(1)} %get-tuple-element.65.other, ...), custom_call_target="tpu_custom_call" | custom-call | tf_op jit(solution)/shard_map/pallas_call | solution.py:493
  17.3 0.6 %collective-permute-start.6 = (f32[160,128]{1,0:T(8,128)S(1)}, f32[160,128]{1,0:T(8,128)S(1)}, u32[]{:S(2)}, u32[]{:S(2)}) collective-permute-start(f32[160,128]{1,0:T(8,128)S(1)} %shard_map.63.mine_edge), channel_id=1, source_target_pairs={{0,16},{16,0},{1,17},{17,1},{2,18},{18,2},{3,19},{19,3},{4,20},{20... | collective-permute-start | bytes 245768 | tf_op jit(solution)/shard_map/ppermute | solution.py:508
  17.9 0.9 %collective-permute-done.6.theirs_edge = f32[160,128]{1,0:T(8,128)S(1)} collective-permute-done((f32[160,128]{1,0:T(8,128)S(1)}, f32[160,128]{1,0:T(8,128)S(1)}, u32[]{:S(2)}, u32[]{:S(2)}) %collective-permute-start.6) | collective-permute-done | bytes 81952 | tf_op jit(solution)/shard_map/ppermute | solution.py:508
  18.8 0.0 collective-permute-done.5.theirs_in
  18.8 1.1 %shard_map.64 = (f32[4,32,1024]{2,1,0:T(8,128)S(1)}, f32[4,32,1024]{2,1,0:T(8,128)S(1)}, f32[4,64,1024]{2,1,0:T(8,128)}) custom-call(f32[4,32,1024]{2,1,0:T(8,128)S(1)} %shard_map.60.mine_in, f32[4,32,1024]{2,1,0:T(8,128)S(1)} %collective-permute-done.5.theirs_in, f32[160,128]{1,0:T(8,128)S(1)} %shard_map.63.mine_edge, ...), custom_call_target="tpu_custom_call", output_to_operand_aliasing={{0}: (0, {}), {1}: (1, {})} | custom-call | tf_op jit(solution)/shard_map/pallas_call | solution.py:493
Async XLA Ops:
  0.0 3.0 %collective-permute-start = (f32[1,4,64,1024]{3,2,1,0:T(8,128)}, f32[1,4,64,1024]{3,2,1,0:T(8,128)S(1)}, u32[]{:S(2)}, u32[]{:S(2)}) collective-permute-start(f32[1,4,64,1024]{3,2,1,0:T(8,128)} %members.1), channel_id=1, source_target_pairs={{0,16},{16,0},{1,17},{17,1},{2,18},{18,2},{3,19},{19,3},{4,20},{20... | collective-permute-start | bytes 3145736 | tf_op jit(solution)/shard_map/ppermute | solution.py:508
  3.2 5.0 %collective-permute-start.1 = (f32[16,128]{1,0:T(8,128)S(1)}, f32[16,128]{1,0:T(8,128)S(1)}, u32[]{:S(2)}, u32[]{:S(2)}) collective-permute-start(f32[16,128]{1,0:T(8,128)S(1)} %get-tuple-element.46), channel_id=1, source_target_pairs={{16,4},{4,16},{17,5},{5,17},{18,6},{6,18},{19,7},{7,19},{20,24},{2... | collective-permute-start | bytes 24584 | tf_op jit(solution)/shard_map/ppermute | solution.py:528
  8.2 7.0 %collective-permute-start.2 = (f32[5,8,1024]{2,1,0:T(8,128)S(1)}, f32[5,8,1024]{2,1,0:T(8,128)S(1)}, u32[]{:S(2)}, u32[]{:S(2)}) collective-permute-start(f32[5,8,1024]{2,1,0:T(8,128)S(1)} %shard_map.61), channel_id=1, source_target_pairs={{16,4},{4,16},{17,5},{5,17},{18,6},{6,18},{19,7},{7,19},{20,24},{2... | collective-permute-start | bytes 491528 | tf_op jit(solution)/shard_map/ppermute | solution.py:528
  10.0 6.5 %collective-permute-start.3 = (f32[48,128]{1,0:T(8,128)S(1)}, f32[48,128]{1,0:T(8,128)S(1)}, u32[]{:S(2)}, u32[]{:S(2)}) collective-permute-start(f32[48,128]{1,0:T(8,128)S(1)} %get-tuple-element.59), channel_id=1, source_target_pairs={{0,1},{1,2},{2,3},{3,0},{4,5},{5,6},{6,7},{7,4},{8,9},{9,10},{10,1... | collective-permute-start | bytes 73736 | tf_op jit(solution)/shard_map/ppermute | solution.py:511
  10.5 6.0 %collective-permute-start.4 = (f32[48,128]{1,0:T(8,128)S(1)}, f32[48,128]{1,0:T(8,128)S(1)}, u32[]{:S(2)}, u32[]{:S(2)}) collective-permute-start(f32[48,128]{1,0:T(8,128)S(1)} %get-tuple-element.60), channel_id=1, source_target_pairs={{0,3},{1,0},{2,1},{3,2},{4,7},{5,4},{6,5},{7,6},{8,11},{9,8},{10,9... | collective-permute-start | bytes 73736 | tf_op jit(solution)/shard_map/ppermute | solution.py:511
  16.6 2.2 %collective-permute-start.5 = (f32[4,32,1024]{2,1,0:T(8,128)S(1)}, f32[4,32,1024]{2,1,0:T(8,128)S(1)}, u32[]{:S(2)}, u32[]{:S(2)}) collective-permute-start(f32[4,32,1024]{2,1,0:T(8,128)S(1)} %shard_map.60.mine_in), channel_id=1, source_target_pairs={{0,16},{16,0},{1,17},{17,1},{2,18},{18,2},{3,19},{19,3},{4,20},{20... | collective-permute-start | bytes 1572872 | tf_op jit(solution)/shard_map/ppermute | solution.py:508
  17.3 1.5 %collective-permute-start.6 = (f32[160,128]{1,0:T(8,128)S(1)}, f32[160,128]{1,0:T(8,128)S(1)}, u32[]{:S(2)}, u32[]{:S(2)}) collective-permute-start(f32[160,128]{1,0:T(8,128)S(1)} %shard_map.63.mine_edge), channel_id=1, source_target_pairs={{0,16},{16,0},{1,17},{17,1},{2,18},{18,2},{3,19},{19,3},{4,20},{20... | collective-permute-start | bytes 245768 | tf_op jit(solution)/shard_map/ppermute | solution.py:508

commit v5 on v4

--- a/solution.py
+++ b/solution.py
@@ -61,7 +61,7 @@
         copy.wait()
 
 
-def pack_coefficients_kernel(gy_size, coef, out):
+def own_ends_kernel(gy_size, own, forcing, coef, out, ends, pack_own, weight_own):
     half = half_of(gy_size)
     width = out.shape[1]
     zm, mm, wet = coef[0], coef[1], coef[2]
@@ -80,6 +80,12 @@
         moved = jnp.where(half == 0, pltpu.roll(first, 7 - r, 0), pltpu.roll(first, (-r) % TILE, 0))
         value = jnp.where((line == jnp.where(half == 0, 7, 4)) & (lane == r), pltpu.roll(moved, r, 1), value)
     out[:, :LANES] = value
+    both = (tile(0), slice(width - LANES, width))
+    ends[...] = edge_coefficient(*(out[:, cols] for cols in both))
+    levels, tall, _ = own.shape
+    pack_own[...] = edge_columns(*([own[l, :, cols] * forcing[l, :, cols] for l in range(levels)] for cols in both))
+    keep = pl.ds(aligned(half * TILE), tall - TILE)
+    weight_own[...] = edge_columns(*([own[l, keep, cols] for l in range(levels)] for cols in both))
 
 
 def outer_rows_of(gy_size, level, own, other, forcing, cols):
@@ -96,21 +102,25 @@
     return jnp.where(row_ids(*first.shape) < TILE // 2, first, second)
 
 
-def pack_corner_kernel(gy_size, own, others, forcing, weights, other, corner):
+def pack_rows_kernel(gy_size, own, others, forcing, weights, coef_ends, other, strip):
     levels, _, width = own.shape
+    tiles = width // LANES
     other[...] = others[0, :, pl.ds(aligned(half_of(gy_size) * (others.shape[2] - TILE)), TILE), :]
-    ends = (tile(0), slice(width - LANES, width))
-    corner[:TILE, :] = edge_columns(
-        *([outer_rows_of(gy_size, level, own, other, forcing, cols) for level in range(levels)] for cols in ends)
-    )
-    corner[TILE:, :] = edge_coefficient(*(weights[:, cols] for cols in ends))
-
-
-def pack_rows_kernel(gy_size, own, other, forcing, weights, strip):
-    levels, _, width = own.shape
-    for level in range(levels):
-        strip[level] = outer_rows_of(gy_size, level, own, other, forcing, slice(0, width))
-    strip[levels] = weights[...]
+    ends = ([], [])
+    for c in range(tiles):
+        for level in range(levels):
+            rows = outer_rows_of(gy_size, level, own, other, forcing, tile(c))
+            strip[strip_rows(level, c, tiles), :] = rows
+            if c in (0, tiles - 1):
+                ends[c > 0].append(rows)
+        strip[strip_rows(levels, c, tiles), :] = weights[:, tile(c)]
+    last = (levels + 1) * tiles * TILE
+    strip[last : last + TILE, :] = edge_columns(*ends)
+    strip[last + TILE :, :] = coef_ends[...]
+
+
+def strip_rows(place, c, tiles):
+    return slice((place * tiles + c) * TILE, (place * tiles + c + 1) * TILE)
 
 
 def inside_domain(gy_size):
@@ -261,7 +271,7 @@
 
 def interior_kernel(
     gy_size, own, others, forcing, east, north,
-    halfway, pack_own, pack_other, weight_own, weight_other,
+    halfway, pack_other, weight_other,
     field, u, u_next,
 ):
     levels, tall, width = own.shape
@@ -271,7 +281,7 @@
     offset = tall - planes
     half = half_of(gy_size)
     part = pl.ds(aligned(half * (mid - TILE)), tall)
-    keep_own, keep_other = pl.ds(aligned(half * TILE), mid), pl.ds(aligned(half * mid), mid)
+    keep_other = pl.ds(aligned(half * mid), mid)
     for c in range(tiles):
         cols = tile(c)
         for level in range(levels):
@@ -283,14 +293,12 @@
         return field[pl.ds((f * tiles + c) * tall, tall), :]
 
     ends = (tile(0), tile(tiles - 1))
-    for k, pack in enumerate((pack_own, pack_other)):
-        pack[...] = edge_columns(*([at(2 * level + k, c) for level in range(levels)] for c in (0, tiles - 1)))
-    weight_own[...] = edge_columns(*([own[level, keep_own, cols] for level in range(levels)] for cols in ends))
+    pack_other[...] = edge_columns(*([at(2 * level + 1, c) for level in range(levels)] for c in (0, tiles - 1)))
     weight_other[...] = edge_columns(*([others[0, level, keep_other, cols] for level in range(levels)] for cols in ends))
     fields = range(2 * levels)
     for q in range(planes):
         u[q, BODY, :] = turn(field, [f * tiles * tall + ch * offset + q for f in fields for ch in range(2)], tall)
-    buffers = [u, u_next, halfway]
+    buffers = [u, u_next, u][:FIRST_STEPS] + [halfway]
     for step in range(FIRST_STEPS):
         count = planes - 2 - 2 * step
         refresh(buffers[step], step + 1, count)
@@ -330,15 +338,16 @@
 
 
 def halo_columns_kernel(
-    gy_size, corner, pack_own, pack_other, pack_coef, full_own, full_other, full_coef, west_out, east_out
+    gy_size, strip, pack_own, pack_other, pack_coef, full_own, full_other, full_coef, west_out, east_out
 ):
     half = half_of(gy_size)
     tall = pack_own.shape[0]
     halo = pl.ds(aligned(half * tall), TILE)
     main = pl.ds(aligned((1 - half) * TILE), tall)
     local = [pack_own[...], pack_other[...]] + [pack_coef[k] for k in range(3)]
-    fields = [unfold(gy_size, corner[:TILE, :], k) for k in range(2)]
-    received = fields + unfold_weights(gy_size, corner[TILE:, :], True)
+    corner = strip.shape[0] - 2 * TILE
+    fields = [unfold(gy_size, strip[corner : corner + TILE, :], k) for k in range(2)]
+    received = fields + unfold_weights(gy_size, strip[corner + TILE :, :], True)
     full = [full_own, full_other] + [full_coef.at[k] for k in range(3)]
     for rows, values in ((main, local), (halo, received)):
         west_out[rows, :] = outgoing(values, True)
@@ -349,7 +358,7 @@
 
 
 def outer_rows_kernel(
-    gy_size, strip, own, other, forcing, coef, sums,
+    gy_size, inside, strip, own, other, forcing, coef, sums,
     zm, mm, wet, field, face, u, u_next, east, north, result,
 ):
     levels, tall, width = own.shape
@@ -359,9 +368,12 @@
     edge = pl.ds(aligned((1 - half) * TILE), TILE)
     halo = pl.ds(aligned(half * TILE), TILE)
     block = 2 * TILE
-    for k, (ref, value) in enumerate(zip((zm, mm, wet), unfold_weights(gy_size, strip[levels], False))):
+    for k, ref in enumerate((zm, mm, wet)):
         ref[edge, :] = coef[k]
-        ref[halo, :] = value
+    for c in range(tiles):
+        values = unfold_weights(gy_size, strip[strip_rows(levels, c, tiles), :], False)
+        for ref, value in zip((zm, mm, wet), values):
+            ref[halo, tile(c)] = value
     wet[block:, :] = jnp.zeros((TILE, width), F32)
     for c in range(tiles):
         cols = tile(c)
@@ -370,7 +382,7 @@
             for k, member in enumerate((own[level, outer, cols], other[level, :, cols])):
                 base = ((2 * level + k) * tiles + c) * block
                 field[pl.ds(aligned(base + (1 - half) * TILE), TILE), :] = member * forcing[level, outer, cols]
-                field[pl.ds(aligned(base + half * TILE), TILE), :] = unfold(gy_size, strip[level, :, cols], k)
+                field[pl.ds(aligned(base + half * TILE), TILE), :] = unfold(gy_size, strip[strip_rows(level, c, tiles), :], k)
 
     fields = range(2 * levels)
     planes = 10
@@ -378,6 +390,8 @@
     for q in range(planes):
         u[q, BODY, :] = turn(field, [f * tiles * block + 2 * ch + q + lead for f in fields for ch in range(2)], block)
         for k, ref in enumerate((east, north)):
+            if q == planes - 1 or (k == 0 and q == 0):
+                continue
             ref[q, BODY, :] = turn(face, [k * tiles * block + 2 * ch + q + lead for f in fields for ch in range(2)], block)
     refresh(east, 0, planes)
     source, target = u, u_next
@@ -392,21 +406,18 @@
             for ch in range(2):
                 group = (2 * f + ch) * tiles
                 result[pl.ds(f * tiles * TILE + 4 * half + 2 * ch + p, tiles, stride=TILE), :] = flat[group : group + tiles]
-    natural = row_ids(TILE, LANES) // 4 == half
+    mine = row_ids(TILE, LANES) // 4 == half
+    place = pl.ds(aligned(half * (tall - 2 * TILE)), TILE)
     for c in range(tiles):
         cols = tile(c)
-        terms = []
         for level in range(levels):
             a, b = (result[pl.ds(((2 * level + k) * tiles + c) * TILE, TILE), :] for k in range(2))
-            terms.append(own[level, outer, cols] * a + other[level, :, cols] * b)
-        for pair in range(levels // 2):
-            sums[pl.ds((c * levels // 2 + pair) * TILE, TILE), :] = jnp.where(
-                natural, terms[2 * pair], pltpu.roll(terms[2 * pair + 1], 4, 0)
-            )
+            term = own[level, outer, cols] * a + other[level, :, cols] * b
+            sums[level, place, cols] = jnp.where(mine, term, sums[level, place, cols])
 
 
 def end_columns_kernel(
-    gy_size, from_west, from_east, own, other, coef, weight_own, weight_other, sums, out,
+    gy_size, from_west, from_east, own, other, coef, weight_own, weight_other, out,
     a, b, a_next, b_next, east, north, wet,
 ):
     full = own.shape[0]
@@ -443,28 +454,19 @@
         now, later = later, now
     mid = weight_own.shape[0]
     rows = pl.ds(2 * TILE, mid)
-    out[:mid, :] = weight_own[...] * now[0][rows, :] + weight_other[...] * now[1][rows, :]
-    out[mid:, :] = sums[...]
+    out[...] = weight_own[...] * now[0][rows, :] + weight_other[...] * now[1][rows, :]
 
 
 def join_kernel(gy_size, mine_in, theirs_in, mine_edge, theirs_edge, mine, theirs, out, sems):
     half = half_of(gy_size)
     levels, mid, width = mine.shape
-    tiles = width // LANES
     lane = lane_ids(mid)
+    first, last = slice(0, LANES), slice(width - LANES, width)
     copies = []
     for k, (ref, edges, where) in enumerate(((mine, mine_edge, half), (theirs, theirs_edge, 1 - half))):
-        outer = pl.ds(aligned(where * (mid - TILE)), TILE)
-        natural = row_ids(TILE, LANES) // 4 == where
+        packed = edges[...]
         for level in range(levels):
-            for c in range(tiles):
-                value = edges[pl.ds(mid + (c * levels // 2 + level // 2) * TILE, TILE), :]
-                if level % 2:
-                    value = pltpu.roll(value, 4, 0)
-                ref[level, outer, tile(c)] = jnp.where(natural, value, ref[level, outer, tile(c)])
-            first, last = tile(0), tile(tiles - 1)
             base = GROUP * level
-            packed = edges[:mid, :]
             ref[level, :, first] = jnp.where(lane < 4, pltpu.roll(packed, (-base - 8) % LANES, 1), ref[level, :, first])
             ref[level, :, last] = jnp.where(
                 lane >= LANES - 4, pltpu.roll(packed, (LANES - 4 - base - 20) % LANES, 1), ref[level, :, last]
@@ -548,31 +550,23 @@
             pltpu.SemaphoreType.DMA((5,)),
         ],
     )
-    weights = held(pack_coefficients_kernel, [coef], kept(TILE, width))
-    other, corner = held(
-        pack_corner_kernel,
-        [own, others, forcing, weights],
-        [kept(levels, TILE, width), kept(2 * TILE, LANES)],
-    )
-    forcing, corner = lax.optimization_barrier((forcing, corner))
-    corner = across(corner)
     packed = kept(tall, LANES)
-    halfway, pack_own, pack_other, weight_own, weight_other = held(
+    weights, coef_ends, pack_own, weight_own = held(
+        own_ends_kernel, [own, forcing, coef], [kept(TILE, width), kept(TILE, LANES), packed, kept(mid, LANES)]
+    )
+    other, strip = held(
+        pack_rows_kernel,
+        [own, others, forcing, weights, coef_ends],
+        [kept(levels, TILE, width), kept((levels + 1) * tiles * TILE + 2 * TILE, LANES)],
+    )
+    forcing, strip = lax.optimization_barrier((forcing, strip))
+    strip = across(strip)
+    halfway, pack_other, weight_other = held(
         interior_kernel,
         [own, others, forcing, face_east, face_north],
-        [turned, packed, packed, kept(mid, LANES), kept(mid, LANES)],
+        [turned, packed, kept(mid, LANES)],
         [scratch(2 * levels * tiles * tall, LANES), scratch(planes, DEPTH, LANES), scratch(planes, DEPTH, LANES)],
     )
-    halfway, weights, corner = lax.optimization_barrier((halfway, weights, corner))
-    strip = across(held(pack_rows_kernel, [own, other, forcing, weights], kept(levels + 1, TILE, width)))
-    full_own, full_other, full_coef, west, east = held(
-        halo_columns_kernel,
-        [corner, pack_own, pack_other, pack_coef],
-        [end, end, kept(3, full, LANES), end, end],
-    )
-    halfway, west, east = lax.optimization_barrier((halfway, west, east))
-    from_west = along(east, 1)
-    from_east = along(west, -1)
     inside = held(
         interior_rest_kernel,
         [halfway, own, others, face_east, face_north],
@@ -583,11 +577,18 @@
             scratch(2 * levels * tiles * tall, LANES),
         ],
     )
-    inside, forcing = lax.optimization_barrier((inside, forcing))
-    sums = held(
+    inside, pack_other = lax.optimization_barrier((inside, pack_other))
+    full_own, full_other, full_coef, west, east = held(
+        halo_columns_kernel,
+        [strip, pack_own, pack_other, pack_coef],
+        [end, end, kept(3, full, LANES), end, end],
+    )
+    from_west = along(east, 1)
+    from_east = along(west, -1)
+    inside = held(
         outer_rows_kernel,
-        [strip, own, other, forcing, coef],
-        kept(levels // 2 * tiles * TILE, LANES),
+        [inside, strip, own, other, forcing, coef],
+        kept(levels, mid, width),
         [
             scratch(2 * TILE, width),
             scratch(2 * TILE, width),
@@ -600,12 +601,13 @@
             scratch(10, DEPTH, LANES),
             scratch(2 * levels * tiles * TILE, LANES),
         ],
-    )
-    inside, sums, from_west, from_east = lax.optimization_barrier((inside, sums, from_west, from_east))
+        aliases={0: 0},
+    )
+    inside, from_west, from_east = lax.optimization_barrier((inside, from_west, from_east))
     edges = held(
         end_columns_kernel,
-        [from_west, from_east, full_own, full_other, full_coef, weight_own, weight_other, sums],
-        kept(mid + levels // 2 * tiles * TILE, LANES),
+        [from_west, from_east, full_own, full_other, full_coef, weight_own, weight_other],
+        kept(mid, LANES),
         [scratch(full + 2 * TILE, LANES)] * 7,
     )
     if n_mem > 2:

time: 20 us -> 19.4 us (0.970)
  starting transfers between devices: 9.54 us -> 7.97 us
  waiting for transfers between devices: 0.94 us -> 1.88 us
    ppermute x2 -> x1, starting transfers between devices: 4.58 us -> 2.77 us  [across(): return lax.ppermute(x, AXES, pairs)]
    ppermute x2, waiting for transfers between devices: 0.01 us -> 0.98 us  [along(): return lax.ppermute(x, 'gx', [(i, (i + shift) % n_gx) for i in range(n_gx)])]
    ppermute x2, starting transfers between devices: 3.88 us -> 4.16 us  [along(): return lax.ppermute(x, 'gx', [(i, (i + shift) % n_gx) for i in range(n_gx)])]
    pallas_call x10 -> x9, Pallas kernels: 9.33 us -> 9.35 us  [call(): pl.pallas_call(functools.partial(kernel, n_gy), out_shape=outs, in_specs=...]
  transfers between devices with their start and end apart: 7 -> 6, of which waited for: 1 -> 4; matrix products, arithmetic and copies ran while one was open for 0% -> 0% of each run, Pallas kernels for 40% -> 42%
where the time goes in v5:
time: 19.4 us; the launch traced here: 19.2 us
  Pallas kernels  9.35 us (48%)
  starting transfers between devices  7.97 us (41%)
  waiting for transfers between devices  1.88 us (10%)
    pallas_call x9, Pallas kernels, call(): pl.pallas_call(functools.partial(kernel, n_gy), out_shape=outs, in_specs=...  9.35 us
    ppermute x2, starting transfers between devices, along(): return lax.ppermute(x, 'gx', [(i, (i + shift) % n_gx) for i in range(n_gx)])  4.16 us
    ppermute x1, starting transfers between devices, across(): return lax.ppermute(x, AXES, pairs)  2.77 us
    ppermute x3, starting transfers between devices, swap(): return lax.ppermute(x, 'mem', [(i, i ^ 1) for i in range(n_mem)])  1.03 us
    ppermute x2, waiting for transfers between devices, along(): return lax.ppermute(x, 'gx', [(i, (i + shift) % n_gx) for i in range(n_gx)])  0.98 us
    ppermute x3, waiting for transfers between devices, swap(): return lax.ppermute(x, 'mem', [(i, i ^ 1) for i in range(n_mem)])  0.84 us
  transfers between devices with their start and end apart: 6, of which 4 were waited for; matrix products, arithmetic and copies ran while one was open for 0% of the time, Pallas kernels for 42%

profile of v5, /device:TPU:0, one launch (start us, length us, event | category | flops | bytes accessed | tf_op | source)
XLA Modules:
  0.0 19.2 jit_solution(11323264789024887577)
XLA Ops:
  0.0 0.5 %collective-permute-start = (f32[1,4,64,1024]{3,2,1,0:T(8,128)}, f32[1,4,64,1024]{3,2,1,0:T(8,128)S(1)}, u32[]{:S(2)}, u32[]{:S(2)}) collective-permute-start(f32[1,4,64,1024]{3,2,1,0:T(8,128)} %members.1), channel_id=1, source_target_pairs={{0,16},{16,0},{1,17},{17,1},{2,18},{18,2},{3,19},{19,3},{4,20},{20... | collective-permute-start | bytes 3145736 | tf_op jit(solution)/shard_map/ppermute | solution.py:510
  0.5 2.4 %shard_map.55 = (f32[4,40,1024]{2,1,0:T(8,128)S(1)}, f32[4,40,1024]{2,1,0:T(8,128)S(1)}, f32[3,8,1024]{2,1,0:T(8,128)S(1)}, f32[24,144,128]{2,1,0:T(8,128)S(1)},...) custom-call(f32[1,4,64,1024]{3,2,1,0:T(8,128)} %members.1, f32[4,64,1024]{2,1,0:T(8,128)} %increment.1, ...), custom_call_target="tpu_custom_call" | custom-call | tf_op jit(solution)/shard_map/pallas_call | solution.py:495
  2.9 0.3 %shard_map.56 = (f32[8,1024]{1,0:T(8,128)S(1)}, f32[8,128]{1,0:T(8,128)S(1)}, f32[40,128]{1,0:T(8,128)S(1)}, f32[32,128]{1,0:T(8,128)S(1)}) custom-call(f32[4,40,1024]{2,1,0:T(8,128)S(1)} %get-tuple-element.33.own, f32[4,40,1024]{2,1,0:T(8,128)S(1)} %get-tuple-element.39.forcing, f32[3,8,1024]{2,1,0:T(8,128)S(1)} %get-tuple-element.35.coef), custom_call_target="tpu_custom_call" | custom-call | tf_op jit(solution)/shard_map/pallas_call | solution.py:495
  3.2 0.0 collective-permute-done.others
  3.2 0.1 shard_map.57
  3.3 2.8 %collective-permute-start.1 = (f32[336,128]{1,0:T(8,128)S(1)}, f32[336,128]{1,0:T(8,128)S(1)}, u32[]{:S(2)}, u32[]{:S(2)}) collective-permute-start(f32[336,128]{1,0:T(8,128)S(1)} %get-tuple-element.45), channel_id=1, source_target_pairs={{16,4},{4,16},{17,5},{5,17},{18,6},{6,18},{19,7},{7,19},{20,24},{2... | collective-permute-start | bytes 516104 | tf_op jit(solution)/shard_map/ppermute | solution.py:530
  6.1 2.0 %shard_map.58 = (f32[24,144,128]{2,1,0:T(8,128)S(1)}, f32[40,128]{1,0:T(8,128)S(1)}, f32[32,128]{1,0:T(8,128)S(1)}) custom-call(f32[4,40,1024]{2,1,0:T(8,128)S(1)} %get-tuple-element.33.own, f32[1,4,64,1024]{3,2,1,0:T(8,128)S(1)} %collective-permute-done.others, f32[4,40,1024]{2,1,0:T(8,128)S(1)} %get-tuple-element.39.forcing, ...), custom_call_target="tpu_custom_call" | custom-call | tf_op jit(solution)/shard_map/pallas_call | solution.py:495
  8.1 1.3 %shard_map.59.inside = f32[4,32,1024]{2,1,0:T(8,128)S(1)} custom-call(f32[24,144,128]{2,1,0:T(8,128)S(1)} %get-tuple-element.42.halfway, f32[4,40,1024]{2,1,0:T(8,128)S(1)} %get-tuple-element.33.own, f32[1,4,64,1024]{3,2,1,0:T(8,128)S(1)} %collective-permute-done.others, f32[24,144,128]{2,1,0:T(8,128)S(1)} %get-tuple-element.40.east, ...), custom_call_target="tpu_custom_call" | custom-call | tf_op jit(solution)/shard_map/pallas_call | solution.py:495
  9.4 0.1 collective-permute-done.1.strip
  9.5 0.1 shard_map.61
  9.6 2.1 %collective-permute-start.2 = (f32[48,128]{1,0:T(8,128)S(1)}, f32[48,128]{1,0:T(8,128)S(1)}, u32[]{:S(2)}, u32[]{:S(2)}) collective-permute-start(f32[48,128]{1,0:T(8,128)S(1)} %get-tuple-element.50), channel_id=1, source_target_pairs={{0,1},{1,2},{2,3},{3,0},{4,5},{5,6},{6,7},{7,4},{8,9},{9,10},{10,1... | collective-permute-start | bytes 73736 | tf_op jit(solution)/shard_map/ppermute | solution.py:513
  11.7 2.1 %collective-permute-start.3 = (f32[48,128]{1,0:T(8,128)S(1)}, f32[48,128]{1,0:T(8,128)S(1)}, u32[]{:S(2)}, u32[]{:S(2)}) collective-permute-start(f32[48,128]{1,0:T(8,128)S(1)} %get-tuple-element.51), channel_id=1, source_target_pairs={{0,3},{1,0},{2,1},{3,2},{4,7},{5,4},{6,5},{7,6},{8,11},{9,8},{10,9... | collective-permute-start | bytes 73736 | tf_op jit(solution)/shard_map/ppermute | solution.py:513
  13.8 1.3 %shard_map.60.mine_in = f32[4,32,1024]{2,1,0:T(8,128)S(1)} custom-call(f32[4,32,1024]{2,1,0:T(8,128)S(1)} %shard_map.59.inside, f32[336,128]{1,0:T(8,128)S(1)} %collective-permute-done.1.strip, f32[4,40,1024]{2,1,0:T(8,128)S(1)} %get-tuple-element.33.own, f32[4,8,1024]{2,1,0:T(8,128)S(1)} %get-tuple-element.46.other, ...), custom_call_target="tpu_custom_call", output_to_operand_aliasing={{}: (0, {})} | custom-call | tf_op jit(solution)/shard_map/pallas_call | solution.py:495
  15.1 0.5 %collective-permute-done.2.from_west = f32[48,128]{1,0:T(8,128)S(1)} collective-permute-done((f32[48,128]{1,0:T(8,128)S(1)}, f32[48,128]{1,0:T(8,128)S(1)}, u32[]{:S(2)}, u32[]{:S(2)}) %collective-permute-start.2) | collective-permute-done | bytes 24608 | tf_op jit(solution)/shard_map/ppermute | solution.py:513
  15.6 0.5 %collective-permute-done.3.from_east = f32[48,128]{1,0:T(8,128)S(1)} collective-permute-done((f32[48,128]{1,0:T(8,128)S(1)}, f32[48,128]{1,0:T(8,128)S(1)}, u32[]{:S(2)}, u32[]{:S(2)}) %collective-permute-start.3) | collective-permute-done | bytes 24608 | tf_op jit(solution)/shard_map/ppermute | solution.py:513
  16.1 0.2 collective-permute-start.4
  16.2 0.7 %shard_map.62.mine_edge = f32[32,128]{1,0:T(8,128)S(1)} custom-call(f32[48,128]{1,0:T(8,128)S(1)} %collective-permute-done.2.from_west, f32[48,128]{1,0:T(8,128)S(1)} %collective-permute-done.3.from_east, f32[48,128]{1,0:T(8,128)S(1)} %get-tuple-element.55.own, f32[48,128]{1,0:T(8,128)S(1)} %get-tuple-element.56.other, ...), custom_call_target="tpu_custom_call" | custom-call | tf_op jit(solution)/shard_map/pallas_call | solution.py:495
  16.9 0.4 %collective-permute-start.5 = (f32[32,128]{1,0:T(8,128)S(1)}, f32[32,128]{1,0:T(8,128)S(1)}, u32[]{:S(2)}, u32[]{:S(2)}) collective-permute-start(f32[32,128]{1,0:T(8,128)S(1)} %shard_map.62.mine_edge), channel_id=1, source_target_pairs={{0,16},{16,0},{1,17},{17,1},{2,18},{18,2},{3,19},{19,3},{4,20},{20... | collective-permute-start | bytes 49160 | tf_op jit(solution)/shard_map/ppermute | solution.py:510
  17.3 0.8 %collective-permute-done.5.theirs_edge = f32[32,128]{1,0:T(8,128)S(1)} collective-permute-done((f32[32,128]{1,0:T(8,128)S(1)}, f32[32,128]{1,0:T(8,128)S(1)}, u32[]{:S(2)}, u32[]{:S(2)}) %collective-permute-start.5) | collective-permute-done | bytes 16416 | tf_op jit(solution)/shard_map/ppermute | solution.py:510
  18.1 0.0 collective-permute-done.4.theirs_in
  18.1 1.1 %shard_map.63 = (f32[4,32,1024]{2,1,0:T(8,128)S(1)}, f32[4,32,1024]{2,1,0:T(8,128)S(1)}, f32[4,64,1024]{2,1,0:T(8,128)}) custom-call(f32[4,32,1024]{2,1,0:T(8,128)S(1)} %shard_map.60.mine_in, f32[4,32,1024]{2,1,0:T(8,128)S(1)} %collective-permute-done.4.theirs_in, f32[32,128]{1,0:T(8,128)S(1)} %shard_map.62.mine_edge, ...), custom_call_target="tpu_custom_call", output_to_operand_aliasing={{0}: (0, {}), {1}: (1, {})} | custom-call | tf_op jit(solution)/shard_map/pallas_call | solution.py:495
Async XLA Ops:
  0.0 3.2 %collective-permute-start = (f32[1,4,64,1024]{3,2,1,0:T(8,128)}, f32[1,4,64,1024]{3,2,1,0:T(8,128)S(1)}, u32[]{:S(2)}, u32[]{:S(2)}) collective-permute-start(f32[1,4,64,1024]{3,2,1,0:T(8,128)} %members.1), channel_id=1, source_target_pairs={{0,16},{16,0},{1,17},{17,1},{2,18},{18,2},{3,19},{19,3},{4,20},{20... | collective-permute-start | bytes 3145736 | tf_op jit(solution)/shard_map/ppermute | solution.py:510
  3.3 6.2 %collective-permute-start.1 = (f32[336,128]{1,0:T(8,128)S(1)}, f32[336,128]{1,0:T(8,128)S(1)}, u32[]{:S(2)}, u32[]{:S(2)}) collective-permute-start(f32[336,128]{1,0:T(8,128)S(1)} %get-tuple-element.45), channel_id=1, source_target_pairs={{16,4},{4,16},{17,5},{5,17},{18,6},{6,18},{19,7},{7,19},{20,24},{2... | collective-permute-start | bytes 516104 | tf_op jit(solution)/shard_map/ppermute | solution.py:530
  9.6 6.0 %collective-permute-start.2 = (f32[48,128]{1,0:T(8,128)S(1)}, f32[48,128]{1,0:T(8,128)S(1)}, u32[]{:S(2)}, u32[]{:S(2)}) collective-permute-start(f32[48,128]{1,0:T(8,128)S(1)} %get-tuple-element.50), channel_id=1, source_target_pairs={{0,1},{1,2},{2,3},{3,0},{4,5},{5,6},{6,7},{7,4},{8,9},{9,10},{10,1... | collective-permute-start | bytes 73736 | tf_op jit(solution)/shard_map/ppermute | solution.py:513
  11.7 4.4 %collective-permute-start.3 = (f32[48,128]{1,0:T(8,128)S(1)}, f32[48,128]{1,0:T(8,128)S(1)}, u32[]{:S(2)}, u32[]{:S(2)}) collective-permute-start(f32[48,128]{1,0:T(8,128)S(1)} %get-tuple-element.51), channel_id=1, source_target_pairs={{0,3},{1,0},{2,1},{3,2},{4,7},{5,4},{6,5},{7,6},{8,11},{9,8},{10,9... | collective-permute-start | bytes 73736 | tf_op jit(solution)/shard_map/ppermute | solution.py:513
  16.1 2.1 %collective-permute-start.4 = (f32[4,32,1024]{2,1,0:T(8,128)S(1)}, f32[4,32,1024]{2,1,0:T(8,128)S(1)}, u32[]{:S(2)}, u32[]{:S(2)}) collective-permute-start(f32[4,32,1024]{2,1,0:T(8,128)S(1)} %shard_map.60.mine_in), channel_id=1, source_target_pairs={{0,16},{16,0},{1,17},{17,1},{2,18},{18,2},{3,19},{19,3},{4,20},{20... | collective-permute-start | bytes 1572872 | tf_op jit(solution)/shard_map/ppermute | solution.py:510
  16.9 1.3 %collective-permute-start.5 = (f32[32,128]{1,0:T(8,128)S(1)}, f32[32,128]{1,0:T(8,128)S(1)}, u32[]{:S(2)}, u32[]{:S(2)}) collective-permute-start(f32[32,128]{1,0:T(8,128)S(1)} %shard_map.62.mine_edge), channel_id=1, source_target_pairs={{0,16},{16,0},{1,17},{17,1},{2,18},{18,2},{3,19},{19,3},{4,20},{20... | collective-permute-start | bytes 49160 | tf_op jit(solution)/shard_map/ppermute | solution.py:510

commit v6 on v5

--- a/solution.py
+++ b/solution.py
@@ -102,7 +102,7 @@
     return jnp.where(row_ids(*first.shape) < TILE // 2, first, second)
 
 
-def pack_rows_kernel(gy_size, own, others, forcing, weights, coef_ends, other, strip):
+def pack_rows_kernel(gy_size, own, others, forcing, weights, coef_ends, other, strip, more):
     levels, _, width = own.shape
     tiles = width // LANES
     other[...] = others[0, :, pl.ds(aligned(half_of(gy_size) * (others.shape[2] - TILE)), TILE), :]
@@ -110,13 +110,18 @@
     for c in range(tiles):
         for level in range(levels):
             rows = outer_rows_of(gy_size, level, own, other, forcing, tile(c))
-            strip[strip_rows(level, c, tiles), :] = rows
+            part, place = strip_place(level, levels, (strip, more))
+            part[strip_rows(place, c, tiles), :] = rows
             if c in (0, tiles - 1):
                 ends[c > 0].append(rows)
-        strip[strip_rows(levels, c, tiles), :] = weights[:, tile(c)]
-    last = (levels + 1) * tiles * TILE
+        strip[strip_rows(levels // 2, c, tiles), :] = weights[:, tile(c)]
+    last = (levels // 2 + 1) * tiles * TILE
     strip[last : last + TILE, :] = edge_columns(*ends)
     strip[last + TILE :, :] = coef_ends[...]
+
+
+def strip_place(level, levels, parts):
+    return parts[level // (levels // 2)], level % (levels // 2)
 
 
 def strip_rows(place, c, tiles):
@@ -358,7 +363,7 @@
 
 
 def outer_rows_kernel(
-    gy_size, inside, strip, own, other, forcing, coef, sums,
+    gy_size, inside, strip, more, own, other, forcing, coef, sums,
     zm, mm, wet, field, face, u, u_next, east, north, result,
 ):
     levels, tall, width = own.shape
@@ -371,7 +376,7 @@
     for k, ref in enumerate((zm, mm, wet)):
         ref[edge, :] = coef[k]
     for c in range(tiles):
-        values = unfold_weights(gy_size, strip[strip_rows(levels, c, tiles), :], False)
+        values = unfold_weights(gy_size, strip[strip_rows(levels // 2, c, tiles), :], False)
         for ref, value in zip((zm, mm, wet), values):
             ref[halo, tile(c)] = value
     wet[block:, :] = jnp.zeros((TILE, width), F32)
@@ -379,10 +384,11 @@
         cols = tile(c)
         face[pl.ds(c * block, block), :], face[pl.ds((tiles + c) * block, block), :] = faces(zm, mm, wet, cols, width, block)
         for level in range(levels):
+            part, where = strip_place(level, levels, (strip, more))
             for k, member in enumerate((own[level, outer, cols], other[level, :, cols])):
                 base = ((2 * level + k) * tiles + c) * block
                 field[pl.ds(aligned(base + (1 - half) * TILE), TILE), :] = member * forcing[level, outer, cols]
-                field[pl.ds(aligned(base + half * TILE), TILE), :] = unfold(gy_size, strip[strip_rows(level, c, tiles), :], k)
+                field[pl.ds(aligned(base + half * TILE), TILE), :] = unfold(gy_size, part[strip_rows(where, c, tiles), :], k)
 
     fields = range(2 * levels)
     planes = 10
@@ -461,22 +467,30 @@
     half = half_of(gy_size)
     levels, mid, width = mine.shape
     lane = lane_ids(mid)
-    first, last = slice(0, LANES), slice(width - LANES, width)
+    first, last, between = slice(0, LANES), slice(width - LANES, width), slice(LANES, width - LANES)
+    halves = ((mine, mine_edge, half), (theirs, theirs_edge, 1 - half))
     copies = []
-    for k, (ref, edges, where) in enumerate(((mine, mine_edge, half), (theirs, theirs_edge, 1 - half))):
+
+    def send(k, cols, place):
+        ref, _, where = halves[k]
+        rows = pl.ds(aligned(where * mid), mid)
+        copies.append(pltpu.make_async_copy(ref.at[:, :, cols], out.at[:, rows, cols], sems.at[k, place]))
+        copies[-1].start()
+
+    for k in range(2):
+        send(k, between, 0)
+    for k, (ref, edges, _) in enumerate(halves):
         packed = edges[...]
         for level in range(levels):
             base = GROUP * level
             ref[level, :, first] = jnp.where(lane < 4, pltpu.roll(packed, (-base - 8) % LANES, 1), ref[level, :, first])
+        send(k, first, 1)
+        for level in range(levels):
+            base = GROUP * level
             ref[level, :, last] = jnp.where(
                 lane >= LANES - 4, pltpu.roll(packed, (LANES - 4 - base - 20) % LANES, 1), ref[level, :, last]
             )
-            copies.append(
-                pltpu.make_async_copy(
-                    ref.at[level], out.at[level, pl.ds(aligned(where * mid), mid), :], sems.at[k, level]
-                )
-            )
-            copies[-1].start()
+        send(k, last, 2)
     for copy in copies:
         copy.wait()
 
@@ -554,13 +568,14 @@
     weights, coef_ends, pack_own, weight_own = held(
         own_ends_kernel, [own, forcing, coef], [kept(TILE, width), kept(TILE, LANES), packed, kept(mid, LANES)]
     )
-    other, strip = held(
+    deep = levels // 2 * tiles * TILE
+    other, strip, more = held(
         pack_rows_kernel,
         [own, others, forcing, weights, coef_ends],
-        [kept(levels, TILE, width), kept((levels + 1) * tiles * TILE + 2 * TILE, LANES)],
-    )
-    forcing, strip = lax.optimization_barrier((forcing, strip))
-    strip = across(strip)
+        [kept(levels, TILE, width), kept(deep + tiles * TILE + 2 * TILE, LANES), kept(deep, LANES)],
+    )
+    forcing, strip, more = lax.optimization_barrier((forcing, strip, more))
+    strip, more = across(strip), across(more)
     halfway, pack_other, weight_other = held(
         interior_kernel,
         [own, others, forcing, face_east, face_north],
@@ -587,7 +602,7 @@
     from_east = along(west, -1)
     inside = held(
         outer_rows_kernel,
-        [inside, strip, own, other, forcing, coef],
+        [inside, strip, more, own, other, forcing, coef],
         kept(levels, mid, width),
         [
             scratch(2 * TILE, width),
@@ -618,7 +633,7 @@
         join_kernel,
         [inside, inside_theirs, edges, edges_theirs],
         [kept(levels, mid, width)] * 2 + [jax.ShapeDtypeStruct(increment.shape, F32)],
-        [pltpu.SemaphoreType.DMA((2, levels))],
+        [pltpu.SemaphoreType.DMA((2, 3))],
         out_specs=[VMEM, VMEM, HBM],
         aliases={0: 0, 1: 1},
     )[2]

time: 19.4 us -> 18.9 us (0.974)
  waiting for transfers between devices: 1.88 us -> 1.51 us
    ppermute x2, waiting for transfers between devices: 0.98 us -> 0.66 us  [along(): return lax.ppermute(x, 'gx', [(i, (i + shift) % n_gx) for i in range(n_gx)])]
    ppermute x1 -> x2, starting transfers between devices: 2.77 us -> 2.85 us  [across(): return lax.ppermute(x, AXES, pairs)]
  transfers between devices with their start and end apart: 6 -> 7, of which waited for: 4 -> 3; matrix products, arithmetic and copies ran while one was open for 0% -> 0% of each run, Pallas kernels for 42% -> 43%
where the time goes in v6:
time: 18.9 us; the launch traced here: 18.8 us
  Pallas kernels  9.26 us (49%)
  starting transfers between devices  7.96 us (42%)
  waiting for transfers between devices  1.51 us (8%)
    pallas_call x9, Pallas kernels, call(): pl.pallas_call(functools.partial(kernel, n_gy), out_shape=outs, in_specs=...  9.26 us
    ppermute x2, starting transfers between devices, along(): return lax.ppermute(x, 'gx', [(i, (i + shift) % n_gx) for i in range(n_gx)])  4.09 us
    ppermute x2, starting transfers between devices, across(): return lax.ppermute(x, AXES, pairs)  2.85 us
    ppermute x3, starting transfers between devices, swap(): return lax.ppermute(x, 'mem', [(i, i ^ 1) for i in range(n_mem)])  1.03 us
    ppermute x3, waiting for transfers between devices, swap(): return lax.ppermute(x, 'mem', [(i, i ^ 1) for i in range(n_mem)])  0.84 us
    ppermute x2, waiting for transfers between devices, along(): return lax.ppermute(x, 'gx', [(i, (i + shift) % n_gx) for i in range(n_gx)])  0.66 us
  transfers between devices with their start and end apart: 7, of which 3 were waited for; matrix products, arithmetic and copies ran while one was open for 0% of the time, Pallas kernels for 43%

profile of v6, /device:TPU:0, one launch (start us, length us, event | category | flops | bytes accessed | tf_op | source)
XLA Modules:
  0.0 18.8 jit_solution(429228477286138805)
XLA Ops:
  0.0 0.5 %collective-permute-start = (f32[1,4,64,1024]{3,2,1,0:T(8,128)}, f32[1,4,64,1024]{3,2,1,0:T(8,128)S(1)}, u32[]{:S(2)}, u32[]{:S(2)}) collective-permute-start(f32[1,4,64,1024]{3,2,1,0:T(8,128)} %members.1), channel_id=1, source_target_pairs={{0,16},{16,0},{1,17},{17,1},{2,18},{18,2},{3,19},{19,3},{4,20},{20... | collective-permute-start | bytes 3145736 | tf_op jit(solution)/shard_map/ppermute | solution.py:524
  0.5 2.4 %shard_map.55 = (f32[4,40,1024]{2,1,0:T(8,128)S(1)}, f32[4,40,1024]{2,1,0:T(8,128)S(1)}, f32[3,8,1024]{2,1,0:T(8,128)S(1)}, f32[24,144,128]{2,1,0:T(8,128)S(1)},...) custom-call(f32[1,4,64,1024]{3,2,1,0:T(8,128)} %members.1, f32[4,64,1024]{2,1,0:T(8,128)} %increment.1, ...), custom_call_target="tpu_custom_call" | custom-call | tf_op jit(solution)/shard_map/pallas_call | solution.py:509
  2.9 0.3 %shard_map.56 = (f32[8,1024]{1,0:T(8,128)S(1)}, f32[8,128]{1,0:T(8,128)S(1)}, f32[40,128]{1,0:T(8,128)S(1)}, f32[32,128]{1,0:T(8,128)S(1)}) custom-call(f32[4,40,1024]{2,1,0:T(8,128)S(1)} %get-tuple-element.35.own, f32[4,40,1024]{2,1,0:T(8,128)S(1)} %get-tuple-element.42.forcing, f32[3,8,1024]{2,1,0:T(8,128)S(1)} %get-tuple-element.37.coef), custom_call_target="tpu_custom_call" | custom-call | tf_op jit(solution)/shard_map/pallas_call | solution.py:509
  3.2 0.0 collective-permute-done.others
  3.2 0.1 shard_map.57
  3.3 2.8 %collective-permute-start.1 = (f32[208,128]{1,0:T(8,128)S(1)}, f32[208,128]{1,0:T(8,128)S(1)}, u32[]{:S(2)}, u32[]{:S(2)}) collective-permute-start(f32[208,128]{1,0:T(8,128)S(1)} %get-tuple-element.48), channel_id=1, source_target_pairs={{16,4},{4,16},{17,5},{5,17},{18,6},{6,18},{19,7},{7,19},{20,24},{2... | collective-permute-start | bytes 319496 | tf_op jit(solution)/shard_map/ppermute | solution.py:544
  6.1 0.1 collective-permute-start.2
  6.1 2.0 %shard_map.58 = (f32[24,144,128]{2,1,0:T(8,128)S(1)}, f32[40,128]{1,0:T(8,128)S(1)}, f32[32,128]{1,0:T(8,128)S(1)}) custom-call(f32[4,40,1024]{2,1,0:T(8,128)S(1)} %get-tuple-element.35.own, f32[1,4,64,1024]{3,2,1,0:T(8,128)S(1)} %collective-permute-done.others, f32[4,40,1024]{2,1,0:T(8,128)S(1)} %get-tuple-element.42.forcing, ...), custom_call_target="tpu_custom_call" | custom-call | tf_op jit(solution)/shard_map/pallas_call | solution.py:509
  8.2 1.3 %shard_map.59.inside = f32[4,32,1024]{2,1,0:T(8,128)S(1)} custom-call(f32[24,144,128]{2,1,0:T(8,128)S(1)} %get-tuple-element.45.halfway, f32[4,40,1024]{2,1,0:T(8,128)S(1)} %get-tuple-element.35.own, f32[1,4,64,1024]{3,2,1,0:T(8,128)S(1)} %collective-permute-done.others, f32[24,144,128]{2,1,0:T(8,128)S(1)} %get-tuple-element.43.east, ...), custom_call_target="tpu_custom_call" | custom-call | tf_op jit(solution)/shard_map/pallas_call | solution.py:509
  9.5 0.0 collective-permute-done.1.strip
  9.5 0.1 shard_map.61
  9.6 2.0 %collective-permute-start.3 = (f32[48,128]{1,0:T(8,128)S(1)}, f32[48,128]{1,0:T(8,128)S(1)}, u32[]{:S(2)}, u32[]{:S(2)}) collective-permute-start(f32[48,128]{1,0:T(8,128)S(1)} %get-tuple-element.54), channel_id=1, source_target_pairs={{0,1},{1,2},{2,3},{3,0},{4,5},{5,6},{6,7},{7,4},{8,9},{9,10},{10,1... | collective-permute-start | bytes 73736 | tf_op jit(solution)/shard_map/ppermute | solution.py:527
  11.6 2.1 %collective-permute-start.4 = (f32[48,128]{1,0:T(8,128)S(1)}, f32[48,128]{1,0:T(8,128)S(1)}, u32[]{:S(2)}, u32[]{:S(2)}) collective-permute-start(f32[48,128]{1,0:T(8,128)S(1)} %get-tuple-element.55), channel_id=1, source_target_pairs={{0,3},{1,0},{2,1},{3,2},{4,7},{5,4},{6,5},{7,6},{8,11},{9,8},{10,9... | collective-permute-start | bytes 73736 | tf_op jit(solution)/shard_map/ppermute | solution.py:527
  13.7 0.0 collective-permute-done.2.more
  13.7 1.3 %shard_map.60.mine_in = f32[4,32,1024]{2,1,0:T(8,128)S(1)} custom-call(f32[4,32,1024]{2,1,0:T(8,128)S(1)} %shard_map.59.inside, f32[208,128]{1,0:T(8,128)S(1)} %collective-permute-done.1.strip, f32[128,128]{1,0:T(8,128)S(1)} %collective-permute-done.2.more, f32[4,40,1024]{2,1,0:T(8,128)S(1)} %get-tuple-element.35.own, ...), custom_call_target="tpu_custom_call", output_to_operand_aliasing={{}: (0, {})} | custom-call | tf_op jit(solution)/shard_map/pallas_call | solution.py:509
  15.0 0.5 %collective-permute-done.3.from_west = f32[48,128]{1,0:T(8,128)S(1)} collective-permute-done((f32[48,128]{1,0:T(8,128)S(1)}, f32[48,128]{1,0:T(8,128)S(1)}, u32[]{:S(2)}, u32[]{:S(2)}) %collective-permute-start.3) | collective-permute-done | bytes 24608 | tf_op jit(solution)/shard_map/ppermute | solution.py:527
  15.6 0.2 collective-permute-done.4.from_east
  15.7 0.0 collective-permute-start.5
  15.7 0.7 %shard_map.62.mine_edge = f32[32,128]{1,0:T(8,128)S(1)} custom-call(f32[48,128]{1,0:T(8,128)S(1)} %collective-permute-done.3.from_west, f32[48,128]{1,0:T(8,128)S(1)} %collective-permute-done.4.from_east, f32[48,128]{1,0:T(8,128)S(1)} %get-tuple-element.59.own, f32[48,128]{1,0:T(8,128)S(1)} %get-tuple-element.60.other, ...), custom_call_target="tpu_custom_call" | custom-call | tf_op jit(solution)/shard_map/pallas_call | solution.py:509
  16.4 0.6 %collective-permute-start.6 = (f32[32,128]{1,0:T(8,128)S(1)}, f32[32,128]{1,0:T(8,128)S(1)}, u32[]{:S(2)}, u32[]{:S(2)}) collective-permute-start(f32[32,128]{1,0:T(8,128)S(1)} %shard_map.62.mine_edge), channel_id=1, source_target_pairs={{0,16},{16,0},{1,17},{17,1},{2,18},{18,2},{3,19},{19,3},{4,20},{20... | collective-permute-start | bytes 49160 | tf_op jit(solution)/shard_map/ppermute | solution.py:524
  16.9 0.8 %collective-permute-done.6.theirs_edge = f32[32,128]{1,0:T(8,128)S(1)} collective-permute-done((f32[32,128]{1,0:T(8,128)S(1)}, f32[32,128]{1,0:T(8,128)S(1)}, u32[]{:S(2)}, u32[]{:S(2)}) %collective-permute-start.6) | collective-permute-done | bytes 16416 | tf_op jit(solution)/shard_map/ppermute | solution.py:524
  17.8 0.0 collective-permute-done.5.theirs_in
  17.8 1.0 %shard_map.63 = (f32[4,32,1024]{2,1,0:T(8,128)S(1)}, f32[4,32,1024]{2,1,0:T(8,128)S(1)}, f32[4,64,1024]{2,1,0:T(8,128)}) custom-call(f32[4,32,1024]{2,1,0:T(8,128)S(1)} %shard_map.60.mine_in, f32[4,32,1024]{2,1,0:T(8,128)S(1)} %collective-permute-done.5.theirs_in, f32[32,128]{1,0:T(8,128)S(1)} %shard_map.62.mine_edge, ...), custom_call_target="tpu_custom_call", output_to_operand_aliasing={{0}: (0, {}), {1}: (1, {})} | custom-call | tf_op jit(solution)/shard_map/pallas_call | solution.py:509
Async XLA Ops:
  0.0 3.2 %collective-permute-start = (f32[1,4,64,1024]{3,2,1,0:T(8,128)}, f32[1,4,64,1024]{3,2,1,0:T(8,128)S(1)}, u32[]{:S(2)}, u32[]{:S(2)}) collective-permute-start(f32[1,4,64,1024]{3,2,1,0:T(8,128)} %members.1), channel_id=1, source_target_pairs={{0,16},{16,0},{1,17},{17,1},{2,18},{18,2},{3,19},{19,3},{4,20},{20... | collective-permute-start | bytes 3145736 | tf_op jit(solution)/shard_map/ppermute | solution.py:524
  3.3 6.2 %collective-permute-start.1 = (f32[208,128]{1,0:T(8,128)S(1)}, f32[208,128]{1,0:T(8,128)S(1)}, u32[]{:S(2)}, u32[]{:S(2)}) collective-permute-start(f32[208,128]{1,0:T(8,128)S(1)} %get-tuple-element.48), channel_id=1, source_target_pairs={{16,4},{4,16},{17,5},{5,17},{18,6},{6,18},{19,7},{7,19},{20,24},{2... | collective-permute-start | bytes 319496 | tf_op jit(solution)/shard_map/ppermute | solution.py:544
  6.1 7.6 %collective-permute-start.2 = (f32[128,128]{1,0:T(8,128)S(1)}, f32[128,128]{1,0:T(8,128)S(1)}, u32[]{:S(2)}, u32[]{:S(2)}) collective-permute-start(f32[128,128]{1,0:T(8,128)S(1)} %get-tuple-element.49), channel_id=1, source_target_pairs={{16,4},{4,16},{17,5},{5,17},{18,6},{6,18},{19,7},{7,19},{20,24},{2... | collective-permute-start | bytes 196616 | tf_op jit(solution)/shard_map/ppermute | solution.py:544
  9.6 5.9 %collective-permute-start.3 = (f32[48,128]{1,0:T(8,128)S(1)}, f32[48,128]{1,0:T(8,128)S(1)}, u32[]{:S(2)}, u32[]{:S(2)}) collective-permute-start(f32[48,128]{1,0:T(8,128)S(1)} %get-tuple-element.54), channel_id=1, source_target_pairs={{0,1},{1,2},{2,3},{3,0},{4,5},{5,6},{6,7},{7,4},{8,9},{9,10},{10,1... | collective-permute-start | bytes 73736 | tf_op jit(solution)/shard_map/ppermute | solution.py:527
  11.6 4.1 %collective-permute-start.4 = (f32[48,128]{1,0:T(8,128)S(1)}, f32[48,128]{1,0:T(8,128)S(1)}, u32[]{:S(2)}, u32[]{:S(2)}) collective-permute-start(f32[48,128]{1,0:T(8,128)S(1)} %get-tuple-element.55), channel_id=1, source_target_pairs={{0,3},{1,0},{2,1},{3,2},{4,7},{5,4},{6,5},{7,6},{8,11},{9,8},{10,9... | collective-permute-start | bytes 73736 | tf_op jit(solution)/shard_map/ppermute | solution.py:527
  15.7 2.1 %collective-permute-start.5 = (f32[4,32,1024]{2,1,0:T(8,128)S(1)}, f32[4,32,1024]{2,1,0:T(8,128)S(1)}, u32[]{:S(2)}, u32[]{:S(2)}) collective-permute-start(f32[4,32,1024]{2,1,0:T(8,128)S(1)} %shard_map.60.mine_in), channel_id=1, source_target_pairs={{0,16},{16,0},{1,17},{17,1},{2,18},{18,2},{3,19},{19,3},{4,20},{20... | collective-permute-start | bytes 1572872 | tf_op jit(solution)/shard_map/ppermute | solution.py:524
  16.4 1.4 %collective-permute-start.6 = (f32[32,128]{1,0:T(8,128)S(1)}, f32[32,128]{1,0:T(8,128)S(1)}, u32[]{:S(2)}, u32[]{:S(2)}) collective-permute-start(f32[32,128]{1,0:T(8,128)S(1)} %shard_map.62.mine_edge), channel_id=1, source_target_pairs={{0,16},{16,0},{1,17},{17,1},{2,18},{18,2},{3,19},{19,3},{4,20},{20... | collective-permute-start | bytes 49160 | tf_op jit(solution)/shard_map/ppermute | solution.py:524

commit v7 on v6

--- a/solution.py
+++ b/solution.py
@@ -237,8 +237,9 @@
     _, tall, width = own.shape
     tiles = width // LANES
     planes = east.shape[0]
-    offset = tall - planes
-    half = half_of(gy_size)
+    offset = planes - 2 * STEPS
+    half = half_of(gy_size)
+    base = half * STEPS
     part = pl.ds(aligned(half * (tall - 2 * TILE)), tall)
     small = [
         pltpu.make_async_copy(mask.at[part, :], mask_buf, sems.at[0]),
@@ -264,7 +265,7 @@
         face[pl.ds(c * tall, tall), :], face[pl.ds((tiles + c) * tall, tall), :] = faces(zm, mm, wet, tile(c), width, tall)
     for q in range(planes):
         for k, ref in enumerate((east, north)):
-            ref[q, BODY, :] = turn(face, [k * tiles * tall + ch * offset + q for _ in range(TILE) for ch in range(2)], tall)
+            ref[q, BODY, :] = turn(face, [k * tiles * tall + ch * offset + q + base for _ in range(TILE) for ch in range(2)], tall)
     refresh(east, 0, planes)
     ends = (tile(0), tile(tiles - 1))
     for k, ref in enumerate((zm, mm, wet)):
@@ -283,8 +284,9 @@
     tiles = width // LANES
     mid = tall - TILE
     planes = east.shape[0]
-    offset = tall - planes
-    half = half_of(gy_size)
+    offset = planes - 2 * STEPS
+    half = half_of(gy_size)
+    base = half * STEPS
     part = pl.ds(aligned(half * (mid - TILE)), tall)
     keep_other = pl.ds(aligned(half * mid), mid)
     for c in range(tiles):
@@ -302,7 +304,7 @@
     weight_other[...] = edge_columns(*([others[0, level, keep_other, cols] for level in range(levels)] for cols in ends))
     fields = range(2 * levels)
     for q in range(planes):
-        u[q, BODY, :] = turn(field, [f * tiles * tall + ch * offset + q for f in fields for ch in range(2)], tall)
+        u[q, BODY, :] = turn(field, [f * tiles * tall + ch * offset + q + base for f in fields for ch in range(2)], tall)
     buffers = [u, u_next, u][:FIRST_STEPS] + [halfway]
     for step in range(FIRST_STEPS):
         count = planes - 2 - 2 * step
@@ -316,8 +318,9 @@
     tiles = width // LANES
     mid = tall - TILE
     planes = east.shape[0]
-    offset = tall - planes
-    half = half_of(gy_size)
+    offset = planes - 2 * STEPS
+    half = half_of(gy_size)
+    base = half * STEPS
     keep_own, keep_other = pl.ds(aligned(half * TILE), mid), pl.ds(aligned(half * mid), mid)
     fields = range(2 * levels)
     source = halfway
@@ -333,7 +336,7 @@
         for f in fields:
             for ch in range(2):
                 group = (2 * f + ch) * tiles
-                result[pl.ds(f * tiles * tall + ch * offset + q, tiles, stride=tall), :] = flat[group : group + tiles]
+                result[pl.ds(f * tiles * tall + ch * offset + q + base, tiles, stride=tall), :] = flat[group : group + tiles]
     for level in range(levels):
         for c in range(tiles):
             a, b = (
@@ -502,7 +505,7 @@
     mid = rows // 2
     tall = mid + TILE
     full = tall + TILE
-    planes = 3 * TILE
+    planes = (mid - STEPS) // 2 + 2 * STEPS
     assert tiles == TILE and 4 * levels * tiles == LANES and tall == 5 * TILE and n_mem % 2 == 0
 
     def call(kernel, ins, specs, outs, scratch=(), out_specs=None, aliases={}):

time: 18.9 us -> 18.7 us (0.989)
  Pallas kernels: 9.26 us -> 8.94 us
    pallas_call x9, Pallas kernels: 9.26 us -> 8.94 us  [call(): pl.pallas_call(functools.partial(kernel, n_gy), out_shape=outs, in_specs=...]
  transfers between devices with their start and end apart: 7 -> 7, of which waited for: 3 -> 3; matrix products, arithmetic and copies ran while one was open for 0% -> 0% of each run, Pallas kernels for 43% -> 42%
where the time goes in v7:
time: 18.7 us; the launch traced here: 18.5 us
  Pallas kernels  8.94 us (48%)
  starting transfers between devices  8.03 us (43%)
  waiting for transfers between devices  1.51 us (8%)
    pallas_call x9, Pallas kernels, call(): pl.pallas_call(functools.partial(kernel, n_gy), out_shape=outs, in_specs=...  8.94 us
    ppermute x2, starting transfers between devices, along(): return lax.ppermute(x, 'gx', [(i, (i + shift) % n_gx) for i in range(n_gx)])  4.09 us
    ppermute x2, starting transfers between devices, across(): return lax.ppermute(x, AXES, pairs)  2.91 us
    ppermute x3, starting transfers between devices, swap(): return lax.ppermute(x, 'mem', [(i, i ^ 1) for i in range(n_mem)])  1.03 us
    ppermute x3, waiting for transfers between devices, swap(): return lax.ppermute(x, 'mem', [(i, i ^ 1) for i in range(n_mem)])  0.84 us
    ppermute x2, waiting for transfers between devices, along(): return lax.ppermute(x, 'gx', [(i, (i + shift) % n_gx) for i in range(n_gx)])  0.66 us
  transfers between devices with their start and end apart: 7, of which 3 were waited for; matrix products, arithmetic and copies ran while one was open for 0% of the time, Pallas kernels for 42%

profile of v7, /device:TPU:0, one launch (start us, length us, event | category | flops | bytes accessed | tf_op | source)
XLA Modules:
  0.0 18.5 jit_solution(17479813180709680968)
XLA Ops:
  0.0 0.5 %collective-permute-start = (f32[1,4,64,1024]{3,2,1,0:T(8,128)}, f32[1,4,64,1024]{3,2,1,0:T(8,128)S(1)}, u32[]{:S(2)}, u32[]{:S(2)}) collective-permute-start(f32[1,4,64,1024]{3,2,1,0:T(8,128)} %members.1), channel_id=1, source_target_pairs={{0,16},{16,0},{1,17},{17,1},{2,18},{18,2},{3,19},{19,3},{4,20},{20... | collective-permute-start | bytes 3145736 | tf_op jit(solution)/shard_map/ppermute | solution.py:527
  0.5 2.3 %shard_map.55 = (f32[4,40,1024]{2,1,0:T(8,128)S(1)}, f32[4,40,1024]{2,1,0:T(8,128)S(1)}, f32[3,8,1024]{2,1,0:T(8,128)S(1)}, f32[22,144,128]{2,1,0:T(8,128)S(1)},...) custom-call(f32[1,4,64,1024]{3,2,1,0:T(8,128)} %members.1, f32[4,64,1024]{2,1,0:T(8,128)} %increment.1, ...), custom_call_target="tpu_custom_call" | custom-call | tf_op jit(solution)/shard_map/pallas_call | solution.py:512
  2.8 0.3 %shard_map.56 = (f32[8,1024]{1,0:T(8,128)S(1)}, f32[8,128]{1,0:T(8,128)S(1)}, f32[40,128]{1,0:T(8,128)S(1)}, f32[32,128]{1,0:T(8,128)S(1)}) custom-call(f32[4,40,1024]{2,1,0:T(8,128)S(1)} %get-tuple-element.35.own, f32[4,40,1024]{2,1,0:T(8,128)S(1)} %get-tuple-element.42.forcing, f32[3,8,1024]{2,1,0:T(8,128)S(1)} %get-tuple-element.37.coef), custom_call_target="tpu_custom_call" | custom-call | tf_op jit(solution)/shard_map/pallas_call | solution.py:512
  3.1 0.0 collective-permute-done.others
  3.1 0.1 shard_map.57
  3.2 2.8 %collective-permute-start.1 = (f32[208,128]{1,0:T(8,128)S(1)}, f32[208,128]{1,0:T(8,128)S(1)}, u32[]{:S(2)}, u32[]{:S(2)}) collective-permute-start(f32[208,128]{1,0:T(8,128)S(1)} %get-tuple-element.48), channel_id=1, source_target_pairs={{16,4},{4,16},{17,5},{5,17},{18,6},{6,18},{19,7},{7,19},{20,24},{2... | collective-permute-start | bytes 319496 | tf_op jit(solution)/shard_map/ppermute | solution.py:547
  6.1 0.1 collective-permute-start.2
  6.1 1.9 %shard_map.58 = (f32[22,144,128]{2,1,0:T(8,128)S(1)}, f32[40,128]{1,0:T(8,128)S(1)}, f32[32,128]{1,0:T(8,128)S(1)}) custom-call(f32[4,40,1024]{2,1,0:T(8,128)S(1)} %get-tuple-element.35.own, f32[1,4,64,1024]{3,2,1,0:T(8,128)S(1)} %collective-permute-done.others, f32[4,40,1024]{2,1,0:T(8,128)S(1)} %get-tuple-element.42.forcing, ...), custom_call_target="tpu_custom_call" | custom-call | tf_op jit(solution)/shard_map/pallas_call | solution.py:512
  8.0 1.2 %shard_map.59.inside = f32[4,32,1024]{2,1,0:T(8,128)S(1)} custom-call(f32[22,144,128]{2,1,0:T(8,128)S(1)} %get-tuple-element.45.halfway, f32[4,40,1024]{2,1,0:T(8,128)S(1)} %get-tuple-element.35.own, f32[1,4,64,1024]{3,2,1,0:T(8,128)S(1)} %collective-permute-done.others, f32[22,144,128]{2,1,0:T(8,128)S(1)} %get-tuple-element.43.east, ...), custom_call_target="tpu_custom_call" | custom-call | tf_op jit(solution)/shard_map/pallas_call | solution.py:512
  9.2 0.0 collective-permute-done.1.strip
  9.2 0.1 shard_map.61
  9.3 2.0 %collective-permute-start.3 = (f32[48,128]{1,0:T(8,128)S(1)}, f32[48,128]{1,0:T(8,128)S(1)}, u32[]{:S(2)}, u32[]{:S(2)}) collective-permute-start(f32[48,128]{1,0:T(8,128)S(1)} %get-tuple-element.54), channel_id=1, source_target_pairs={{0,1},{1,2},{2,3},{3,0},{4,5},{5,6},{6,7},{7,4},{8,9},{9,10},{10,1... | collective-permute-start | bytes 73736 | tf_op jit(solution)/shard_map/ppermute | solution.py:530
  11.3 2.1 %collective-permute-start.4 = (f32[48,128]{1,0:T(8,128)S(1)}, f32[48,128]{1,0:T(8,128)S(1)}, u32[]{:S(2)}, u32[]{:S(2)}) collective-permute-start(f32[48,128]{1,0:T(8,128)S(1)} %get-tuple-element.55), channel_id=1, source_target_pairs={{0,3},{1,0},{2,1},{3,2},{4,7},{5,4},{6,5},{7,6},{8,11},{9,8},{10,9... | collective-permute-start | bytes 73736 | tf_op jit(solution)/shard_map/ppermute | solution.py:530
  13.4 0.0 collective-permute-done.2.more
  13.4 1.3 %shard_map.60.mine_in = f32[4,32,1024]{2,1,0:T(8,128)S(1)} custom-call(f32[4,32,1024]{2,1,0:T(8,128)S(1)} %shard_map.59.inside, f32[208,128]{1,0:T(8,128)S(1)} %collective-permute-done.1.strip, f32[128,128]{1,0:T(8,128)S(1)} %collective-permute-done.2.more, f32[4,40,1024]{2,1,0:T(8,128)S(1)} %get-tuple-element.35.own, ...), custom_call_target="tpu_custom_call", output_to_operand_aliasing={{}: (0, {})} | custom-call | tf_op jit(solution)/shard_map/pallas_call | solution.py:512
  14.8 0.5 %collective-permute-done.3.from_west = f32[48,128]{1,0:T(8,128)S(1)} collective-permute-done((f32[48,128]{1,0:T(8,128)S(1)}, f32[48,128]{1,0:T(8,128)S(1)}, u32[]{:S(2)}, u32[]{:S(2)}) %collective-permute-start.3) | collective-permute-done | bytes 24608 | tf_op jit(solution)/shard_map/ppermute | solution.py:530
  15.3 0.2 collective-permute-done.4.from_east
  15.4 0.0 collective-permute-start.5
  15.4 0.7 %shard_map.62.mine_edge = f32[32,128]{1,0:T(8,128)S(1)} custom-call(f32[48,128]{1,0:T(8,128)S(1)} %collective-permute-done.3.from_west, f32[48,128]{1,0:T(8,128)S(1)} %collective-permute-done.4.from_east, f32[48,128]{1,0:T(8,128)S(1)} %get-tuple-element.59.own, f32[48,128]{1,0:T(8,128)S(1)} %get-tuple-element.60.other, ...), custom_call_target="tpu_custom_call" | custom-call | tf_op jit(solution)/shard_map/pallas_call | solution.py:512
  16.1 0.6 %collective-permute-start.6 = (f32[32,128]{1,0:T(8,128)S(1)}, f32[32,128]{1,0:T(8,128)S(1)}, u32[]{:S(2)}, u32[]{:S(2)}) collective-permute-start(f32[32,128]{1,0:T(8,128)S(1)} %shard_map.62.mine_edge), channel_id=1, source_target_pairs={{0,16},{16,0},{1,17},{17,1},{2,18},{18,2},{3,19},{19,3},{4,20},{20... | collective-permute-start | bytes 49160 | tf_op jit(solution)/shard_map/ppermute | solution.py:527
  16.7 0.8 %collective-permute-done.6.theirs_edge = f32[32,128]{1,0:T(8,128)S(1)} collective-permute-done((f32[32,128]{1,0:T(8,128)S(1)}, f32[32,128]{1,0:T(8,128)S(1)}, u32[]{:S(2)}, u32[]{:S(2)}) %collective-permute-start.6) | collective-permute-done | bytes 16416 | tf_op jit(solution)/shard_map/ppermute | solution.py:527
  17.5 0.0 collective-permute-done.5.theirs_in
  17.5 1.0 %shard_map.63 = (f32[4,32,1024]{2,1,0:T(8,128)S(1)}, f32[4,32,1024]{2,1,0:T(8,128)S(1)}, f32[4,64,1024]{2,1,0:T(8,128)}) custom-call(f32[4,32,1024]{2,1,0:T(8,128)S(1)} %shard_map.60.mine_in, f32[4,32,1024]{2,1,0:T(8,128)S(1)} %collective-permute-done.5.theirs_in, f32[32,128]{1,0:T(8,128)S(1)} %shard_map.62.mine_edge, ...), custom_call_target="tpu_custom_call", output_to_operand_aliasing={{0}: (0, {}), {1}: (1, {})} | custom-call | tf_op jit(solution)/shard_map/pallas_call | solution.py:512
Async XLA Ops:
  0.0 3.1 %collective-permute-start = (f32[1,4,64,1024]{3,2,1,0:T(8,128)}, f32[1,4,64,1024]{3,2,1,0:T(8,128)S(1)}, u32[]{:S(2)}, u32[]{:S(2)}) collective-permute-start(f32[1,4,64,1024]{3,2,1,0:T(8,128)} %members.1), channel_id=1, source_target_pairs={{0,16},{16,0},{1,17},{17,1},{2,18},{18,2},{3,19},{19,3},{4,20},{20... | collective-permute-start | bytes 3145736 | tf_op jit(solution)/shard_map/ppermute | solution.py:527
  3.2 6.0 %collective-permute-start.1 = (f32[208,128]{1,0:T(8,128)S(1)}, f32[208,128]{1,0:T(8,128)S(1)}, u32[]{:S(2)}, u32[]{:S(2)}) collective-permute-start(f32[208,128]{1,0:T(8,128)S(1)} %get-tuple-element.48), channel_id=1, source_target_pairs={{16,4},{4,16},{17,5},{5,17},{18,6},{6,18},{19,7},{7,19},{20,24},{2... | collective-permute-start | bytes 319496 | tf_op jit(solution)/shard_map/ppermute | solution.py:547
  6.1 7.4 %collective-permute-start.2 = (f32[128,128]{1,0:T(8,128)S(1)}, f32[128,128]{1,0:T(8,128)S(1)}, u32[]{:S(2)}, u32[]{:S(2)}) collective-permute-start(f32[128,128]{1,0:T(8,128)S(1)} %get-tuple-element.49), channel_id=1, source_target_pairs={{16,4},{4,16},{17,5},{5,17},{18,6},{6,18},{19,7},{7,19},{20,24},{2... | collective-permute-start | bytes 196616 | tf_op jit(solution)/shard_map/ppermute | solution.py:547
  9.3 5.9 %collective-permute-start.3 = (f32[48,128]{1,0:T(8,128)S(1)}, f32[48,128]{1,0:T(8,128)S(1)}, u32[]{:S(2)}, u32[]{:S(2)}) collective-permute-start(f32[48,128]{1,0:T(8,128)S(1)} %get-tuple-element.54), channel_id=1, source_target_pairs={{0,1},{1,2},{2,3},{3,0},{4,5},{5,6},{6,7},{7,4},{8,9},{9,10},{10,1... | collective-permute-start | bytes 73736 | tf_op jit(solution)/shard_map/ppermute | solution.py:530
  11.3 4.1 %collective-permute-start.4 = (f32[48,128]{1,0:T(8,128)S(1)}, f32[48,128]{1,0:T(8,128)S(1)}, u32[]{:S(2)}, u32[]{:S(2)}) collective-permute-start(f32[48,128]{1,0:T(8,128)S(1)} %get-tuple-element.55), channel_id=1, source_target_pairs={{0,3},{1,0},{2,1},{3,2},{4,7},{5,4},{6,5},{7,6},{8,11},{9,8},{10,9... | collective-permute-start | bytes 73736 | tf_op jit(solution)/shard_map/ppermute | solution.py:530
  15.4 2.1 %collective-permute-start.5 = (f32[4,32,1024]{2,1,0:T(8,128)S(1)}, f32[4,32,1024]{2,1,0:T(8,128)S(1)}, u32[]{:S(2)}, u32[]{:S(2)}) collective-permute-start(f32[4,32,1024]{2,1,0:T(8,128)S(1)} %shard_map.60.mine_in), channel_id=1, source_target_pairs={{0,16},{16,0},{1,17},{17,1},{2,18},{18,2},{3,19},{19,3},{4,20},{20... | collective-permute-start | bytes 1572872 | tf_op jit(solution)/shard_map/ppermute | solution.py:527
  16.1 1.4 %collective-permute-start.6 = (f32[32,128]{1,0:T(8,128)S(1)}, f32[32,128]{1,0:T(8,128)S(1)}, u32[]{:S(2)}, u32[]{:S(2)}) collective-permute-start(f32[32,128]{1,0:T(8,128)S(1)} %shard_map.62.mine_edge), channel_id=1, source_target_pairs={{0,16},{16,0},{1,17},{17,1},{2,18},{18,2},{3,19},{19,3},{4,20},{20... | collective-permute-start | bytes 49160 | tf_op jit(solution)/shard_map/ppermute | solution.py:527

commit v8 on v7

--- a/solution.py
+++ b/solution.py
@@ -7,7 +7,7 @@
 from jax.sharding import PartitionSpec as P
 
 STEPS = 4
-FIRST_STEPS = 2
+FIRST_STEPS = 4
 TILE = 8
 LANES = 128
 AXES = ("mem", "gy", "gx")
@@ -16,7 +16,7 @@
 HBM = pl.BlockSpec(memory_space=pltpu.HBM)
 
 BODY = slice(TILE, TILE + LANES)
-DEPTH = LANES + 2 * TILE
+DEPTH = LANES + 3 * TILE
 GROUP = 32
 
 
@@ -305,12 +305,13 @@
     fields = range(2 * levels)
     for q in range(planes):
         u[q, BODY, :] = turn(field, [f * tiles * tall + ch * offset + q + base for f in fields for ch in range(2)], tall)
-    buffers = [u, u_next, u][:FIRST_STEPS] + [halfway]
+    buffers = [u, u_next, u, u_next][:FIRST_STEPS] + [halfway]
     for step in range(FIRST_STEPS):
         count = planes - 2 - 2 * step
         refresh(buffers[step], step + 1, count)
         sweep(buffers[step], buffers[step + 1], east, north, step + 1, step + count)
-    refresh(halfway, FIRST_STEPS + 1, planes - 2 - 2 * FIRST_STEPS)
+    if FIRST_STEPS < STEPS:
+        refresh(halfway, FIRST_STEPS + 1, planes - 2 - 2 * FIRST_STEPS)
 
 
 def interior_rest_kernel(gy_size, halfway, own, others, east, north, out, u, u_next, result):
@@ -585,6 +586,14 @@
         [turned, packed, kept(mid, LANES)],
         [scratch(2 * levels * tiles * tall, LANES), scratch(planes, DEPTH, LANES), scratch(planes, DEPTH, LANES)],
     )
+    full_own, full_other, full_coef, west, east = held(
+        halo_columns_kernel,
+        [strip, pack_own, pack_other, pack_coef],
+        [end, end, kept(3, full, LANES), end, end],
+    )
+    halfway, west, east = lax.optimization_barrier((halfway, west, east))
+    from_west = along(east, 1)
+    from_east = along(west, -1)
     inside = held(
         interior_rest_kernel,
         [halfway, own, others, face_east, face_north],
@@ -595,14 +604,7 @@
             scratch(2 * levels * tiles * tall, LANES),
         ],
     )
-    inside, pack_other = lax.optimization_barrier((inside, pack_other))
-    full_own, full_other, full_coef, west, east = held(
-        halo_columns_kernel,
-        [strip, pack_own, pack_other, pack_coef],
-        [end, end, kept(3, full, LANES), end, end],
-    )
-    from_west = along(east, 1)
-    from_east = along(west, -1)
+    inside, forcing = lax.optimization_barrier((inside, forcing))
     inside = held(
         outer_rows_kernel,
         [inside, strip, more, own, other, forcing, coef],

time: 18.7 us -> 18.7 us (level)
  waiting for transfers between devices: 1.51 us -> 1.24 us
  Pallas kernels: 8.94 us -> 9.2 us
    ppermute x2, waiting for transfers between devices: 0.66 us -> 0.39 us  [along(): return lax.ppermute(x, 'gx', [(i, (i + shift) % n_gx) for i in range(n_gx)])]
    pallas_call x9, Pallas kernels: 8.94 us -> 9.2 us  [call(): pl.pallas_call(functools.partial(kernel, n_gy), out_shape=outs, in_specs=...]
  transfers between devices with their start and end apart: 7 -> 7, of which waited for: 3 -> 3; matrix products, arithmetic and copies ran while one was open for 0% -> 0% of each run, Pallas kernels for 42% -> 44%
where the time goes in v8:
time: 18.7 us; the launch traced here: 18.5 us
  Pallas kernels  9.2 us (49%)
  starting transfers between devices  8.02 us (43%)
  waiting for transfers between devices  1.24 us (7%)
    pallas_call x9, Pallas kernels, call(): pl.pallas_call(functools.partial(kernel, n_gy), out_shape=outs, in_specs=...  9.2 us
    ppermute x2, starting transfers between devices, along(): return lax.ppermute(x, 'gx', [(i, (i + shift) % n_gx) for i in range(n_gx)])  4.09 us
    ppermute x2, starting transfers between devices, across(): return lax.ppermute(x, AXES, pairs)  2.9 us
    ppermute x3, starting transfers between devices, swap(): return lax.ppermute(x, 'mem', [(i, i ^ 1) for i in range(n_mem)])  1.03 us
    ppermute x3, waiting for transfers between devices, swap(): return lax.ppermute(x, 'mem', [(i, i ^ 1) for i in range(n_mem)])  0.84 us
    ppermute x2, waiting for transfers between devices, along(): return lax.ppermute(x, 'gx', [(i, (i + shift) % n_gx) for i in range(n_gx)])  0.39 us
  transfers between devices with their start and end apart: 7, of which 3 were waited for; matrix products, arithmetic and copies ran while one was open for 0% of the time, Pallas kernels for 44%

profile of v8, /device:TPU:0, one launch (start us, length us, event | category | flops | bytes accessed | tf_op | source)
XLA Modules:
  0.0 18.5 jit_solution(642325084322283385)
XLA Ops:
  0.0 0.5 %collective-permute-start = (f32[1,4,64,1024]{3,2,1,0:T(8,128)}, f32[1,4,64,1024]{3,2,1,0:T(8,128)S(1)}, u32[]{:S(2)}, u32[]{:S(2)}) collective-permute-start(f32[1,4,64,1024]{3,2,1,0:T(8,128)} %members.1), channel_id=1, source_target_pairs={{0,16},{16,0},{1,17},{17,1},{2,18},{18,2},{3,19},{19,3},{4,20},{20... | collective-permute-start | bytes 3145736 | tf_op jit(solution)/shard_map/ppermute | solution.py:528
  0.5 2.3 %shard_map.55 = (f32[4,40,1024]{2,1,0:T(8,128)S(1)}, f32[4,40,1024]{2,1,0:T(8,128)S(1)}, f32[3,8,1024]{2,1,0:T(8,128)S(1)}, f32[22,152,128]{2,1,0:T(8,128)S(1)},...) custom-call(f32[1,4,64,1024]{3,2,1,0:T(8,128)} %members.1, f32[4,64,1024]{2,1,0:T(8,128)} %increment.1, ...), custom_call_target="tpu_custom_call" | custom-call | tf_op jit(solution)/shard_map/pallas_call | solution.py:513
  2.8 0.3 %shard_map.56 = (f32[8,1024]{1,0:T(8,128)S(1)}, f32[8,128]{1,0:T(8,128)S(1)}, f32[40,128]{1,0:T(8,128)S(1)}, f32[32,128]{1,0:T(8,128)S(1)}) custom-call(f32[4,40,1024]{2,1,0:T(8,128)S(1)} %get-tuple-element.38.own, f32[4,40,1024]{2,1,0:T(8,128)S(1)} %get-tuple-element.59.forcing, f32[3,8,1024]{2,1,0:T(8,128)S(1)} %get-tuple-element.40.coef), custom_call_target="tpu_custom_call" | custom-call | tf_op jit(solution)/shard_map/pallas_call | solution.py:513
  3.1 0.0 collective-permute-done.others
  3.1 0.1 shard_map.57
  3.2 2.8 %collective-permute-start.1 = (f32[208,128]{1,0:T(8,128)S(1)}, f32[208,128]{1,0:T(8,128)S(1)}, u32[]{:S(2)}, u32[]{:S(2)}) collective-permute-start(f32[208,128]{1,0:T(8,128)S(1)} %get-tuple-element.49), channel_id=1, source_target_pairs={{16,4},{4,16},{17,5},{5,17},{18,6},{6,18},{19,7},{7,19},{20,24},{2... | collective-permute-start | bytes 319496 | tf_op jit(solution)/shard_map/ppermute | solution.py:548
  6.1 0.1 collective-permute-start.2
  6.1 2.9 %shard_map.58 = (f32[22,152,128]{2,1,0:T(8,128)S(1)}, f32[40,128]{1,0:T(8,128)S(1)}, f32[32,128]{1,0:T(8,128)S(1)}) custom-call(f32[4,40,1024]{2,1,0:T(8,128)S(1)} %get-tuple-element.38.own, f32[1,4,64,1024]{3,2,1,0:T(8,128)S(1)} %collective-permute-done.others, f32[4,40,1024]{2,1,0:T(8,128)S(1)} %get-tuple-element.59.forcing, ...), custom_call_target="tpu_custom_call" | custom-call | tf_op jit(solution)/shard_map/pallas_call | solution.py:513
  9.1 0.0 collective-permute-done.1.strip
  9.1 0.1 shard_map.59
  9.2 2.0 %collective-permute-start.3 = (f32[48,128]{1,0:T(8,128)S(1)}, f32[48,128]{1,0:T(8,128)S(1)}, u32[]{:S(2)}, u32[]{:S(2)}) collective-permute-start(f32[48,128]{1,0:T(8,128)S(1)} %get-tuple-element.60), channel_id=1, source_target_pairs={{0,1},{1,2},{2,3},{3,0},{4,5},{5,6},{6,7},{7,4},{8,9},{9,10},{10,1... | collective-permute-start | bytes 73736 | tf_op jit(solution)/shard_map/ppermute | solution.py:531
  11.2 2.1 %collective-permute-start.4 = (f32[48,128]{1,0:T(8,128)S(1)}, f32[48,128]{1,0:T(8,128)S(1)}, u32[]{:S(2)}, u32[]{:S(2)}) collective-permute-start(f32[48,128]{1,0:T(8,128)S(1)} %get-tuple-element.61), channel_id=1, source_target_pairs={{0,3},{1,0},{2,1},{3,2},{4,7},{5,4},{6,5},{7,6},{8,11},{9,8},{10,9... | collective-permute-start | bytes 73736 | tf_op jit(solution)/shard_map/ppermute | solution.py:531
  13.3 0.4 %shard_map.60.inside = f32[4,32,1024]{2,1,0:T(8,128)S(1)} custom-call(f32[22,152,128]{2,1,0:T(8,128)S(1)} %get-tuple-element.55.halfway, f32[4,40,1024]{2,1,0:T(8,128)S(1)} %get-tuple-element.38.own, f32[1,4,64,1024]{3,2,1,0:T(8,128)S(1)} %collective-permute-done.others, f32[22,152,128]{2,1,0:T(8,128)S(1)} %get-tuple-element.46.east, ...), custom_call_target="tpu_custom_call" | custom-call | tf_op jit(solution)/shard_map/pallas_call | solution.py:513
  13.7 0.0 collective-permute-done.2.more
  13.7 1.3 %shard_map.61.mine_in = f32[4,32,1024]{2,1,0:T(8,128)S(1)} custom-call(f32[4,32,1024]{2,1,0:T(8,128)S(1)} %shard_map.60.inside, f32[208,128]{1,0:T(8,128)S(1)} %collective-permute-done.1.strip, f32[128,128]{1,0:T(8,128)S(1)} %collective-permute-done.2.more, f32[4,40,1024]{2,1,0:T(8,128)S(1)} %get-tuple-element.38.own, ...), custom_call_target="tpu_custom_call", output_to_operand_aliasing={{}: (0, {})} | custom-call | tf_op jit(solution)/shard_map/pallas_call | solution.py:513
  15.0 0.2 collective-permute-done.3.from_west
  15.2 0.2 %collective-permute-done.4.from_east = f32[48,128]{1,0:T(8,128)S(1)} collective-permute-done((f32[48,128]{1,0:T(8,128)S(1)}, f32[48,128]{1,0:T(8,128)S(1)}, u32[]{:S(2)}, u32[]{:S(2)}) %collective-permute-start.4) | collective-permute-done | bytes 24608 | tf_op jit(solution)/shard_map/ppermute | solution.py:531
  15.4 0.0 collective-permute-start.5
  15.4 0.7 %shard_map.62.mine_edge = f32[32,128]{1,0:T(8,128)S(1)} custom-call(f32[48,128]{1,0:T(8,128)S(1)} %collective-permute-done.3.from_west, f32[48,128]{1,0:T(8,128)S(1)} %collective-permute-done.4.from_east, f32[48,128]{1,0:T(8,128)S(1)} %get-tuple-element.65.own, f32[48,128]{1,0:T(8,128)S(1)} %get-tuple-element.66.other, ...), custom_call_target="tpu_custom_call" | custom-call | tf_op jit(solution)/shard_map/pallas_call | solution.py:513
  16.1 0.6 %collective-permute-start.6 = (f32[32,128]{1,0:T(8,128)S(1)}, f32[32,128]{1,0:T(8,128)S(1)}, u32[]{:S(2)}, u32[]{:S(2)}) collective-permute-start(f32[32,128]{1,0:T(8,128)S(1)} %shard_map.62.mine_edge), channel_id=1, source_target_pairs={{0,16},{16,0},{1,17},{17,1},{2,18},{18,2},{3,19},{19,3},{4,20},{20... | collective-permute-start | bytes 49160 | tf_op jit(solution)/shard_map/ppermute | solution.py:528
  16.7 0.8 %collective-permute-done.6.theirs_edge = f32[32,128]{1,0:T(8,128)S(1)} collective-permute-done((f32[32,128]{1,0:T(8,128)S(1)}, f32[32,128]{1,0:T(8,128)S(1)}, u32[]{:S(2)}, u32[]{:S(2)}) %collective-permute-start.6) | collective-permute-done | bytes 16416 | tf_op jit(solution)/shard_map/ppermute | solution.py:528
  17.5 0.0 collective-permute-done.5.theirs_in
  17.5 1.0 %shard_map.63 = (f32[4,32,1024]{2,1,0:T(8,128)S(1)}, f32[4,32,1024]{2,1,0:T(8,128)S(1)}, f32[4,64,1024]{2,1,0:T(8,128)}) custom-call(f32[4,32,1024]{2,1,0:T(8,128)S(1)} %shard_map.61.mine_in, f32[4,32,1024]{2,1,0:T(8,128)S(1)} %collective-permute-done.5.theirs_in, f32[32,128]{1,0:T(8,128)S(1)} %shard_map.62.mine_edge, ...), custom_call_target="tpu_custom_call", output_to_operand_aliasing={{0}: (0, {}), {1}: (1, {})} | custom-call | tf_op jit(solution)/shard_map/pallas_call | solution.py:513
Async XLA Ops:
  0.0 3.1 %collective-permute-start = (f32[1,4,64,1024]{3,2,1,0:T(8,128)}, f32[1,4,64,1024]{3,2,1,0:T(8,128)S(1)}, u32[]{:S(2)}, u32[]{:S(2)}) collective-permute-start(f32[1,4,64,1024]{3,2,1,0:T(8,128)} %members.1), channel_id=1, source_target_pairs={{0,16},{16,0},{1,17},{17,1},{2,18},{18,2},{3,19},{19,3},{4,20},{20... | collective-permute-start | bytes 3145736 | tf_op jit(solution)/shard_map/ppermute | solution.py:528
  3.2 5.8 %collective-permute-start.1 = (f32[208,128]{1,0:T(8,128)S(1)}, f32[208,128]{1,0:T(8,128)S(1)}, u32[]{:S(2)}, u32[]{:S(2)}) collective-permute-start(f32[208,128]{1,0:T(8,128)S(1)} %get-tuple-element.49), channel_id=1, source_target_pairs={{16,4},{4,16},{17,5},{5,17},{18,6},{6,18},{19,7},{7,19},{20,24},{2... | collective-permute-start | bytes 319496 | tf_op jit(solution)/shard_map/ppermute | solution.py:548
  6.1 7.7 %collective-permute-start.2 = (f32[128,128]{1,0:T(8,128)S(1)}, f32[128,128]{1,0:T(8,128)S(1)}, u32[]{:S(2)}, u32[]{:S(2)}) collective-permute-start(f32[128,128]{1,0:T(8,128)S(1)} %get-tuple-element.57), channel_id=1, source_target_pairs={{16,4},{4,16},{17,5},{5,17},{18,6},{6,18},{19,7},{7,19},{20,24},{2... | collective-permute-start | bytes 196616 | tf_op jit(solution)/shard_map/ppermute | solution.py:548
  9.2 6.0 %collective-permute-start.3 = (f32[48,128]{1,0:T(8,128)S(1)}, f32[48,128]{1,0:T(8,128)S(1)}, u32[]{:S(2)}, u32[]{:S(2)}) collective-permute-start(f32[48,128]{1,0:T(8,128)S(1)} %get-tuple-element.60), channel_id=1, source_target_pairs={{0,1},{1,2},{2,3},{3,0},{4,5},{5,6},{6,7},{7,4},{8,9},{9,10},{10,1... | collective-permute-start | bytes 73736 | tf_op jit(solution)/shard_map/ppermute | solution.py:531
  11.2 4.2 %collective-permute-start.4 = (f32[48,128]{1,0:T(8,128)S(1)}, f32[48,128]{1,0:T(8,128)S(1)}, u32[]{:S(2)}, u32[]{:S(2)}) collective-permute-start(f32[48,128]{1,0:T(8,128)S(1)} %get-tuple-element.61), channel_id=1, source_target_pairs={{0,3},{1,0},{2,1},{3,2},{4,7},{5,4},{6,5},{7,6},{8,11},{9,8},{10,9... | collective-permute-start | bytes 73736 | tf_op jit(solution)/shard_map/ppermute | solution.py:531
  15.4 2.1 %collective-permute-start.5 = (f32[4,32,1024]{2,1,0:T(8,128)S(1)}, f32[4,32,1024]{2,1,0:T(8,128)S(1)}, u32[]{:S(2)}, u32[]{:S(2)}) collective-permute-start(f32[4,32,1024]{2,1,0:T(8,128)S(1)} %shard_map.61.mine_in), channel_id=1, source_target_pairs={{0,16},{16,0},{1,17},{17,1},{2,18},{18,2},{3,19},{19,3},{4,20},{20... | collective-permute-start | bytes 1572872 | tf_op jit(solution)/shard_map/ppermute | solution.py:528
  16.1 1.4 %collective-permute-start.6 = (f32[32,128]{1,0:T(8,128)S(1)}, f32[32,128]{1,0:T(8,128)S(1)}, u32[]{:S(2)}, u32[]{:S(2)}) collective-permute-start(f32[32,128]{1,0:T(8,128)S(1)} %shard_map.62.mine_edge), channel_id=1, source_target_pairs={{0,16},{16,0},{1,17},{17,1},{2,18},{18,2},{3,19},{19,3},{4,20},{20... | collective-permute-start | bytes 49160 | tf_op jit(solution)/shard_map/ppermute | solution.py:528
